TPU v7x, 32 devices: a whole 2x2x4 slice. The times are simulated.
32 devices in a mesh: ctx: 8 (over z, y), tp: 4 (over x, core).
Axes of the slice: x: 2, y: 2, z: 4, core: 2. Of those that a mesh axis runs over, the one named last changes fastest.
Arguments:
- lin_query: bfloat16 [2048, 4096], P('ctx', 'tp'), may hold values from -6 to 6
- lin_key: bfloat16 [2048, 4096], P('ctx', 'tp'), may hold values from -0.35 to 0.35
- lin_value: bfloat16 [2048, 4096], P('ctx', 'tp'), may hold values from -7 to 7
- log_decay: float32 [32, 2048], P('tp', 'ctx'), may hold values from -1 to 0
- norm_gain: float32 [4096], P('tp'), may hold values from 0.5 to 1.5
- lin_gate: bfloat16 [2048, 4096], P('ctx', 'tp'), may hold values from -6 to 6
- lin_grad: bfloat16 [2048, 4096], P('ctx', 'tp'), may hold values from -6 to 6
- soft_query: bfloat16 [2048, 4096], P('ctx', 'tp'), may hold values from -6 to 6
- soft_key: bfloat16 [2048, 1024], P('ctx', 'tp'), may hold values from -6 to 6
- soft_value: bfloat16 [2048, 1024], P('ctx', 'tp'), may hold values from -6 to 6
- soft_grad: bfloat16 [2048, 4096], P('ctx', 'tp'), may hold values from -6 to 6
Outputs:
- lin_out: bfloat16 [2048, 4096], P('ctx', 'tp')
- lin_query_grad: bfloat16 [2048, 4096], P('ctx', 'tp')
- lin_key_grad: bfloat16 [2048, 4096], P('ctx', 'tp')
- lin_value_grad: bfloat16 [2048, 4096], P('ctx', 'tp')
- lin_gate_grad: bfloat16 [2048, 4096], P('ctx', 'tp')
- soft_out: bfloat16 [2048, 4096], P('ctx', 'tp')
- soft_query_grad: bfloat16 [2048, 4096], P('ctx', 'tp')
- soft_key_grad: bfloat16 [2048, 1024], P('ctx', 'tp')
- soft_value_grad: bfloat16 [2048, 1024], P('ctx', 'tp')
All inputs are finite; a program needn't handle non-finite values.
Results may differ from a plain program's by a relative error of at most 0.035.
Values may be sent and summed in bfloat16 or wider, within the bound.
No kernel may reach another device: no remote copies, remote signals or barrier semaphores. Data moves between devices by JAX's collectives and lax.ppermute only.
A program may use at most 128 MiB of HBM per device.

v0:
```python
import jax
import jax.numpy as jnp
from jax import lax
from jax.sharding import PartitionSpec as P

DH = 128
LINEAR_HEADS = 32


negative_fill = -1e30
top_precision = lax.Precision.HIGHEST


def carried_in(shard, axis, join, neutral, backward):
    count = lax.axis_size(axis)
    place = lax.axis_index(axis)
    ahead = count - 1 - place if backward else place
    gathered = jax.tree.map(
        lambda a, kind: lax.all_gather(a.astype(kind), axis), shard, (jnp.bfloat16, jnp.bfloat16)
    )
    state = jax.tree.map(lambda a, e: jnp.zeros_like(a) + jnp.asarray(e, a.dtype), shard, neutral)

    def one(lap, state):
        source = count - 1 - lap if backward else lap
        return join(
            state,
            jax.tree.map(
                lambda a, own: lax.dynamic_index_in_dim(a, source, 0, False).astype(own.dtype),
                gathered,
                shard,
            ),
        )

    return lax.fori_loop(0, ahead, one, state)


def combine_state(earlier, later):
    return (earlier[0] + later[0], jnp.exp(later[0])[:, None, None] * earlier[1] + later[1])


def lightning(lin_query, lin_key, lin_value, log_decay, norm_gain, lin_gate, lin_grad):
    row_count = lin_query.shape[0]
    head_count = lin_query.shape[1] // DH
    query3 = lin_query.reshape(row_count, head_count, DH)
    key3 = lin_key.reshape(row_count, head_count, DH)
    value3 = lin_value.reshape(row_count, head_count, DH)
    blocklog = jnp.cumsum(log_decay, axis=1)
    totals = blocklog[:, -1]
    order_ids = jnp.arange(row_count)
    causal = (order_ids[:, None] >= order_ids[None, :])[None]
    spread = blocklog[:, :, None] - blocklog[:, None, :]
    decay_mask = jnp.where(causal, jnp.exp(jnp.where(causal, spread, 0.0)), 0.0)
    tail_decay = jnp.exp(totals[:, None] - blocklog).T[:, :, None]
    lead_decay = jnp.exp(blocklog).T[:, :, None]
    raw_scores = jnp.einsum("thd,shd->hts", query3, key3, preferred_element_type=jnp.float32)
    weights = (raw_scores * decay_mask).astype(jnp.bfloat16)
    key_tail = key3.astype(jnp.float32) * tail_decay
    value_f = value3.astype(jnp.float32)
    query_lead = query3.astype(jnp.float32) * lead_decay
    local_state = jnp.einsum("shd,she->hde", key_tail, value_f, precision=top_precision)
    identity = (jnp.zeros_like(totals), jnp.zeros_like(local_state))
    carried = carried_in((totals, local_state), "ctx", combine_state, identity, False)[1]
    attended = jnp.einsum("hts,she->the", weights, value3, preferred_element_type=jnp.float32)
    attended = attended + jnp.einsum("thd,hde->the", query_lead, carried, precision=top_precision)
    flat_out = attended.reshape(row_count, head_count * DH)
    squares = lax.psum(jnp.sum(flat_out * flat_out, axis=1), "tp")
    scaling = lax.rsqrt(squares / (LINEAR_HEADS * DH) + 1e-05)[:, None]
    normed = flat_out * scaling
    gate_sig = jax.nn.sigmoid(lin_gate.astype(jnp.float32))
    gain_row = norm_gain[None, :]
    lin_out = (normed * gain_row * gate_sig).astype(jnp.bfloat16)
    grad_f = lin_grad.astype(jnp.float32)
    scaled = grad_f * gain_row * gate_sig
    gate_grad = (grad_f * normed * gain_row * gate_sig * (1.0 - gate_sig)).astype(jnp.bfloat16)
    cross_term = lax.psum(jnp.sum(scaled * normed, axis=1), "tp")
    att_grad = (scaling * (scaled - normed * (cross_term / (LINEAR_HEADS * DH))[:, None])).astype(
        jnp.bfloat16
    )
    grad3 = att_grad.reshape(row_count, head_count, DH)
    grad_weights = (
        jnp.einsum("the,she->hts", grad3, value3, preferred_element_type=jnp.float32) * decay_mask
    ).astype(jnp.bfloat16)
    grad_lead = grad3.astype(jnp.float32) * lead_decay
    local_grad = jnp.einsum(
        "thd,the->hde", query_lead, grad3.astype(jnp.float32), precision=top_precision
    )
    grad_identity = (jnp.zeros_like(totals), jnp.zeros_like(local_grad))
    returned = carried_in((totals, local_grad), "ctx", combine_state, grad_identity, True)[1]
    query_grad = jnp.einsum("hts,shd->thd", grad_weights, key3, preferred_element_type=jnp.float32)
    query_grad = query_grad + jnp.einsum(
        "the,hde->thd", grad_lead, carried, precision=top_precision
    )
    key_grad = jnp.einsum("hts,thd->shd", grad_weights, query3, preferred_element_type=jnp.float32)
    key_grad = key_grad + jnp.einsum(
        "she,hde->shd", value_f * tail_decay, returned, precision=top_precision
    )
    value_grad = jnp.einsum("hts,the->she", weights, grad3, preferred_element_type=jnp.float32)
    value_grad = value_grad + jnp.einsum(
        "shd,hde->she", key_tail, returned, precision=top_precision
    )
    width = head_count * DH
    return (
        lin_out,
        query_grad.reshape(row_count, width).astype(jnp.bfloat16),
        key_grad.reshape(row_count, width).astype(jnp.bfloat16),
        value_grad.reshape(row_count, width).astype(jnp.bfloat16),
        gate_grad,
    )


def key_tiles(keys_all, values_all, start_row, piece_rows):
    kv_heads = keys_all.shape[1] // DH
    key_tile = lax.dynamic_slice_in_dim(keys_all, start_row, piece_rows, 0).reshape(
        piece_rows, kv_heads, DH
    )
    value_tile = lax.dynamic_slice_in_dim(values_all, start_row, piece_rows, 0).reshape(
        piece_rows, kv_heads, DH
    )
    return (key_tile, value_tile)


def half_forward(query4, positions, last_row, keys_all, values_all, block_rows):
    score_scale = DH ** (-0.5)
    half_rows, kv_heads, group_size = (query4.shape[0], query4.shape[1], query4.shape[2])
    block_count = keys_all.shape[0] // block_rows

    def keep_same(current):
        return current

    def half_block_step(running, block_index):
        start_row = block_index * block_rows

        def half_compute(current):
            row_peak, row_total, accumulated = current
            key_tile, value_tile = key_tiles(keys_all, values_all, start_row, block_rows)
            scores = (
                jnp.einsum("rkgd,ckd->kgrc", query4, key_tile, preferred_element_type=jnp.float32)
                * score_scale
            )
            allowed = positions[:, None] >= (start_row + jnp.arange(block_rows))[None, :]
            fresh_peak = jnp.maximum(
                row_peak, jnp.max(jnp.where(allowed, scores, negative_fill), axis=-1)
            )
            probs = jnp.where(allowed, jnp.exp(scores - fresh_peak[..., None]), 0.0)
            correction = jnp.exp(row_peak - fresh_peak)
            row_total = row_total * correction + jnp.sum(probs, axis=-1)
            product = jnp.einsum(
                "kgrc,ckd->kgrd",
                probs.astype(jnp.bfloat16),
                value_tile,
                preferred_element_type=jnp.float32,
            )
            accumulated = accumulated * correction[..., None] + product
            return (fresh_peak, row_total, accumulated)

        return (lax.cond(start_row <= last_row, half_compute, keep_same, running), None)

    initial = (
        jnp.full((kv_heads, group_size, half_rows), negative_fill, jnp.float32),
        jnp.zeros((kv_heads, group_size, half_rows), jnp.float32),
        jnp.zeros((kv_heads, group_size, half_rows, DH), jnp.float32),
    )
    final_state, _ = lax.scan(half_block_step, initial, jnp.arange(block_count))
    return final_state


def block_grads(half_data, start_row, piece_rows, keys_all, values_all):
    score_scale = DH ** (-0.5)
    query4, grad_block, positions, last_row, logsum, delta_rows = half_data
    key_tile, value_tile = key_tiles(keys_all, values_all, start_row, piece_rows)
    scores = (
        jnp.einsum("rkgd,ckd->kgrc", query4, key_tile, preferred_element_type=jnp.float32)
        * score_scale
    )
    allowed = positions[:, None] >= (start_row + jnp.arange(piece_rows))[None, :]
    probs = jnp.where(allowed, jnp.exp(scores - logsum[..., None]), 0.0)
    prob_grad = jnp.einsum(
        "rkgd,ckd->kgrc", grad_block, value_tile, preferred_element_type=jnp.float32
    )
    score_grad = (probs * (prob_grad - delta_rows[..., None])).astype(jnp.bfloat16)
    results = []
    results.append(
        jnp.einsum("kgrc,ckd->kgrd", score_grad, key_tile, preferred_element_type=jnp.float32)
        * score_scale
    )
    results.append(
        jnp.einsum("kgrc,rkgd->ckd", score_grad, query4, preferred_element_type=jnp.float32)
        * score_scale
    )
    results.append(
        jnp.einsum(
            "kgrc,rkgd->ckd",
            probs.astype(jnp.bfloat16),
            grad_block,
            preferred_element_type=jnp.float32,
        )
    )
    return tuple(results)


def guarded_grads(half_data, start_row, piece_rows, keys_all, values_all):
    query4 = half_data[0]
    half_rows, kv_heads, group_size = (query4.shape[0], query4.shape[1], query4.shape[2])
    zero_query = jnp.zeros((kv_heads, group_size, half_rows, DH), jnp.float32)
    zero_keys = jnp.zeros((piece_rows, kv_heads, DH), jnp.float32)
    empty_terms = (zero_query, zero_keys, zero_keys)

    def guarded_compute():
        return block_grads(half_data, start_row, piece_rows, keys_all, values_all)

    def skip_block():
        return empty_terms

    return lax.cond(start_row <= half_data[3], guarded_compute, skip_block)


def soft_attention(query_rows, keys_all, values_all, grad_rows, starts):
    row_count = query_rows.shape[0]
    half_rows = row_count // 2
    query_width = query_rows.shape[1]
    kv_heads = keys_all.shape[1] // DH
    group_size = query_width // DH // kv_heads
    key_count = keys_all.shape[0]
    block_rows = max(min(512, key_count), key_count // 16)
    block_count = key_count // block_rows
    halves = []
    out_halves = []
    for half_index in range(2):
        lower_row = half_index * half_rows
        upper_row = lower_row + half_rows
        query4 = query_rows[lower_row:upper_row].reshape(half_rows, kv_heads, group_size, DH)
        grad_block = grad_rows[lower_row:upper_row].reshape(half_rows, kv_heads, group_size, DH)
        positions = starts[half_index] + jnp.arange(half_rows)
        last_row = starts[half_index] + half_rows - 1
        row_peak, row_total, accumulated = half_forward(
            query4, positions, last_row, keys_all, values_all, block_rows
        )
        out_half = (
            (accumulated / row_total[..., None])
            .transpose(2, 0, 1, 3)
            .reshape(half_rows, query_width)
            .astype(jnp.bfloat16)
        )
        logsum = row_peak + jnp.log(row_total)
        out_back = (
            lax.optimization_barrier(out_half)
            .astype(jnp.float32)
            .reshape(half_rows, kv_heads, group_size, DH)
        )
        delta_rows = jnp.sum(grad_block.astype(jnp.float32) * out_back, axis=-1).transpose(1, 2, 0)
        halves.append((query4, grad_block, positions, last_row, logsum, delta_rows))
        out_halves.append(out_half)
    key_width = kv_heads * DH
    zero_query = jnp.zeros((kv_heads, group_size, half_rows, DH), jnp.float32)

    def soft_block_step(running, block_index):
        start_row = block_index * block_rows
        first_part = guarded_grads(halves[0], start_row, block_rows, keys_all, values_all)
        second_part = guarded_grads(halves[1], start_row, block_rows, keys_all, values_all)
        return (
            (running[0] + first_part[0], running[1] + second_part[0]),
            (first_part[1] + second_part[1], first_part[2] + second_part[2]),
        )

    query_parts, (key_terms, value_terms) = lax.scan(
        soft_block_step, (zero_query, zero_query), jnp.arange(block_count)
    )
    key_grad, value_grad = (
        lax.psum_scatter(
            key_terms.reshape(key_count, key_width).astype(jnp.bfloat16),
            "ctx",
            scatter_dimension=0,
            tiled=True,
        ).astype(jnp.float32),
        lax.psum_scatter(
            value_terms.reshape(key_count, key_width).astype(jnp.bfloat16),
            "ctx",
            scatter_dimension=0,
            tiled=True,
        ).astype(jnp.float32),
    )
    query_halves = [
        query_parts[half_index]
        .transpose(2, 0, 1, 3)
        .reshape(half_rows, query_width)
        .astype(jnp.bfloat16)
        for half_index in range(2)
    ]
    return (
        out_halves,
        query_halves,
        key_grad.astype(jnp.bfloat16),
        value_grad.astype(jnp.bfloat16),
    )


def body(
    lin_query,
    lin_key,
    lin_value,
    log_decay,
    norm_gain,
    lin_gate,
    lin_grad,
    soft_query,
    soft_key,
    soft_value,
    soft_grad,
):
    lin_out, lin_query_grad, lin_key_grad, lin_value_grad, lin_gate_grad = lightning(
        lin_query, lin_key, lin_value, log_decay, norm_gain, lin_gate, lin_grad
    )
    keys_all, values_all = (
        lax.all_gather(soft_key, "ctx", axis=0, tiled=True),
        lax.all_gather(soft_value, "ctx", axis=0, tiled=True),
    )
    row_count = soft_query.shape[0]
    half_rows = row_count // 2
    ctx_index = lax.axis_index("ctx")
    starts = (ctx_index * row_count, ctx_index * row_count + half_rows)
    out_halves, query_halves, soft_key_grad, soft_value_grad = soft_attention(
        soft_query, keys_all, values_all, soft_grad, starts
    )
    second_out = out_halves[1]
    second_query = query_halves[1]
    soft_out = jnp.concatenate((out_halves[0], second_out), axis=0)
    soft_query_grad = jnp.concatenate((query_halves[0], second_query), axis=0)
    return (
        lin_out,
        lin_query_grad,
        lin_key_grad,
        lin_value_grad,
        lin_gate_grad,
        soft_out,
        soft_query_grad,
        soft_key_grad,
        soft_value_grad,
    )


def solution(mesh):
    placed = (
        P("ctx", "tp"),
        P("ctx", "tp"),
        P("ctx", "tp"),
        P("tp", "ctx"),
        P("tp"),
        P("ctx", "tp"),
        P("ctx", "tp"),
        P("ctx", "tp"),
        P("ctx", "tp"),
        P("ctx", "tp"),
        P("ctx", "tp"),
    )
    return jax.shard_map(
        body,
        mesh=mesh,
        in_specs=placed,
        out_specs=(
            P("ctx", "tp"),
            P("ctx", "tp"),
            P("ctx", "tp"),
            P("ctx", "tp"),
            P("ctx", "tp"),
            P("ctx", "tp"),
            P("ctx", "tp"),
            P("ctx", "tp"),
            P("ctx", "tp"),
        ),
        check_vma=False,
    )
```

profile of v0, /device:TPU:0, one launch (start us, length us, event | category | flops | bytes accessed | tf_op | source)
XLA Modules:
  0.0 402.5 jit_solution(12081458563050500736)
XLA Ops:
  9.1 3.1 convolution_convert_fusion.1
  17.3 23.3 %all-reduce = bf16[64]{0:T(256)(128)(2,1)S(1)} all-reduce(bf16[64]{0:T(256)(128)(2,1)S(1)} %dynamic-update-slice), channel_id=2, replica_groups=mesh['ctx'=8,'tp'=4] {'ctx'}, use_global_device_ids=true, to_apply=%add | all-reduce | flops 64 | bytes 256
  42.6 22.0 %all-gather.12.cloned.1.call-done = bf16[64,128,128]{2,1,0:T(8,128)(2,1)} async-done(((bf16[8,128,128]{2,1,0:T(8,128)(2,1)}), bf16[64,128,128]{2,1,0:T(8,128)(2,1)}) %all-gather.12.cloned.1.call-update) | async-done | bytes 2097168 | tf_op jit(solution)/shard_map/all_gather | solution.py:19
  64.7 2.1 multiply_reduce_fusion.1
  68.4 5.8 %psum.14 = f32[256]{0:T(256)S(1)} all-reduce(f32[256]{0:T(256)S(1)} %get-tuple-element.906), channel_id=1, replica_groups=mesh['ctx'=8,'tp'=4] {'tp'}, use_global_device_ids=true, to_apply=%region_5.6 | all-reduce | flops 256 | bytes 2048 | tf_op jit(solution)/shard_map/psum | solution.py:66
  75.8 6.6 %psum.15 = f32[256]{0:T(256)S(1)} all-reduce(f32[256]{0:T(256)S(1)} %multiply_reduce_fusion), channel_id=1, replica_groups=mesh['ctx'=8,'tp'=4] {'tp'}, use_global_device_ids=true, to_apply=%region_7.8 | all-reduce | flops 256 | bytes 2048 | tf_op jit(solution)/shard_map/psum | solution.py:75
  89.2 16.0 %all-gather.10.cloned.1.call-done = bf16[2048,256]{0,1:T(8,128)(2,1)} async-done(((bf16[256,256]{0,1:T(8,128)(2,1)}), bf16[2048,256]{0,1:T(8,128)(2,1)}) %all-gather.10.cloned.1.call-update) | async-done | bytes 1048592 | tf_op jit(solution)/shard_map/all_gather | solution.py:315
  105.2 41.1 %all-gather.8.cloned.1.call-done = bf16[2048,256]{0,1:T(8,128)(2,1)} async-done(((bf16[256,256]{0,1:T(8,128)(2,1)}), bf16[2048,256]{0,1:T(8,128)(2,1)}) %all-gather.8.cloned.1.call-update) | async-done | bytes 1048592 | tf_op jit(solution)/shard_map/all_gather | solution.py:314
  146.4 8.8 %while.76 = (s32[]{:T(128)}, f32[2,4,128]{2,1,0:T(4,128)S(1)}, f32[2,4,128]{2,1,0:T(4,128)S(1)}, f32[2,4,128,128]{3,2,1,0:T(8,128)S(1)}, s32[4]{0:T(128)S(1)}, /...) while((s32[]{:T(128)}, f32[2,4,128]{2,1,0:T(4,128)S(1)}, ...), condition=%wide.region_21.22_spmd.clone, body=%wide.region_16.21_spmd.clone.sunk | while | flops 274532992 | bytes 9509193 | solution.py:163
  147.8 3.4 conditional.13
  156.5 9.5 %while.75 = (s32[]{:T(128)}, f32[2,4,128]{2,1,0:T(4,128)S(1)}, f32[2,4,128]{2,1,0:T(4,128)S(1)}, f32[2,4,128,128]{3,2,1,0:T(8,128)S(1)}, s32[4]{0:T(128)S(1)}, /...) while((s32[]{:T(128)}, f32[2,4,128]{2,1,0:T(4,128)S(1)}, ...), condition=%wide.region_15.16_spmd.clone, body=%wide.region_10.15_spmd.clone.sunk | while | flops 274532992 | bytes 9509193 | solution.py:163
  157.7 4.4 %conditional.12 = ((f32[2,4,128]{2,1,0:T(4,128)S(1)}, f32[2,4,128]{2,1,0:T(4,128)S(1)}, f32[2,4,128,128]{3,2,1,0:T(8,128)S(1)})) conditional(s32[]{:T(128)} %convert_element_type.333, (f32[2,4,128]{2,1,0:T(4,128)S(1)}, f32[2,4,128]{2,1,0:T(4,128)S(1)}, f32[2,4,128,128]{3,2,1,0:T(8,128)S(1)}) %tuple.177, (s32[]{:T(128)}, s32[]{:T(128)}, ...), branch_computations={%region_11.11_spmd, %region_12.14_spmd} | conditional | flops 274532992 | bytes 9508430 | solution.py:156
  167.3 37.0 %while.77 = (s32[]{:T(128)}, f32[2,4,128,128]{3,2,1,0:T(8,128)}, f32[2,4,128,128]{3,2,1,0:T(8,128)}, bf16[4,512,2,128]{3,1,2,0:T(8,128)(2,1)}, bf16[4,512,2,128]...) while((s32[]{:T(128)}, f32[2,4,128,128]{3,2,1,0:T(8,128)}, ...), condition=%wide.region_29.30_spmd.clone, body=%wide.region_24.29_spmd.clone.sunk | while | flops 1350960384 | bytes 36467804 | solution.py:265
  168.6 7.9 %conditional.15 = (f32[2,4,128,128]{3,2,1,0:T(8,128)S(1)}, f32[512,2,128]{2,0,1:T(8,128)S(1)}, f32[512,2,128]{2,0,1:T(8,128)S(1)}) conditional(s32[]{:T(128)} %convert_element_type.336, () %tuple.187, (s32[]{:T(128)}, s32[]{:T(128)}, bf16[2048,256]{0,1:T(8,128)(2,1)}, bf16[128,2,4,128]{3,0,2,1:T(8,128)(2,1)}, f32[2,4,128]{2,1,0:T(4,128)S(1)}, ...), branch_computations={%region_25.25_spmd, %region_26.26_spmd} | conditional | flops 675086976 | bytes 14038598 | solution.py:214
  176.5 5.0 %conditional.14 = (f32[2,4,128,128]{3,2,1,0:T(8,128)S(1)}, f32[512,2,128]{2,0,1:T(8,128)S(1)}, f32[512,2,128]{2,0,1:T(8,128)}) conditional(s32[]{:T(128)} %convert_element_type.335, () %tuple.185, (s32[]{:T(128)}, s32[]{:T(128)}, bf16[2048,256]{0,1:T(8,128)(2,1)}, bf16[128,2,4,128]{3,0,2,1:T(8,128)(2,1)S(1)}, f32[2,4,128]{2,1,0:T(4,128)S(1)}, ...), branch_computations={%region_27.27_spmd, %region_28.28_spmd} | conditional | flops 675086976 | bytes 16135806 | solution.py:214
  188.9 2.3 select_add_fusion.3
  195.5 2.3 select_add_fusion.3
  202.0 2.3 select_add_fusion.3
  204.3 2.3 copy.225
  219.4 8.1 %while.74 = (s32[]{:T(128)}, f32[8,128,128]{2,1,0:T(8,128)S(1)}, s32[]{:T(128)}, bf16[8,8]{1,0:T(8,128)(2,1)S(1)}, bf16[8,8,128,128]{3,2,1,0:T(8,128)(2,1)}, /*index=5*/s32[]{:T(128)}, s32[]{:T(128)}, s32[]{:T(128)}, s32[]{:T(128)}) while((s32[]{:T(128)}, f32[8,128,128]{2,1,0:T(8,128)S(1)}, s32[]{:T(128)}, bf16[8,8]{1,0:T(8,128)(2,1)S(1)}, ...), condition=%wide.region_9.10_spmd, body=%wide.region_8.9_spmd.sunk | while | flops 393230 | bytes 1310947 | solution.py:34
  227.5 2.2 fusion.51
  231.7 2.2 convolution_bitcast_fusion.5
  235.3 93.6 %reduce-scatter.3.cloned.1.call-done = bf16[256,256]{1,0:T(8,128)(2,1)} async-done(((bf16[2048,256]{1,0:T(8,128)(2,1)}), bf16[256,256]{1,0:T(8,128)(2,1)}) %reduce-scatter.3.cloned.1.call-update) | async-done | bytes 131088 | tf_op jit(solution)/shard_map/reduce_scatter | solution.py:269
  329.0 66.7 %reduce-scatter.5.cloned.1.call-done = bf16[256,256]{1,0:T(8,128)(2,1)} async-done(((bf16[2048,256]{1,0:T(8,128)(2,1)}), bf16[256,256]{1,0:T(8,128)(2,1)}) %reduce-scatter.5.cloned.1.call-update) | async-done | bytes 131088 | tf_op jit(solution)/shard_map/reduce_scatter | solution.py:275
  (267 shorter events, 87.3 us)
Async XLA Ops:
  7.2 5.1 %copy-start.25 = (bf16[256,256]{1,0:T(8,128)(2,1)S(1)}, bf16[256,256]{1,0:T(8,128)(2,1)}, u32[]{:S(2)}) copy-start(bf16[256,256]{1,0:T(8,128)(2,1)} %param.38) | copy-start | bytes 393220
  7.2 6.0 %copy-start.26 = (bf16[256,256]{1,0:T(8,128)(2,1)S(1)}, bf16[256,256]{1,0:T(8,128)(2,1)}, u32[]{:S(2)}) copy-start(bf16[256,256]{1,0:T(8,128)(2,1)} %param.37) | copy-start | bytes 393220
  7.2 7.1 %copy-start.22 = (bf16[256,1024]{1,0:T(8,128)(2,1)S(1)}, bf16[256,1024]{1,0:T(8,128)(2,1)}, u32[]{:S(2)}) copy-start(bf16[256,1024]{1,0:T(8,128)(2,1)} %param.36) | copy-start | bytes 1572868
  7.2 57.4 %all-gather.12.cloned.1.call-start = ((), (), s32[]{:S(2)}) async-start(), calls=%async_computation.6 | async-start | bytes 2359296 | tf_op jit(solution)/shard_map/all_gather | solution.py:19
  12.2 3.5 copy-start.28
  12.3 28.4 %copy-start.23 = (bf16[256,1024]{1,0:T(8,128)(2,1)S(1)}, bf16[256,1024]{1,0:T(8,128)(2,1)}, u32[]{:S(2)}) copy-start(bf16[256,1024]{1,0:T(8,128)(2,1)} %param.29) | copy-start | bytes 1572868
  12.3 93.0 %all-gather.10.cloned.1.call-start = ((), (), s32[]{:S(2)}) async-start(), calls=%async_computation.3 | async-start | bytes 1179648 | tf_op jit(solution)/shard_map/all_gather | solution.py:315
  13.1 133.2 %all-gather.8.cloned.1.call-start = ((), (), s32[]{:S(2)}) async-start(), calls=%async_computation.2 | async-start | bytes 1179648 | tf_op jit(solution)/shard_map/all_gather | solution.py:314
  14.0 205.4 %all-gather.14.cloned.1.call-start = ((), (), s32[]{:S(2)}) async-start(), calls=%async_computation.7 | async-start | bytes 2359296 | tf_op jit(solution)/shard_map/all_gather | solution.py:19
  40.8 44.7 %copy-start.9 = (bf16[256,1024]{0,1:T(8,128)(2,1)}, bf16[256,1024]{0,1:T(8,128)(2,1)S(1)}, u32[]{:S(2)}) copy-start(bf16[256,1024]{0,1:T(8,128)(2,1)S(1)} %copy.277) | copy-start | bytes 1572868
  42.1 22.5 %copy-start.11 = (bf16[8,256,256]{2,1,0:T(8,128)(2,1)}, bf16[8,256,256]{2,1,0:T(8,128)(2,1)S(1)}, u32[]{:S(2)}) copy-start(bf16[8,256,256]{2,1,0:T(8,128)(2,1)S(1)} %multiply_convert_fusion.1) | copy-start | bytes 3145732
  64.6 3.8 copy-start.1
  64.7 9.6 %copy-start.27 = (f32[1024]{0:T(1024)S(1)}, f32[1024]{0:T(1024)}, u32[]{:S(2)}) copy-start(f32[1024]{0:T(1024)} %param.33) | copy-start | bytes 12292
  66.8 7.5 %copy-start.17 = (bf16[256,1024]{1,0:T(8,128)(2,1)S(1)}, bf16[256,1024]{1,0:T(8,128)(2,1)}, u32[]{:S(2)}) copy-start(bf16[256,1024]{1,0:T(8,128)(2,1)} %param.35) | copy-start | bytes 1572868
  68.4 14.0 %copy-start.18 = (bf16[256,1024]{1,0:T(8,128)(2,1)S(1)}, bf16[256,1024]{1,0:T(8,128)(2,1)}, u32[]{:S(2)}) copy-start(bf16[256,1024]{1,0:T(8,128)(2,1)} %param.34) | copy-start | bytes 1572868
  84.3 2.8 copy-start.24
  85.6 2.8 copy-start.7
  87.0 241.9 %reduce-scatter.3.cloned.1.call-start = ((), (), s32[]{:S(2)}) async-start(), calls=%async_computation.4 | async-start | bytes 1179648 | tf_op jit(solution)/shard_map/reduce_scatter | solution.py:269
  176.6 2.2 copy-start.3
  207.7 188.0 %reduce-scatter.5.cloned.1.call-start = ((), (), s32[]{:S(2)}) async-start(), calls=%async_computation.5 | async-start | bytes 1179648 | tf_op jit(solution)/shard_map/reduce_scatter | solution.py:275
  208.2 2.3 copy-start.5
  210.9 2.2 copy-start.8
  211.0 2.2 copy-start.12
  229.6 4.4 %copy-start.10 = (bf16[256,1024]{0,1:T(8,128)(2,1)S(1)}, bf16[256,1024]{0,1:T(8,128)(2,1)}, u32[]{:S(2)}) copy-start(bf16[256,1024]{0,1:T(8,128)(2,1)} %copy-done.9) | copy-start | bytes 1572868
  (11 other events, 13.1 us)
Sparse Core Ops, SparseCore 0:
  12.4 52.1 all-gather.11
  67.2 38.0 all-gather.9
  107.9 38.4 all-gather.7
  148.3 48.2 all-gather.13
  207.9 121.0 reduce-scatter.2
  333.2 62.4 reduce-scatter.4
where the time goes:
time: 405 us; the launch traced here: 403 us
  waiting for transfers between devices  240 us (59%)
  local copies, waits for them, and re-layouts  40.5 us (10%)
  blocking collectives  35.7 us (9%)
  other arithmetic  32.3 us (8%)
  matrix products  29.6 us (7%)
  between operations  15.4 us (4%)
  loops' own time  9.33 us (2%)
    reduce_scatter x1, waiting for transfers between devices, soft_attention(): lax.psum_scatter(key_terms.reshape(key_count, key_width).astype(jnp.bfloa...  93.6 us
    reduce_scatter x1, waiting for transfers between devices, soft_attention(): lax.psum_scatter(value_terms.reshape(key_count, key_width).astype(jnp.bfl...  66.7 us
    all_gather x1, waiting for transfers between devices, body(): lax.all_gather(soft_key, 'ctx', axis=0, tiled=True)  41.1 us
    unnamed x1, blocking collectives  23.3 us
    all_gather x2, waiting for transfers between devices, carried_in(): lax.all_gather(a.astype(kind), axis)  22 us
    all_gather x1, waiting for transfers between devices, body(): lax.all_gather(soft_value, 'ctx', axis=0, tiled=True)  16 us
    unnamed x72, local copies, waits for them, and re-layouts  15.9 us
  transfers between devices with their start and end apart: 6, of which 5 were waited for; matrix products, arithmetic and copies ran while one was open for 24% of the time, Pallas kernels for 0%

commit v1 on v0

v1 whole, which is shorter than its diff:
```python
import functools

import jax
import jax.numpy as jnp
from jax import lax
from jax.experimental import pallas as pl
from jax.experimental.pallas import tpu as pltpu
from jax.sharding import PartitionSpec as P

DH = 128
LOG2E = 1.4426950408889634
LN2 = 0.6931471805599453
negative_fill = -1e30
f32 = jnp.float32
bf16 = jnp.bfloat16
VMEM_BYTES = 48 * 1024 * 1024
CHUNK = 256

SMEM_SPEC = pl.BlockSpec(memory_space=pltpu.SMEM)
VMEM_SPEC = pl.BlockSpec(memory_space=pltpu.VMEM)


def nn(a, b):
    return jnp.dot(a, b, preferred_element_type=f32)


def nt(a, b):
    return lax.dot_general(a, b, (((1,), (1,)), ((), ())), preferred_element_type=f32)


def tn(a, b):
    return lax.dot_general(a, b, (((0,), (0,)), ((), ())), preferred_element_type=f32)


def whole_call(kernel, place, arrays, outs, flops=0):
    moved = sum(a.size * a.dtype.itemsize for a in arrays)
    moved += sum(int(jnp.dtype(o.dtype).itemsize) * o.size for o in outs)
    return pl.pallas_call(
        kernel,
        out_shape=outs,
        in_specs=[SMEM_SPEC] + [VMEM_SPEC] * len(arrays),
        out_specs=[VMEM_SPEC] * len(outs),
        compiler_params=pltpu.CompilerParams(vmem_limit_bytes=VMEM_BYTES),
        cost_estimate=pl.CostEstimate(flops=flops, bytes_accessed=moved, transcendentals=0),
    )(place, *arrays)


def split3(x):
    hi = x.astype(bf16)
    rest = x - hi.astype(f32)
    lo = rest.astype(bf16)
    return hi, lo, (rest - lo.astype(f32)).astype(bf16)


def extra_rows(heads):
    return 16 * pl.cdiv(3 * heads, 16)


def pack_logs(rows):
    heads = rows.shape[0]
    pad = extra_rows(heads) - 3 * heads
    parts = [p.astype(f32) for p in split3(rows)]
    if pad:
        parts.append(jnp.zeros((pad, DH), f32))
    return jnp.concatenate(parts, axis=0).astype(bf16)


def read_logs(ref, heads):
    part = ref[heads * DH :, :].astype(f32)
    return part[:heads] + part[heads : 2 * heads] + part[2 * heads : 3 * heads]


def head_rows(h):
    return slice(h * DH, (h + 1) * DH)


def lin_state_kernel(heads, fold, place, log_ref, key_ref, value_ref, msg_ref, row_ref, col_ref):
    rows = key_ref.shape[0]
    y = place[0]
    later = lax.broadcasted_iota(jnp.int32, (rows, rows), 0)
    earlier = lax.broadcasted_iota(jnp.int32, (rows, rows), 1)
    tri = (earlier <= later).astype(f32)
    logs = log_ref[...]
    exact = lax.Precision.HIGHEST
    dims = (((1,), (1,)), ((), ()))
    by_row = lax.dot_general(logs, tri, dims, precision=exact, preferred_element_type=f32)
    by_col = lax.dot_general(tri, logs, dims, precision=exact, preferred_element_type=f32)
    row_ref[...] = by_row
    col_ref[...] = by_col
    totals = by_row[:, rows - 1 : rows]
    tail = jnp.exp(totals - by_row)
    group = heads // fold
    for g in range(fold):
        slot = lax.rem(g + y, fold) if fold > 1 else 0
        for i in range(group):
            h = g * group + i
            key_t = key_ref[:, head_rows(h)].astype(f32).T * tail[h : h + 1, :]
            state = nn(key_t.astype(bf16), value_ref[:, head_rows(h)])
            msg_ref[slot, head_rows(i), :] = state.astype(bf16)
        wide = jnp.broadcast_to(totals[g * group : (g + 1) * group], (group, DH))
        msg_ref[slot, group * DH :, :] = pack_logs(wide)


def lin_pair_kernel(heads, backward, place, own_ref, rec_ref, out_ref):
    y = place[0]
    own_logs, rec_logs = read_logs(own_ref, heads), read_logs(rec_ref, heads)
    out_ref[heads * DH :, :] = pack_logs(own_logs + rec_logs)
    own_far = (y == 1) if backward else (y == 0)
    near_scale = jnp.exp(jnp.where(own_far, rec_logs, own_logs))
    own_scale = jnp.where(own_far, near_scale, 1.0)
    rec_scale = jnp.where(own_far, 1.0, near_scale)
    for i in range(heads):
        own, rec = own_ref[head_rows(i), :].astype(f32), rec_ref[head_rows(i), :].astype(f32)
        joint = own * own_scale[i : i + 1] + rec * rec_scale[i : i + 1]
        out_ref[head_rows(i), :] = joint.astype(bf16)


def lin_scan_kernel(heads, fold, count, backward, place, own_ref, rec_ref, *rest):
    far, outs = rest[:count], rest[count:]
    y = place[0]
    if fold > 1:
        own_logs, rec_logs = read_logs(own_ref, heads), read_logs(rec_ref, heads)
        own_near = (y == 1) if backward else (y == 0)
        near_scale = jnp.exp(jnp.where(own_near, own_logs, rec_logs))
    far_scales = []
    passed = jnp.zeros((heads, DH), f32)
    for s in range(count):
        far_scales.append(jnp.exp(passed))
        passed = passed + read_logs(far[s], heads)
    for i in range(heads):
        total = jnp.zeros((DH, DH), f32)
        for s in range(count):
            total = total + far_scales[s][i : i + 1] * far[s][head_rows(i), :].astype(f32)
        if fold == 1:
            outs[0][head_rows(i), :] = total.astype(bf16)
            continue
        own, rec = own_ref[head_rows(i), :].astype(f32), rec_ref[head_rows(i), :].astype(f32)
        beyond = jnp.where(own_near, own, rec) + near_scale[i : i + 1] * total
        outs[0][head_rows(i), :] = jnp.where(own_near, total, beyond).astype(bf16)
        outs[1][head_rows(i), :] = jnp.where(own_near, beyond, total).astype(bf16)


def pick_state(refs, h, group, y):
    i = h % group
    if len(refs) == 1:
        return refs[0][head_rows(i), :]
    own, rec = refs[0][head_rows(i), :].astype(f32), refs[1][head_rows(i), :].astype(f32)
    return jnp.where(y == h // group, own, rec).astype(bf16)


def lin_attend_kernel(
    heads, fold, place, row_ref, col_ref, query_ref, key_ref, value_ref, gate_ref, grad_ref, gain_ref, *rest
):
    states, (att_ref, stat_ref) = rest[:fold], rest[fold:]
    rows = query_ref.shape[0]
    y = place[0]
    causal = lax.broadcasted_iota(jnp.int32, (rows, rows), 0) >= lax.broadcasted_iota(
        jnp.int32, (rows, rows), 1
    )
    squares = jnp.zeros((rows, DH), f32)
    crosses = jnp.zeros((rows, DH), f32)
    for h in range(heads):
        query, key, value = (r[:, head_rows(h)] for r in (query_ref, key_ref, value_ref))
        col = col_ref[:, h : h + 1]
        decay = jnp.exp(jnp.where(causal, col - row_ref[h : h + 1, :], negative_fill))
        weights = (nt(query, key) * decay).astype(bf16)
        state = pick_state(states, h, heads // fold, y)
        att = nn(weights, value) + jnp.exp(col) * nn(query, state)
        att_ref[:, head_rows(h)] = att
        sig = jax.nn.sigmoid(gate_ref[:, head_rows(h)].astype(f32))
        scaled = grad_ref[:, head_rows(h)].astype(f32) * gain_ref[:, head_rows(h)] * sig
        squares = squares + att * att
        crosses = crosses + scaled * att
    stat_ref[...] = jnp.concatenate(
        (
            jnp.sum(squares.T, axis=0, keepdims=True),
            jnp.sum(crosses.T, axis=0, keepdims=True),
            jnp.zeros((6, rows), f32),
        ),
        axis=0,
    )


def lin_norm_kernel(
    heads, fold, width, place, row_ref, stat_ref, att_ref, gate_ref, grad_ref, gain_ref, query_ref, own_ref, oth_ref,
    out_ref, gate_grad_ref, att_grad_ref, msg_ref,
):
    y = place[0]
    rows = query_ref.shape[0]
    stats = jnp.concatenate((stat_ref[...], jnp.zeros((DH - 8, rows), f32)), axis=0).T
    scaling = lax.rsqrt(stats[:, 0:1] / width + 1e-05)
    cross = scaling * stats[:, 1:2] / width
    group = heads // fold
    lead = jnp.exp(row_ref[...])
    for g in range(fold):
        slot = lax.rem(g + y, fold) if fold > 1 else 0
        for i in range(group):
            h = g * group + i
            gain = gain_ref[:, head_rows(h)]
            sig = jax.nn.sigmoid(gate_ref[:, head_rows(h)].astype(f32))
            normed = att_ref[:, head_rows(h)] * scaling
            scaled = grad_ref[:, head_rows(h)].astype(f32) * gain * sig
            out_ref[:, head_rows(h)] = (normed * gain * sig).astype(bf16)
            gate_grad_ref[:, head_rows(h)] = (scaled * normed * (1.0 - sig)).astype(bf16)
            att_grad = (scaling * (scaled - normed * cross)).astype(bf16)
            att_grad_ref[:, head_rows(h)] = att_grad
            query_t = query_ref[:, head_rows(h)].astype(f32).T * lead[h : h + 1, :]
            msg_ref[slot, head_rows(i), :] = nn(query_t.astype(bf16), att_grad).astype(bf16)
    msg_ref[0, group * DH :, :] = own_ref[group * DH :, :]
    if fold > 1:
        msg_ref[1, group * DH :, :] = oth_ref[group * DH :, :]


def lin_grad_kernel(heads, fold, place, row_ref, col_ref, query_ref, key_ref, value_ref, att_grad_ref, *rest):
    states, back_states = rest[:fold], rest[fold : 2 * fold]
    query_grad_ref, key_grad_ref, value_grad_ref = rest[2 * fold :]
    y = place[0]
    rows = query_ref.shape[0]
    first = lax.broadcasted_iota(jnp.int32, (rows, rows), 0)
    second = lax.broadcasted_iota(jnp.int32, (rows, rows), 1)
    causal, causal_t = first >= second, first <= second
    for h in range(heads):
        query, key, value, grad = (
            r[:, head_rows(h)] for r in (query_ref, key_ref, value_ref, att_grad_ref)
        )
        col, row = col_ref[:, h : h + 1], row_ref[h : h + 1, :]
        decay = jnp.exp(jnp.where(causal, col - row, negative_fill))
        decay_t = jnp.exp(jnp.where(causal_t, row - col, negative_fill))
        lead, tail = jnp.exp(col), jnp.exp(row[:, rows - 1 : rows] - col)
        state = pick_state(states, h, heads // fold, y)
        back = pick_state(back_states, h, heads // fold, y)
        grad_weights = (nt(grad, value) * decay).astype(bf16)
        grad_weights_t = (nt(value, grad) * decay_t).astype(bf16)
        weights_t = (nt(key, query) * decay_t).astype(bf16)
        query_grad = nn(grad_weights, key) + lead * nt(grad, state)
        key_grad = nn(grad_weights_t, query) + tail * nt(value, back)
        value_grad = nn(weights_t, grad) + tail * nn(key, back)
        query_grad_ref[:, head_rows(h)] = query_grad.astype(bf16)
        key_grad_ref[:, head_rows(h)] = key_grad.astype(bf16)
        value_grad_ref[:, head_rows(h)] = value_grad.astype(bf16)


def diagonal_mask(y, keys, first, count, tokens, rows):
    key_at = lax.rem(lax.broadcasted_iota(jnp.int32, (keys, count), 0) + y * tokens, rows)
    query_at = lax.rem(lax.broadcasted_iota(jnp.int32, (keys, count), 1) + first + y * tokens, rows)
    return key_at <= query_at


def stack_rows(refs):
    parts = [r[...] for r in refs]
    return parts[0] if len(parts) == 1 else jnp.concatenate(parts, axis=0)


def soft_forward_kernel(fold, tokens, shift, first, last, place, *refs):
    refs = list(refs)
    take = lambda count: [refs.pop(0) for _ in range(count)]
    query_refs = take(fold)
    grad_refs = take(fold) if last else []
    (kv_ref,) = take(1)
    carry = take(0 if first else 3)
    outs = take(fold + 2 if last else 3)
    peak, total, acc = refs
    b = pl.program_id(1)
    rows = tokens * fold

    @pl.when(b == 0)
    def _():
        if first:
            peak[...] = jnp.full((1, rows), negative_fill, f32)
            total[...] = jnp.zeros((1, rows), f32)
            acc[...] = jnp.zeros((DH, rows), f32)
        else:
            peak[...], total[...], acc[...] = (r[0] for r in carry)

    @pl.when(place[1] >= shift + b)
    def _():
        key, value = kv_ref[0, :, :DH], kv_ref[0, :, DH:]
        query = stack_rows(query_refs)
        step = min(CHUNK, rows)
        for at in range(0, rows, step):
            span = slice(at, at + step)
            scores = nt(key, query[span]) * (LOG2E * DH**-0.5)
            if shift == 0:
                mask = diagonal_mask(place[0], rows, at, step, tokens, rows)
                scores = jnp.where(mask, scores, negative_fill)
            old = peak[:, span]
            fresh = jnp.maximum(old, jnp.max(scores, axis=0, keepdims=True))
            probs = jnp.exp2(scores - fresh)
            fade = jnp.exp2(old - fresh)
            peak[:, span] = fresh
            total[:, span] = total[:, span] * fade + jnp.sum(probs, axis=0, keepdims=True)
            acc[:, span] = acc[:, span] * fade + tn(value, probs.astype(bf16))

    @pl.when(b == pl.num_programs(1) - 1)
    def _():
        if not last:
            for out, value in zip(outs, (peak, total, acc)):
                out[0] = value[...]
            return
        out_t = (acc[...] / total[...]).astype(bf16).astype(f32)
        out = out_t.T.astype(bf16)
        for i in range(fold):
            outs[i][...] = out[i * tokens : (i + 1) * tokens]
        grad_t = stack_rows(grad_refs).astype(f32).T
        outs[fold][0] = peak[...] + jnp.log(total[...]) * LOG2E
        outs[fold + 1][0] = jnp.sum(grad_t * out_t, axis=0, keepdims=True)


def soft_specs(fold, tokens, group, head_of):
    own = pl.BlockSpec((tokens, DH), lambda *a: (0, a[-1][0] * group + head_of(*a)))
    rec = pl.BlockSpec((tokens, DH), lambda *a: (0, head_of(*a)))
    return [own, rec][:fold]


def soft_call(kernel, place, grid, in_specs, arrays, out_specs, outs, scratch, flops):
    moved = sum(a.size * a.dtype.itemsize for a in arrays)
    return pl.pallas_call(
        kernel,
        out_shape=outs,
        grid_spec=pltpu.PrefetchScalarGridSpec(
            num_scalar_prefetch=1,
            grid=grid,
            in_specs=in_specs,
            out_specs=out_specs,
            scratch_shapes=scratch,
        ),
        compiler_params=pltpu.CompilerParams(
            dimension_semantics=("arbitrary", "arbitrary"), vmem_limit_bytes=VMEM_BYTES
        ),
        cost_estimate=pl.CostEstimate(flops=flops, bytes_accessed=moved, transcendentals=0),
    )(place, *arrays)


def soft_forward(place, queries, grads, kv, shift, carry, last):
    fold, tokens = len(queries), queries[0].shape[0]
    group = queries[0].shape[1] // DH // fold
    blocks, rows = kv.shape[0], kv.shape[1]
    first = carry is None
    row_specs = soft_specs(fold, tokens, group, lambda h, b, p: h)
    line = pl.BlockSpec((1, 1, rows), lambda h, b, p: (h, 0, 0))
    tall = pl.BlockSpec((1, DH, rows), lambda h, b, p: (h, 0, 0))
    kv_spec = pl.BlockSpec((1, rows, 2 * DH), lambda h, b, p: (b, 0, 0))
    lines = jax.ShapeDtypeStruct((group, 1, rows), f32)
    talls = jax.ShapeDtypeStruct((group, DH, rows), f32)
    arrays, specs = list(queries), list(row_specs)
    if last:
        arrays, specs = arrays + list(grads), specs + row_specs
    arrays, specs = arrays + [kv], specs + [kv_spec]
    if not first:
        arrays, specs = arrays + list(carry), specs + [line, line, tall]
    if last:
        half = pl.BlockSpec((tokens, DH), lambda h, b, p: (0, h))
        out_specs = [half] * fold + [line, line]
        outs = [jax.ShapeDtypeStruct((tokens, group * DH), bf16)] * fold + [lines, lines]
    else:
        out_specs, outs = [line, line, tall], [lines, lines, talls]
    scratch = [pltpu.VMEM((1, rows), f32), pltpu.VMEM((1, rows), f32), pltpu.VMEM((DH, rows), f32)]
    kernel = functools.partial(soft_forward_kernel, fold, tokens, shift, first, last)
    flops = 4 * group * blocks * rows * rows * DH
    return soft_call(kernel, place, (group, blocks), specs, arrays, out_specs, outs, scratch, flops)


def soft_backward_kernel(fold, tokens, shift, first, last, place, *refs):
    refs = list(refs)
    take = lambda count: [refs.pop(0) for _ in range(count)]
    query_refs, grad_refs = take(fold), take(fold)
    log_ref, delta_ref, kv_ref = take(3)
    carry = take(0 if first else 1)
    (kv_grad_ref,) = take(1)
    outs = take(fold if last else 1)
    key_acc, value_acc, query_acc = refs
    b, h = pl.program_id(0), pl.program_id(1)
    rows = tokens * fold

    @pl.when(h == 0)
    def _():
        key_acc[...] = jnp.zeros((rows, DH), f32)
        value_acc[...] = jnp.zeros((rows, DH), f32)

    @pl.when(b == 0)
    def _():
        query_acc[h] = jnp.zeros((DH, rows), f32) if first else carry[0][0]

    @pl.when(place[1] >= shift + b)
    def _():
        key, value = kv_ref[0, :, :DH], kv_ref[0, :, DH:]
        query, grad = stack_rows(query_refs), stack_rows(grad_refs)
        step = min(CHUNK, rows)
        for at in range(0, rows, step):
            span = slice(at, at + step)
            scores = nt(key, query[span]) * (LOG2E * DH**-0.5) - log_ref[0, :, span]
            if shift == 0:
                mask = diagonal_mask(place[0], rows, at, step, tokens, rows)
                scores = jnp.where(mask, scores, negative_fill)
            probs = jnp.exp2(scores)
            score_grad = (probs * (nt(value, grad[span]) - delta_ref[0, :, span])).astype(bf16)
            value_acc[...] += nn(probs.astype(bf16), grad[span])
            key_acc[...] += nn(score_grad, query[span])
            query_acc[h, :, span] += tn(key, score_grad)

    @pl.when(h == pl.num_programs(1) - 1)
    def _():
        kv_grad_ref[0, :, :DH] = (key_acc[...] * DH**-0.5).astype(kv_grad_ref.dtype)
        kv_grad_ref[0, :, DH:] = value_acc[...].astype(kv_grad_ref.dtype)

    @pl.when(b == pl.num_programs(0) - 1)
    def _():
        if not last:
            outs[0][0] = query_acc[h]
            return
        query_grad = (query_acc[h] * DH**-0.5).T.astype(bf16)
        for i in range(fold):
            outs[i][...] = query_grad[i * tokens : (i + 1) * tokens]


def soft_backward(place, queries, grads, logs, deltas, kv, shift, carry, last):
    fold, tokens = len(queries), queries[0].shape[0]
    group = queries[0].shape[1] // DH // fold
    blocks, rows = kv.shape[0], kv.shape[1]
    first = carry is None
    row_specs = soft_specs(fold, tokens, group, lambda b, h, p: h)
    line = pl.BlockSpec((1, 1, rows), lambda b, h, p: (h, 0, 0))
    tall = pl.BlockSpec((1, DH, rows), lambda b, h, p: (h, 0, 0))
    kv_spec = pl.BlockSpec((1, rows, 2 * DH), lambda b, h, p: (b, 0, 0))
    arrays = list(queries) + list(grads) + [logs, deltas, kv]
    specs = row_specs + row_specs + [line, line, kv_spec]
    if not first:
        arrays, specs = arrays + [carry], specs + [tall]
    outs = [jax.ShapeDtypeStruct((blocks, rows, 2 * DH), f32 if last else bf16)]
    out_specs = [kv_spec]
    if last:
        half = pl.BlockSpec((tokens, DH), lambda b, h, p: (0, h))
        out_specs += [half] * fold
        outs += [jax.ShapeDtypeStruct((tokens, group * DH), bf16)] * fold
    else:
        out_specs += [tall]
        outs += [jax.ShapeDtypeStruct((group, DH, rows), f32)]
    scratch = [
        pltpu.VMEM((rows, DH), f32),
        pltpu.VMEM((rows, DH), f32),
        pltpu.VMEM((group, DH, rows), f32),
    ]
    kernel = functools.partial(soft_backward_kernel, fold, tokens, shift, first, last)
    flops = 10 * group * blocks * rows * rows * DH
    return soft_call(kernel, place, (blocks, group), specs, arrays, out_specs, outs, scratch, flops)


def body(
    lin_query,
    lin_key,
    lin_value,
    log_decay,
    norm_gain,
    lin_gate,
    lin_grad,
    soft_query,
    soft_key,
    soft_value,
    soft_grad,
):
    count = lax.axis_size("ctx")
    kv_heads = soft_key.shape[1] // DH
    fold = 2 if kv_heads == 2 and count % 2 == 0 else 1
    laps = count // fold
    index = lax.axis_index("ctx")
    y, z = lax.rem(index, fold), lax.div(index, fold)
    place = jnp.stack((y, z)).astype(jnp.int32)
    tokens = soft_query.shape[0]
    rows = tokens * fold
    heads = lin_query.shape[1] // DH
    group = heads // fold
    width = lin_query.shape[1] * lax.axis_size("tp")
    gain = norm_gain[None, :]

    def swap(a):
        return lax.ppermute(a, "ctx", [(i, i ^ 1) for i in range(count)])

    def up(a, s):
        return lax.ppermute(a, "ctx", [(i, i + fold * s) for i in range(count - fold * s)])

    def down(a, s):
        return lax.ppermute(a, "ctx", [(i + fold * s, i) for i in range(count - fold * s)])

    def columns(a, part):
        size = a.shape[1] // fold
        return lax.dynamic_slice_in_dim(a, part * size, size, 1) if fold > 1 else a

    def joined(own, rec):
        if fold == 1:
            return own
        low, high = jnp.where(y == 0, own, rec), jnp.where(y == 0, rec, own)
        return jnp.concatenate((low, high), axis=1)

    kv = jnp.concatenate((columns(soft_key, y), columns(soft_value, y)), axis=1)
    queries, grads = [soft_query], [soft_grad]
    if fold > 1:
        kv_sent = jnp.concatenate((columns(soft_key, 1 - y), columns(soft_value, 1 - y)), axis=1)
        kv = jnp.concatenate((kv, swap(kv_sent)), axis=0)
        queries.append(swap(columns(soft_query, 1 - y)))
        grads.append(swap(columns(soft_grad, 1 - y)))
    stack = laps > 8
    kv_far = [up(kv, s) for s in range(1, laps)]

    msg_rows = group * DH + extra_rows(group)
    msg = jax.ShapeDtypeStruct((msg_rows, DH), bf16)
    msgs = jax.ShapeDtypeStruct((fold, msg_rows, DH), bf16)
    state = jax.ShapeDtypeStruct((group * DH, DH), bf16)
    flat = jax.ShapeDtypeStruct((tokens, heads * DH), bf16)
    state_msgs, log_rows, log_cols = whole_call(
        functools.partial(lin_state_kernel, heads, fold),
        place,
        (log_decay, lin_key, lin_value),
        [
            msgs,
            jax.ShapeDtypeStruct((heads, tokens), f32),
            jax.ShapeDtypeStruct((tokens, heads), f32),
        ],
        2 * heads * tokens * DH * DH,
    )

    def carry_over(own, other, backward):
        rec = swap(other) if fold > 1 else own
        joint = own
        if fold > 1:
            (joint,) = whole_call(
                functools.partial(lin_pair_kernel, group, backward), place, (own, rec), [msg]
            )
        far = [(down if backward else up)(joint, s) for s in range(1, laps)]
        got = whole_call(
            functools.partial(lin_scan_kernel, group, fold, laps - 1, backward),
            place,
            (own, rec, *far),
            [state] * fold,
        )
        return (got[0], swap(got[1])) if fold > 1 else tuple(got)

    own_msg, oth_msg = state_msgs[0], state_msgs[fold - 1]
    carried = carry_over(own_msg, oth_msg, False)
    square = 2 * heads * tokens * tokens * DH
    attended, stats = whole_call(
        functools.partial(lin_attend_kernel, heads, fold),
        place,
        (log_rows, log_cols, lin_query, lin_key, lin_value, lin_gate, lin_grad, gain, *carried),
        [
            jax.ShapeDtypeStruct((tokens, heads * DH), f32),
            jax.ShapeDtypeStruct((8, tokens), f32),
        ],
        3 * square,
    )
    stats = lax.psum(stats, "tp")
    lin_out, lin_gate_grad, att_grad, back_msgs = whole_call(
        functools.partial(lin_norm_kernel, heads, fold, width),
        place,
        (log_rows, stats, attended, lin_gate, lin_grad, gain, lin_query, own_msg, oth_msg),
        [flat, flat, flat, msgs],
        square,
    )
    returned = carry_over(back_msgs[0], back_msgs[fold - 1], True)
    lin_query_grad, lin_key_grad, lin_value_grad = whole_call(
        functools.partial(lin_grad_kernel, heads, fold),
        place,
        (log_rows, log_cols, lin_query, lin_key, lin_value, att_grad, *carried, *returned),
        [flat, flat, flat],
        8 * square,
    )

    if stack:
        steps = [(0, kv[None]), (1, jnp.stack(kv_far))]
    else:
        steps = [(s, a[None]) for s, a in enumerate([kv] + kv_far)]
    carry = None
    for s, blocks in steps:
        carry = soft_forward(place, queries, grads, blocks, s, carry, s == steps[-1][0])
    outs, (logs, deltas) = carry[:fold], carry[fold:]
    carry = None
    terms = []
    for s, blocks in steps[::-1]:
        kv_grad, *carry = soft_backward(
            place, queries, grads, logs, deltas, blocks, s, carry[0] if carry else None, s == 0
        )
        if s > 0:
            terms += [down(kv_grad[i], s + i) for i in range(blocks.shape[0])]
    total = kv_grad[0]
    for term in terms:
        total = total + term.astype(f32)
    total = total.astype(bf16)
    kv_own = total[:tokens]
    kv_rec = swap(total[tokens:]) if fold > 1 else None
    if fold > 1:
        soft_out = joined(outs[0], swap(outs[1]))
        soft_query_grad = joined(carry[0], swap(carry[1]))
        soft_key_grad = joined(kv_own[:, :DH], kv_rec[:, :DH])
        soft_value_grad = joined(kv_own[:, DH:], kv_rec[:, DH:])
    else:
        soft_out, soft_query_grad = outs[0], carry[0]
        soft_key_grad, soft_value_grad = kv_own[:, :DH], kv_own[:, DH:]
    return (
        lin_out,
        lin_query_grad,
        lin_key_grad,
        lin_value_grad,
        lin_gate_grad,
        soft_out,
        soft_query_grad,
        soft_key_grad,
        soft_value_grad,
    )


def solution(mesh):
    spread = P("ctx", "tp")
    return jax.shard_map(
        body,
        mesh=mesh,
        in_specs=(spread, spread, spread, P("tp", "ctx"), P("tp")) + (spread,) * 6,
        out_specs=(spread,) * 9,
        check_vma=False,
    )
```

time: 405 us -> 150 us (0.37)
  waiting for transfers between devices: 240 us -> 43.2 us
  starting transfers between devices: 0.25 us -> 49.4 us
  Pallas kernels: 0 us -> 31.8 us
  matrix products: 29.6 us -> 0 us
  blocking collectives: 35.7 us -> 7.02 us
  local copies, waits for them, and re-layouts: 40.5 us -> 11.9 us
  other arithmetic: 32.3 us -> 4.55 us
  between operations: 15.4 us -> 1.26 us
  loops' own time: 9.33 us -> 0 us
    reduce_scatter x2 -> x0, waiting for transfers between devices: 160 us -> none  [the longest x1 93.6 us: soft_attention(): lax.psum_scatter(key_terms.reshape(key_count, key_width).astype(jnp.bfloa...]
    all_gather x4 -> x0, waiting for transfers between devices: 79 us -> none  [the longest x1 41.1 us: body(): lax.all_gather(soft_key, 'ctx', axis=0, tiled=True)]
    ppermute x0 -> x22, starting transfers between devices: none -> 49.4 us  [the longest x6 30.1 us: up(): lax.ppermute(a, 'ctx', [(i, i + fold * s) for i in range(count - fold * s)])]
    ppermute x0 -> x22, waiting for transfers between devices: none -> 43.2 us  [the longest x6 24.7 us: down(): lax.ppermute(a, 'ctx', [(i + fold * s, i) for i in range(count - fold * s)])]
    pallas_call x0 -> x16, Pallas kernels: none -> 31.8 us  [the longest x8 19.2 us: soft_call(): pl.pallas_call(kernel, out_shape=outs, grid_spec=pltpu.PrefetchScalarGrid...]
    dot_general x26 -> x0, matrix products: 29.6 us -> none  [the longest x1 3.1 us: lightning(): jnp.einsum('shd,she->hde', key_tail, value_f, precision=top_precision)]
    unnamed x1 -> x0, blocking collectives: 23.3 us -> none
    add x22 -> x0, other arithmetic: 15.7 us -> none  [the longest x4 7.91 us: soft_block_step(): running[1] + second_part[0]]
  transfers between devices with their start and end apart: 6 -> 22, of which waited for: 5 -> 6; matrix products, arithmetic and copies ran while one was open for 24% -> 4% of each run, Pallas kernels for 0% -> 19%
where the time goes in v1:
time: 150 us; the launch traced here: 149 us
  starting transfers between devices  49.4 us (33%)
  waiting for transfers between devices  43.2 us (29%)
  Pallas kernels  31.8 us (21%)
  local copies, waits for them, and re-layouts  11.9 us (8%)
  blocking collectives  7.02 us (5%)
  other arithmetic  4.55 us (3%)
    ppermute x6, starting transfers between devices, up(): lax.ppermute(a, 'ctx', [(i, i + fold * s) for i in range(count - fold * s)])  30.1 us
    ppermute x6, waiting for transfers between devices, down(): lax.ppermute(a, 'ctx', [(i + fold * s, i) for i in range(count - fold * s)])  24.7 us
    pallas_call x8, Pallas kernels, soft_call(): pl.pallas_call(kernel, out_shape=outs, grid_spec=pltpu.PrefetchScalarGrid...  19.2 us
    pallas_call x8, Pallas kernels, whole_call(): pl.pallas_call(kernel, out_shape=outs, in_specs=[SMEM_SPEC] + [VMEM_SPEC]...  12.7 us
    ppermute x10, starting transfers between devices, swap(): return lax.ppermute(a, 'ctx', [(i, i ^ 1) for i in range(count)])  11.5 us
    unnamed x82, local copies, waits for them, and re-layouts  10.2 us
    ppermute x10, waiting for transfers between devices, swap(): return lax.ppermute(a, 'ctx', [(i, i ^ 1) for i in range(count)])  9.61 us
    ppermute x6, waiting for transfers between devices, up(): lax.ppermute(a, 'ctx', [(i, i + fold * s) for i in range(count - fold * s)])  8.91 us
  transfers between devices with their start and end apart: 22, of which 6 were waited for; matrix products, arithmetic and copies ran while one was open for 4% of the time, Pallas kernels for 19%

profile of v1, /device:TPU:0, one launch (start us, length us, event | category | flops | bytes accessed | tf_op | source)
XLA Modules:
  0.0 149.2 jit_solution(14593657170580622694)
XLA Ops:
  1.7 3.0 %collective-permute-start.12 = (bf16[256,256]{1,0:T(8,128)(2,1)S(1)}, bf16[256,256]{1,0:T(8,128)(2,1)S(1)}, u32[]{:S(2)}, u32[]{:S(2)}) collective-permute-start(bf16[256,256]{1,0:T(8,128)(2,1)S(1)} %pad_maximum_fusion.3), channel_id=1, source_target_pairs={{0,4},{4,0},{8,12},{12,8},{16,20},{20,16},{24,28},{28,24},{1,5},{5... | collective-permute-start | bytes 393224 | tf_op jit(solution)/shard_map/ppermute | solution.py:476
  5.9 1.4 shard_map.178
  8.6 1.5 collective-permute-start.10
  10.1 4.4 %collective-permute-done.rec_ref = bf16[528,128]{1,0:T(8,128)(2,1)S(1)} collective-permute-done((bf16[528,128]{1,0:T(8,128)(2,1)S(1)}, bf16[528,128]{1,0:T(8,128)(2,1)S(1)}, u32[]{:S(2)}, u32[]{:S(2)}) %collective-permute-start) | collective-permute-done | bytes 135200 | tf_op jit(solution)/shard_map/ppermute | solution.py:476
  15.1 3.5 %collective-permute-start.1 = (bf16[528,128]{1,0:T(8,128)(2,1)S(1)}, bf16[528,128]{1,0:T(8,128)(2,1)S(1)}, u32[]{:S(2)}, u32[]{:S(2)}) collective-permute-start(bf16[528,128]{1,0:T(8,128)(2,1)S(1)} %shard_map.179), channel_id=1, source_target_pairs={{0,8},{4,12},{8,16},{12,20},{16,24},{20,28},{1,9},{5,13},{9,17},{1... | collective-permute-start | bytes 405512 | tf_op jit(solution)/shard_map/ppermute | solution.py:479
  18.7 3.5 %collective-permute-start.15 = (bf16[512,256]{1,0:T(8,128)(2,1)S(1)}, bf16[512,256]{1,0:T(8,128)(2,1)S(1)}, u32[]{:S(2)}, u32[]{:S(2)}) collective-permute-start(bf16[512,256]{1,0:T(8,128)(2,1)S(1)} %get-tuple-element.98), channel_id=1, source_target_pairs={{0,8},{4,12},{8,16},{12,20},{16,24},{20,28},{1,9},{5,13},{9,17},{1... | collective-permute-start | bytes 786440 | tf_op jit(solution)/shard_map/ppermute | solution.py:479
  22.2 2.9 %collective-permute-start.14 = (bf16[512,256]{1,0:T(8,128)(2,1)S(1)}, bf16[512,256]{1,0:T(8,128)(2,1)S(1)}, u32[]{:S(2)}, u32[]{:S(2)}) collective-permute-start(bf16[512,256]{1,0:T(8,128)(2,1)S(1)} %get-tuple-element.98), channel_id=1, source_target_pairs={{0,16},{4,20},{8,24},{12,28},{1,17},{5,21},{9,25},{13,29},{2,18},{... | collective-permute-start | bytes 786440 | tf_op jit(solution)/shard_map/ppermute | solution.py:479
  28.4 8.9 %collective-permute-done.2.rest_1_ = bf16[528,128]{1,0:T(8,128)(2,1)S(1)} collective-permute-done((bf16[528,128]{1,0:T(8,128)(2,1)S(1)}, bf16[528,128]{1,0:T(8,128)(2,1)S(1)}, u32[]{:S(2)}, u32[]{:S(2)}) %collective-permute-start.2) | collective-permute-done | bytes 135200 | tf_op jit(solution)/shard_map/ppermute | solution.py:479
  37.3 17.6 %collective-permute-start.3 = (bf16[528,128]{1,0:T(8,128)(2,1)S(1)}, bf16[528,128]{1,0:T(8,128)(2,1)S(1)}, u32[]{:S(2)}, u32[]{:S(2)}) collective-permute-start(bf16[528,128]{1,0:T(8,128)(2,1)S(1)} %shard_map.179), channel_id=1, source_target_pairs={{0,24},{4,28},{1,25},{5,29},{2,26},{6,30},{3,27},{7,31}} | collective-permute-start | bytes 405512 | tf_op jit(solution)/shard_map/ppermute | solution.py:479
  54.9 4.6 %shard_map.186 = (f32[4,1,512]{2,1,0:T(1,128)S(1)}, f32[4,1,512]{2,1,0:T(1,128)S(1)}, f32[4,128,512]{2,1,0:T(8,128)S(1)}) custom-call(s32[2]{0:T(128)S(1)} %pad_add_fusion.place, bf16[256,1024]{1,0:T(8,128)(2,1)S(1)} %copy-done, bf16[256,512]{1,0:T(8,128)(2,1)S(1)} %collective-permute-done.10.refs_1_, bf16[1,512,256]{2,1,0:T(8,128)(2,1)S(1)} %get-tuple-element.97.refs_2_.refs_6_), custom_call_target="tpu_custom_call" | custom-call | flops 536870912 | bytes 1048576 | tf_op jit(solution)/shard_map/pallas_call | solution.py:317
  60.2 1.4 collective-permute-start.4
  63.6 1.7 %shard_map.189 = (bf16[256,512]{1,0:T(8,128)(2,1)S(1)}, bf16[256,512]{1,0:T(8,128)(2,1)S(1)}, f32[4,1,512]{2,1,0:T(1,128)S(1)}, f32[4,1,512]{2,1,0:T(1,128)S(1)}) custom-call(s32[2]{0:T(128)S(1)} %pad_add_fusion.place, bf16[256,1024]{1,0:T(8,128)(2,1)S(1)} %copy-done, bf16[256,512]{1,0:T(8,128)(2,1)S(1)} %collective-permute-done.10.refs_1_, ...), custom_call_target="tpu_custom_call" | custom-call | flops 536870912 | bytes 2899968 | tf_op jit(solution)/shard_map/pallas_call | solution.py:317
  65.4 1.9 %shard_map.190 = (bf16[1,512,256]{2,1,0:T(8,128)(2,1)}, f32[4,128,512]{2,1,0:T(8,128)S(1)}) custom-call(s32[2]{0:T(128)S(1)} %pad_add_fusion.place, bf16[256,1024]{1,0:T(8,128)(2,1)S(1)} %copy-done, bf16[256,512]{1,0:T(8,128)(2,1)S(1)} %collective-permute-done.10.refs_1_, bf16[256,1024]{1,0:T(8,128)(2,1)S(1)} %copy-done.7, ...), custom_call_target="tpu_custom_call" | custom-call | flops 1342177280 | bytes 1851392 | tf_op jit(solution)/shard_map/pallas_call | solution.py:317
  67.3 1.9 %shard_map.191 = (bf16[1,512,256]{2,1,0:T(8,128)(2,1)}, f32[4,128,512]{2,1,0:T(8,128)S(1)}) custom-call(s32[2]{0:T(128)S(1)} %pad_add_fusion.place, bf16[256,1024]{1,0:T(8,128)(2,1)S(1)} %copy-done, bf16[256,512]{1,0:T(8,128)(2,1)S(1)} %collective-permute-done.10.refs_1_, bf16[256,1024]{1,0:T(8,128)(2,1)S(1)} %copy-done.7, ...), custom_call_target="tpu_custom_call" | custom-call | flops 1342177280 | bytes 2899968 | tf_op jit(solution)/shard_map/pallas_call | solution.py:317
  69.2 1.9 %shard_map.192 = (bf16[1,512,256]{2,1,0:T(8,128)(2,1)}, f32[4,128,512]{2,1,0:T(8,128)S(1)}) custom-call(s32[2]{0:T(128)S(1)} %pad_add_fusion.place, bf16[256,1024]{1,0:T(8,128)(2,1)S(1)} %copy-done, bf16[256,512]{1,0:T(8,128)(2,1)S(1)} %collective-permute-done.10.refs_1_, bf16[256,1024]{1,0:T(8,128)(2,1)S(1)} %copy-done.7, ...), custom_call_target="tpu_custom_call" | custom-call | flops 1342177280 | bytes 2899968 | tf_op jit(solution)/shard_map/pallas_call | solution.py:317
  75.1 2.0 %shard_map.181 = (f32[256,1024]{1,0:T(8,128)S(1)}, f32[8,256]{1,0:T(8,128)S(1)}) custom-call(s32[2]{0:T(128)S(1)} %pad_add_fusion.place, f32[8,256]{1,0:T(8,128)S(1)} %get-tuple-element.47.row_ref, f32[256,8]{1,0:T(8,128)S(1)} %copy-done.20, bf16[256,1024]{1,0:T(8,128)(2,1)S(1)} %copy-done.3, bf16[256,1024]{1,0:T(8,128)(2,1)S(1)} %copy-done.4, ...), custom_call_target="tpu_custom_call" | custom-call | flops 402653184 | bytes 3960832 | tf_op jit(solution)/shard_map/pallas_call | solution.py:38
  78.7 7.0 %psum.7.stat_ref = f32[8,256]{1,0:T(8,128)} all-reduce(f32[8,256]{1,0:T(8,128)} %copy-done.30), channel_id=1, replica_groups=mesh['ctx'=8,'tp'=4] {'tp'}, use_global_device_ids=true, to_apply=%region_0.0 | all-reduce | flops 2048 | bytes 16384 | tf_op jit(solution)/shard_map/psum | solution.py:550
  89.3 2.5 %shard_map.182 = (bf16[256,1024]{1,0:T(8,128)(2,1)}, bf16[256,1024]{1,0:T(8,128)(2,1)}, bf16[256,1024]{1,0:T(8,128)(2,1)S(1)}, bf16[2,528,128]{2,1,0:T(8,128)(2,1)S(1)}) custom-call(s32[2]{0:T(128)S(1)} %pad_add_fusion.place, f32[8,256]{1,0:T(8,128)S(1)} %get-tuple-element.47.row_ref, f32[8,256]{1,0:T(8,128)S(1)} %copy-done.26, f32[256,1024]{1,0:T(8,128)S(1)} %copy-done.10, ...), custom_call_target="tpu_custom_call" | custom-call | flops 134217728 | bytes 4755456 | tf_op jit(solution)/shard_map/pallas_call | solution.py:38
  96.5 5.2 %shard_map.193 = (f32[1,512,256]{2,1,0:T(8,128)S(1)}, bf16[256,512]{1,0:T(8,128)(2,1)S(1)}, bf16[256,512]{1,0:T(8,128)(2,1)S(1)}) custom-call(s32[2]{0:T(128)S(1)} %pad_add_fusion.place, bf16[256,1024]{1,0:T(8,128)(2,1)S(1)} %copy-done, bf16[256,512]{1,0:T(8,128)(2,1)S(1)} %collective-permute-done.10.refs_1_, bf16[256,1024]{1,0:T(8,128)(2,1)S(1)} %copy-done.8, ...), custom_call_target="tpu_custom_call" | custom-call | flops 1342177280 | bytes 2899968 | tf_op jit(solution)/shard_map/pallas_call | solution.py:317
  107.0 3.3 %collective-permute-done.18 = bf16[512,256]{1,0:T(8,128)(2,1)} collective-permute-done((bf16[512,256]{1,0:T(8,128)(2,1)}, bf16[512,256]{1,0:T(8,128)(2,1)}, u32[]{:S(2)}, u32[]{:S(2)}) %collective-permute-start.18) | collective-permute-done | bytes 262176 | tf_op jit(solution)/shard_map/ppermute | solution.py:482
  113.2 2.9 %collective-permute-done.16 = bf16[256,512]{1,0:T(8,128)(2,1)S(1)} collective-permute-done((bf16[256,512]{1,0:T(8,128)(2,1)S(1)}, bf16[256,512]{1,0:T(8,128)(2,1)S(1)}, u32[]{:S(2)}, u32[]{:S(2)}) %collective-permute-start.16) | collective-permute-done | bytes 262176 | tf_op jit(solution)/shard_map/ppermute | solution.py:476
  117.9 21.4 %collective-permute-done.8.rest_2_ = bf16[528,128]{1,0:T(8,128)(2,1)S(1)} collective-permute-done((bf16[528,128]{1,0:T(8,128)(2,1)S(1)}, bf16[528,128]{1,0:T(8,128)(2,1)S(1)}, u32[]{:S(2)}, u32[]{:S(2)}) %collective-permute-start.8) | collective-permute-done | bytes 135200 | tf_op jit(solution)/shard_map/ppermute | solution.py:482
  142.8 2.3 %collective-permute-done.9.rest_3_ = bf16[512,128]{1,0:T(8,128)(2,1)S(1)} collective-permute-done((bf16[512,128]{1,0:T(8,128)(2,1)S(1)}, bf16[512,128]{1,0:T(8,128)(2,1)S(1)}, u32[]{:S(2)}, u32[]{:S(2)}) %collective-permute-start.9) | collective-permute-done | bytes 131104 | tf_op jit(solution)/shard_map/ppermute | solution.py:476
  145.1 4.1 %shard_map.185 = (bf16[256,1024]{1,0:T(8,128)(2,1)}, bf16[256,1024]{1,0:T(8,128)(2,1)}, bf16[256,1024]{1,0:T(8,128)(2,1)}) custom-call(s32[2]{0:T(128)S(1)} %pad_add_fusion.place, f32[8,256]{1,0:T(8,128)S(1)} %get-tuple-element.47.row_ref, f32[256,8]{1,0:T(8,128)S(1)} %copy-done.21, bf16[256,1024]{1,0:T(8,128)(2,1)S(1)} %copy-done.3, ...), custom_call_target="tpu_custom_call" | custom-call | flops 1073741824 | bytes 4210688 | tf_op jit(solution)/shard_map/pallas_call | solution.py:38
  (136 shorter events, 36.9 us)
Async XLA Ops:
  1.7 16.9 %collective-permute-start.12 = (bf16[256,256]{1,0:T(8,128)(2,1)S(1)}, bf16[256,256]{1,0:T(8,128)(2,1)S(1)}, u32[]{:S(2)}, u32[]{:S(2)}) collective-permute-start(bf16[256,256]{1,0:T(8,128)(2,1)S(1)} %pad_maximum_fusion.3), channel_id=1, source_target_pairs={{0,4},{4,0},{8,12},{12,8},{16,20},{20,16},{24,28},{28,24},{1,5},{5... | collective-permute-start | bytes 393224 | tf_op jit(solution)/shard_map/ppermute | solution.py:476
  8.0 6.5 %collective-permute-start = (bf16[528,128]{1,0:T(8,128)(2,1)S(1)}, bf16[528,128]{1,0:T(8,128)(2,1)S(1)}, u32[]{:S(2)}, u32[]{:S(2)}) collective-permute-start(bf16[528,128]{1,0:T(8,128)(2,1)S(1)} %get-tuple-element.95.oth_ref), channel_id=1, source_target_pairs={{0,4},{4,0},{8,12},{12,8},{16,20},{20,16},{24,28},{28,24},{1,5},{5... | collective-permute-start | bytes 405512 | tf_op jit(solution)/shard_map/ppermute | solution.py:476
  8.6 17.8 %collective-permute-start.10 = (bf16[256,512]{1,0:T(8,128)(2,1)S(1)}, bf16[256,512]{1,0:T(8,128)(2,1)S(1)}, u32[]{:S(2)}, u32[]{:S(2)}) collective-permute-start(bf16[256,512]{1,0:T(8,128)(2,1)S(1)} %constant_dynamic-slice_fusion.5), channel_id=1, source_target_pairs={{0,4},{4,0},{8,12},{12,8},{16,20},{20,16},{24,28},{28,24},{1,5},{5... | collective-permute-start | bytes 786440 | tf_op jit(solution)/shard_map/ppermute | solution.py:476
  15.1 12.0 %collective-permute-start.1 = (bf16[528,128]{1,0:T(8,128)(2,1)S(1)}, bf16[528,128]{1,0:T(8,128)(2,1)S(1)}, u32[]{:S(2)}, u32[]{:S(2)}) collective-permute-start(bf16[528,128]{1,0:T(8,128)(2,1)S(1)} %shard_map.179), channel_id=1, source_target_pairs={{0,8},{4,12},{8,16},{12,20},{16,24},{20,28},{1,9},{5,13},{9,17},{1... | collective-permute-start | bytes 405512 | tf_op jit(solution)/shard_map/ppermute | solution.py:479
  18.6 36.2 %copy-start.13 = (bf16[1,512,256]{2,1,0:T(8,128)(2,1)}, bf16[1,512,256]{2,1,0:T(8,128)(2,1)S(1)}, u32[]{:S(2)}) copy-start(bf16[1,512,256]{2,1,0:T(8,128)(2,1)S(1)} %get-tuple-element.97.refs_2_.refs_6_) | copy-start | bytes 786436
  18.7 43.0 %collective-permute-start.15 = (bf16[512,256]{1,0:T(8,128)(2,1)S(1)}, bf16[512,256]{1,0:T(8,128)(2,1)S(1)}, u32[]{:S(2)}, u32[]{:S(2)}) collective-permute-start(bf16[512,256]{1,0:T(8,128)(2,1)S(1)} %get-tuple-element.98), channel_id=1, source_target_pairs={{0,8},{4,12},{8,16},{12,20},{16,24},{20,28},{1,9},{5,13},{9,17},{1... | collective-permute-start | bytes 786440 | tf_op jit(solution)/shard_map/ppermute | solution.py:479
  22.2 40.4 %collective-permute-start.14 = (bf16[512,256]{1,0:T(8,128)(2,1)S(1)}, bf16[512,256]{1,0:T(8,128)(2,1)S(1)}, u32[]{:S(2)}, u32[]{:S(2)}) collective-permute-start(bf16[512,256]{1,0:T(8,128)(2,1)S(1)} %get-tuple-element.98), channel_id=1, source_target_pairs={{0,16},{4,20},{8,24},{12,28},{1,17},{5,21},{9,25},{13,29},{2,18},{... | collective-permute-start | bytes 786440 | tf_op jit(solution)/shard_map/ppermute | solution.py:479
  25.1 12.2 %collective-permute-start.2 = (bf16[528,128]{1,0:T(8,128)(2,1)S(1)}, bf16[528,128]{1,0:T(8,128)(2,1)S(1)}, u32[]{:S(2)}, u32[]{:S(2)}) collective-permute-start(bf16[528,128]{1,0:T(8,128)(2,1)S(1)} %shard_map.179), channel_id=1, source_target_pairs={{0,16},{4,20},{8,24},{12,28},{1,17},{5,21},{9,25},{13,29},{2,18},{... | collective-permute-start | bytes 405512 | tf_op jit(solution)/shard_map/ppermute | solution.py:479
  26.5 37.1 %collective-permute-start.11 = (bf16[256,512]{1,0:T(8,128)(2,1)S(1)}, bf16[256,512]{1,0:T(8,128)(2,1)S(1)}, u32[]{:S(2)}, u32[]{:S(2)}) collective-permute-start(bf16[256,512]{1,0:T(8,128)(2,1)S(1)} %constant_dynamic-slice_fusion.4), channel_id=1, source_target_pairs={{0,4},{4,0},{8,12},{12,8},{16,20},{20,16},{24,28},{28,24},{1,5},{5... | collective-permute-start | bytes 786440 | tf_op jit(solution)/shard_map/ppermute | solution.py:476
  27.1 36.5 %collective-permute-start.13 = (bf16[512,256]{1,0:T(8,128)(2,1)S(1)}, bf16[512,256]{1,0:T(8,128)(2,1)S(1)}, u32[]{:S(2)}, u32[]{:S(2)}) collective-permute-start(bf16[512,256]{1,0:T(8,128)(2,1)S(1)} %get-tuple-element.98), channel_id=1, source_target_pairs={{0,24},{4,28},{1,25},{5,29},{2,26},{6,30},{3,27},{7,31}} | collective-permute-start | bytes 786440 | tf_op jit(solution)/shard_map/ppermute | solution.py:479
  37.3 22.3 %collective-permute-start.3 = (bf16[528,128]{1,0:T(8,128)(2,1)S(1)}, bf16[528,128]{1,0:T(8,128)(2,1)S(1)}, u32[]{:S(2)}, u32[]{:S(2)}) collective-permute-start(bf16[528,128]{1,0:T(8,128)(2,1)S(1)} %shard_map.179), channel_id=1, source_target_pairs={{0,24},{4,28},{1,25},{5,29},{2,26},{6,30},{3,27},{7,31}} | collective-permute-start | bytes 405512 | tf_op jit(solution)/shard_map/ppermute | solution.py:479
  60.2 14.8 %copy-start.22 = (bf16[512,128]{1,0:T(8,128)(2,1)}, bf16[512,128]{1,0:T(8,128)(2,1)S(1)}, u32[]{:S(2)}) copy-start(bf16[512,128]{1,0:T(8,128)(2,1)S(1)} %get-tuple-element.50.rest_0_) | copy-start | bytes 393220
  60.2 14.8 %collective-permute-start.4 = (bf16[512,128]{1,0:T(8,128)(2,1)S(1)}, bf16[512,128]{1,0:T(8,128)(2,1)S(1)}, u32[]{:S(2)}, u32[]{:S(2)}) collective-permute-start(bf16[512,128]{1,0:T(8,128)(2,1)S(1)} %get-tuple-element.51), channel_id=1, source_target_pairs={{0,4},{4,0},{8,12},{12,8},{16,20},{20,16},{24,28},{28,24},{1,5},{5... | collective-permute-start | bytes 393224 | tf_op jit(solution)/shard_map/ppermute | solution.py:476
  71.1 33.3 %collective-permute-start.20 = (bf16[512,256]{1,0:T(8,128)(2,1)}, bf16[512,256]{1,0:T(8,128)(2,1)}, u32[]{:S(2)}, u32[]{:S(2)}) collective-permute-start(bf16[512,256]{1,0:T(8,128)(2,1)} %bitcast.14), channel_id=1, source_target_pairs={{8,0},{12,4},{16,8},{20,12},{24,16},{28,20},{9,1},{13,5},{17,9},{2... | collective-permute-start | bytes 786440 | tf_op jit(solution)/shard_map/ppermute | solution.py:482
  72.4 33.3 %collective-permute-start.19 = (bf16[512,256]{1,0:T(8,128)(2,1)}, bf16[512,256]{1,0:T(8,128)(2,1)}, u32[]{:S(2)}, u32[]{:S(2)}) collective-permute-start(bf16[512,256]{1,0:T(8,128)(2,1)} %bitcast.13), channel_id=1, source_target_pairs={{16,0},{20,4},{24,8},{28,12},{17,1},{21,5},{25,9},{29,13},{18,2},{... | collective-permute-start | bytes 786440 | tf_op jit(solution)/shard_map/ppermute | solution.py:482
  73.7 36.6 %collective-permute-start.18 = (bf16[512,256]{1,0:T(8,128)(2,1)}, bf16[512,256]{1,0:T(8,128)(2,1)}, u32[]{:S(2)}, u32[]{:S(2)}) collective-permute-start(bf16[512,256]{1,0:T(8,128)(2,1)} %bitcast.12), channel_id=1, source_target_pairs={{24,0},{28,4},{25,1},{29,5},{26,2},{30,6},{27,3},{31,7}} | collective-permute-start | bytes 786440 | tf_op jit(solution)/shard_map/ppermute | solution.py:482
  92.6 10.4 %collective-permute-start.5 = (bf16[528,128]{1,0:T(8,128)(2,1)}, bf16[528,128]{1,0:T(8,128)(2,1)S(1)}, u32[]{:S(2)}, u32[]{:S(2)}) collective-permute-start(bf16[528,128]{1,0:T(8,128)(2,1)} %get-tuple-element.93), channel_id=1, source_target_pairs={{0,4},{4,0},{8,12},{12,8},{16,20},{20,16},{24,28},{28,24},{1,5},{5... | collective-permute-start | bytes 405512 | tf_op jit(solution)/shard_map/ppermute | solution.py:476
  101.7 11.2 %collective-permute-start.17 = (bf16[256,512]{1,0:T(8,128)(2,1)S(1)}, bf16[256,512]{1,0:T(8,128)(2,1)S(1)}, u32[]{:S(2)}, u32[]{:S(2)}) collective-permute-start(bf16[256,512]{1,0:T(8,128)(2,1)S(1)} %get-tuple-element.80), channel_id=1, source_target_pairs={{0,4},{4,0},{8,12},{12,8},{16,20},{20,16},{24,28},{28,24},{1,5},{5... | collective-permute-start | bytes 786440 | tf_op jit(solution)/shard_map/ppermute | solution.py:476
  103.1 13.1 %collective-permute-start.16 = (bf16[256,512]{1,0:T(8,128)(2,1)S(1)}, bf16[256,512]{1,0:T(8,128)(2,1)S(1)}, u32[]{:S(2)}, u32[]{:S(2)}) collective-permute-start(bf16[256,512]{1,0:T(8,128)(2,1)S(1)} %copy-done.34), channel_id=1, source_target_pairs={{0,4},{4,0},{8,12},{12,8},{16,20},{20,16},{24,28},{28,24},{1,5},{5... | collective-permute-start | bytes 786440 | tf_op jit(solution)/shard_map/ppermute | solution.py:476
  104.4 13.5 %collective-permute-start.6 = (bf16[528,128]{1,0:T(8,128)(2,1)S(1)}, bf16[528,128]{1,0:T(8,128)(2,1)S(1)}, u32[]{:S(2)}, u32[]{:S(2)}) collective-permute-start(bf16[528,128]{1,0:T(8,128)(2,1)S(1)} %shard_map.183), channel_id=1, source_target_pairs={{8,0},{12,4},{16,8},{20,12},{24,16},{28,20},{9,1},{13,5},{17,9},{2... | collective-permute-start | bytes 405512 | tf_op jit(solution)/shard_map/ppermute | solution.py:482
  105.7 12.2 %collective-permute-start.7 = (bf16[528,128]{1,0:T(8,128)(2,1)S(1)}, bf16[528,128]{1,0:T(8,128)(2,1)S(1)}, u32[]{:S(2)}, u32[]{:S(2)}) collective-permute-start(bf16[528,128]{1,0:T(8,128)(2,1)S(1)} %shard_map.183), channel_id=1, source_target_pairs={{16,0},{20,4},{24,8},{28,12},{17,1},{21,5},{25,9},{29,13},{18,2},{... | collective-permute-start | bytes 405512 | tf_op jit(solution)/shard_map/ppermute | solution.py:482
  110.3 29.0 %collective-permute-start.8 = (bf16[528,128]{1,0:T(8,128)(2,1)S(1)}, bf16[528,128]{1,0:T(8,128)(2,1)S(1)}, u32[]{:S(2)}, u32[]{:S(2)}) collective-permute-start(bf16[528,128]{1,0:T(8,128)(2,1)S(1)} %shard_map.183), channel_id=1, source_target_pairs={{24,0},{28,4},{25,1},{29,5},{26,2},{30,6},{27,3},{31,7}} | collective-permute-start | bytes 405512 | tf_op jit(solution)/shard_map/ppermute | solution.py:482
  112.9 28.5 %collective-permute-start.21 = (bf16[256,256]{1,0:T(8,128)(2,1)S(1)}, bf16[256,256]{1,0:T(8,128)(2,1)S(1)}, u32[]{:S(2)}, u32[]{:S(2)}) collective-permute-start(bf16[256,256]{1,0:T(8,128)(2,1)S(1)} %slice.40), channel_id=1, source_target_pairs={{0,4},{4,0},{8,12},{12,8},{16,20},{20,16},{24,28},{28,24},{1,5},{5... | collective-permute-start | bytes 393224 | tf_op jit(solution)/shard_map/ppermute | solution.py:476
  140.0 5.0 %collective-permute-start.9 = (bf16[512,128]{1,0:T(8,128)(2,1)S(1)}, bf16[512,128]{1,0:T(8,128)(2,1)S(1)}, u32[]{:S(2)}, u32[]{:S(2)}) collective-permute-start(bf16[512,128]{1,0:T(8,128)(2,1)S(1)} %get-tuple-element.58), channel_id=1, source_target_pairs={{0,4},{4,0},{8,12},{12,8},{16,20},{20,16},{24,28},{28,24},{1,5},{5... | collective-permute-start | bytes 393224 | tf_op jit(solution)/shard_map/ppermute | solution.py:476
  (39 other events, 116.9 us)

commit v2 on v1

v2 whole, which is shorter than its diff:
```python
import functools

import jax
import jax.numpy as jnp
from jax import lax
from jax.experimental import pallas as pl
from jax.experimental.pallas import tpu as pltpu
from jax.sharding import PartitionSpec as P

DH = 128
LOG2E = 1.4426950408889634
LN2 = 0.6931471805599453
negative_fill = -1e30
f32 = jnp.float32
bf16 = jnp.bfloat16
VMEM_BYTES = 24 * 1024 * 1024
FORWARD_CHUNK = 128
FLOPS_PER_MICRO = 1150 * 10**6
BACKWARD_CHUNK = 256

SMEM_SPEC = pl.BlockSpec(memory_space=pltpu.SMEM)
VMEM_SPEC = pl.BlockSpec(memory_space=pltpu.VMEM)
ANY_SPEC = pl.BlockSpec(memory_space=pl.ANY)


def nn(a, b):
    return jnp.dot(a, b, preferred_element_type=f32)


def nt(a, b):
    return lax.dot_general(a, b, (((1,), (1,)), ((), ())), preferred_element_type=f32)


def tn(a, b):
    return lax.dot_general(a, b, (((0,), (0,)), ((), ())), preferred_element_type=f32)


def whole_call(kernel, place, arrays, outs, micros, after=(), aliases={}, scratch=()):
    def ordered(place, *refs):
        kernel(place, *refs[: len(arrays)], *refs[len(arrays) + len(after) :])

    return pl.pallas_call(
        ordered,
        out_shape=outs,
        in_specs=[SMEM_SPEC] + [VMEM_SPEC] * len(arrays) + [ANY_SPEC] * len(after),
        out_specs=[VMEM_SPEC] * len(outs),
        scratch_shapes=list(scratch),
        input_output_aliases={i + 1: o for i, o in aliases.items()},
        compiler_params=pltpu.CompilerParams(vmem_limit_bytes=VMEM_BYTES),
        cost_estimate=pl.CostEstimate(
            flops=int(micros * FLOPS_PER_MICRO), bytes_accessed=1, transcendentals=0
        ),
    )(place, *arrays, *after)


def split3(x):
    hi = x.astype(bf16)
    rest = x - hi.astype(f32)
    lo = rest.astype(bf16)
    return hi, lo, (rest - lo.astype(f32)).astype(bf16)


def extra_rows(heads):
    return 16 * pl.cdiv(3 * heads, 16)


def pack_logs(rows):
    heads = rows.shape[0]
    pad = extra_rows(heads) - 3 * heads
    parts = [p.astype(f32) for p in split3(rows)]
    if pad:
        parts.append(jnp.zeros((pad, DH), f32))
    return jnp.concatenate(parts, axis=0).astype(bf16)


def read_logs(ref, heads):
    part = ref[heads * DH :, :].astype(f32)
    return part[:heads] + part[heads : 2 * heads] + part[2 * heads : 3 * heads]


def head_rows(h):
    return slice(h * DH, (h + 1) * DH)


def lin_state_kernel(heads, fold, place, log_ref, key_ref, value_ref, msg_ref, row_ref, col_ref):
    rows = key_ref.shape[0]
    y = place[0]
    later = lax.broadcasted_iota(jnp.int32, (rows, rows), 0)
    earlier = lax.broadcasted_iota(jnp.int32, (rows, rows), 1)
    tri = (earlier <= later).astype(f32)
    logs = log_ref[...]
    exact = lax.Precision.HIGHEST
    dims = (((1,), (1,)), ((), ()))
    by_row = lax.dot_general(logs, tri, dims, precision=exact, preferred_element_type=f32)
    by_col = lax.dot_general(tri, logs, dims, precision=exact, preferred_element_type=f32)
    row_ref[...] = by_row
    col_ref[...] = by_col
    totals = by_row[:, rows - 1 : rows]
    tail = jnp.exp(totals - by_row)
    group = heads // fold
    for g in range(fold):
        slot = lax.rem(g + y, fold) if fold > 1 else 0
        for i in range(group):
            h = g * group + i
            key_t = key_ref[:, head_rows(h)].astype(f32).T * tail[h : h + 1, :]
            state = nn(key_t.astype(bf16), value_ref[:, head_rows(h)])
            msg_ref[slot, head_rows(i), :] = state.astype(bf16)
        wide = jnp.broadcast_to(totals[g * group : (g + 1) * group], (group, DH))
        msg_ref[slot, group * DH :, :] = pack_logs(wide)


def lin_pair_kernel(heads, backward, place, own_ref, rec_ref, out_ref):
    y = place[0]
    own_logs, rec_logs = read_logs(own_ref, heads), read_logs(rec_ref, heads)
    out_ref[heads * DH :, :] = pack_logs(own_logs + rec_logs)
    own_far = (y == 1) if backward else (y == 0)
    near_scale = jnp.exp(jnp.where(own_far, rec_logs, own_logs))
    own_scale = jnp.where(own_far, near_scale, 1.0)
    rec_scale = jnp.where(own_far, 1.0, near_scale)
    for i in range(heads):
        own, rec = own_ref[head_rows(i), :].astype(f32), rec_ref[head_rows(i), :].astype(f32)
        joint = own * own_scale[i : i + 1] + rec * rec_scale[i : i + 1]
        out_ref[head_rows(i), :] = joint.astype(bf16)


def lin_combine_kernel(heads, place, own_ref, rec_ref, out_ref):
    own_logs = read_logs(own_ref, heads)
    out_ref[heads * DH :, :] = pack_logs(own_logs + read_logs(rec_ref, heads))
    scale = jnp.exp(own_logs)
    for i in range(heads):
        own, rec = own_ref[head_rows(i), :].astype(f32), rec_ref[head_rows(i), :].astype(f32)
        out_ref[head_rows(i), :] = (own + rec * scale[i : i + 1]).astype(bf16)


def lin_scan_kernel(heads, fold, count, backward, place, own_ref, rec_ref, *rest):
    far, outs = rest[:count], rest[count:]
    y = place[0]
    if fold > 1:
        own_logs, rec_logs = read_logs(own_ref, heads), read_logs(rec_ref, heads)
        own_near = (y == 1) if backward else (y == 0)
        near_scale = jnp.exp(jnp.where(own_near, own_logs, rec_logs))
    far_scales = []
    passed = jnp.zeros((heads, DH), f32)
    for s in range(count):
        far_scales.append(jnp.exp(passed))
        passed = passed + read_logs(far[s], heads)
    for i in range(heads):
        total = jnp.zeros((DH, DH), f32)
        for s in range(count):
            total = total + far_scales[s][i : i + 1] * far[s][head_rows(i), :].astype(f32)
        if fold == 1:
            outs[0][head_rows(i), :] = total.astype(bf16)
            continue
        own, rec = own_ref[head_rows(i), :].astype(f32), rec_ref[head_rows(i), :].astype(f32)
        beyond = jnp.where(own_near, own, rec) + near_scale[i : i + 1] * total
        outs[0][head_rows(i), :] = jnp.where(own_near, total, beyond).astype(bf16)
        outs[1][head_rows(i), :] = jnp.where(own_near, beyond, total).astype(bf16)


def pick_state(refs, h, group, y):
    i = h % group
    if len(refs) == 1:
        return refs[0][head_rows(i), :]
    own, rec = refs[0][head_rows(i), :].astype(f32), refs[1][head_rows(i), :].astype(f32)
    return jnp.where(y == h // group, own, rec).astype(bf16)


def lin_attend_kernel(
    heads, fold, place, row_ref, col_ref, query_ref, key_ref, value_ref, gate_ref, grad_ref, gain_ref, *rest
):
    states, (att_ref, stat_ref) = rest[:fold], rest[fold:]
    rows = query_ref.shape[0]
    y = place[0]
    causal = lax.broadcasted_iota(jnp.int32, (rows, rows), 0) >= lax.broadcasted_iota(
        jnp.int32, (rows, rows), 1
    )
    squares = jnp.zeros((rows, DH), f32)
    crosses = jnp.zeros((rows, DH), f32)
    for h in range(heads):
        query, key, value = (r[:, head_rows(h)] for r in (query_ref, key_ref, value_ref))
        col = col_ref[:, h : h + 1]
        decay = jnp.exp(jnp.where(causal, col - row_ref[h : h + 1, :], negative_fill))
        weights = (nt(query, key) * decay).astype(bf16)
        state = pick_state(states, h, heads // fold, y)
        att = nn(weights, value) + jnp.exp(col) * nn(query, state)
        att_ref[:, head_rows(h)] = att
        sig = jax.nn.sigmoid(gate_ref[:, head_rows(h)].astype(f32))
        scaled = grad_ref[:, head_rows(h)].astype(f32) * gain_ref[:, head_rows(h)] * sig
        squares = squares + att * att
        crosses = crosses + scaled * att
    stat_ref[...] = jnp.concatenate(
        (
            jnp.sum(squares.T, axis=0, keepdims=True),
            jnp.sum(crosses.T, axis=0, keepdims=True),
            jnp.zeros((6, rows), f32),
        ),
        axis=0,
    )


def lin_norm_kernel(
    heads, fold, width, place, row_ref, att_ref, gate_ref, grad_ref, gain_ref, query_ref, own_ref, oth_ref, *rest
):
    *stat_refs, out_ref, gate_grad_ref, att_grad_ref, msg_ref = rest
    y = place[0]
    rows = query_ref.shape[0]
    stats = sum((r[...] for r in stat_refs[1:]), stat_refs[0][...])
    stats = jnp.concatenate((stats, jnp.zeros((DH - 8, rows), f32)), axis=0).T
    scaling = lax.rsqrt(stats[:, 0:1] / width + 1e-05)
    cross = scaling * stats[:, 1:2] / width
    group = heads // fold
    lead = jnp.exp(row_ref[...])
    for g in range(fold):
        slot = lax.rem(g + y, fold) if fold > 1 else 0
        for i in range(group):
            h = g * group + i
            gain = gain_ref[:, head_rows(h)]
            sig = jax.nn.sigmoid(gate_ref[:, head_rows(h)].astype(f32))
            normed = att_ref[:, head_rows(h)] * scaling
            scaled = grad_ref[:, head_rows(h)].astype(f32) * gain * sig
            out_ref[:, head_rows(h)] = (normed * gain * sig).astype(bf16)
            gate_grad_ref[:, head_rows(h)] = (scaled * normed * (1.0 - sig)).astype(bf16)
            att_grad = (scaling * (scaled - normed * cross)).astype(bf16)
            att_grad_ref[:, head_rows(h)] = att_grad
            query_t = query_ref[:, head_rows(h)].astype(f32).T * lead[h : h + 1, :]
            msg_ref[slot, head_rows(i), :] = nn(query_t.astype(bf16), att_grad).astype(bf16)
    msg_ref[0, group * DH :, :] = own_ref[group * DH :, :]
    if fold > 1:
        msg_ref[1, group * DH :, :] = oth_ref[group * DH :, :]


def lin_local_kernel(heads, fold, place, row_ref, col_ref, query_ref, key_ref, value_ref, att_grad_ref, *rest):
    states, (query_grad_ref, key_part_ref, value_part_ref) = rest[:fold], rest[fold:]
    y = place[0]
    rows = query_ref.shape[0]
    first = lax.broadcasted_iota(jnp.int32, (rows, rows), 0)
    second = lax.broadcasted_iota(jnp.int32, (rows, rows), 1)
    causal, causal_t = first >= second, first <= second
    for h in range(heads):
        query, key, value, grad = (
            r[:, head_rows(h)] for r in (query_ref, key_ref, value_ref, att_grad_ref)
        )
        col, row = col_ref[:, h : h + 1], row_ref[h : h + 1, :]
        decay = jnp.exp(jnp.where(causal, col - row, negative_fill))
        decay_t = jnp.exp(jnp.where(causal_t, row - col, negative_fill))
        state = pick_state(states, h, heads // fold, y)
        grad_weights = (nt(grad, value) * decay).astype(bf16)
        grad_weights_t = (nt(value, grad) * decay_t).astype(bf16)
        weights_t = (nt(key, query) * decay_t).astype(bf16)
        query_grad = nn(grad_weights, key) + jnp.exp(col) * nt(grad, state)
        query_grad_ref[:, head_rows(h)] = query_grad.astype(bf16)
        key_part_ref[:, head_rows(h)] = nn(grad_weights_t, query)
        value_part_ref[:, head_rows(h)] = nn(weights_t, grad)


def final_kernel(heads, fold, place, row_ref, col_ref, key_ref, value_ref, key_part_ref, value_part_ref, *rest):
    states, rest = rest[:fold], rest[fold:]
    halves, outs = rest[:-6], rest[-6:]
    y = place[0]
    rows = key_ref.shape[0]
    for h in range(heads):
        key, value = key_ref[:, head_rows(h)], value_ref[:, head_rows(h)]
        tail = jnp.exp(row_ref[h : h + 1, rows - 1 : rows] - col_ref[:, h : h + 1])
        state = pick_state(states, h, heads // fold, y)
        key_grad = key_part_ref[:, head_rows(h)] + tail * nt(value, state)
        value_grad = value_part_ref[:, head_rows(h)] + tail * nn(key, state)
        outs[0][:, head_rows(h)] = key_grad.astype(bf16)
        outs[1][:, head_rows(h)] = value_grad.astype(bf16)
    count = len(halves) // 3
    for i in range(fold):
        at = (y + i) % fold
        for out, part in ((outs[2], halves[i]), (outs[3], halves[count + i])):
            size = part.shape[1]
            out[:, pl.ds(pl.multiple_of(at * size, DH), size)] = part[...]
        part = halves[2 * count + i]
        for j in range(2):
            there = pl.ds(pl.multiple_of(at * DH, DH), DH)
            outs[4 + j][:, there] = part[:rows, j * DH : (j + 1) * DH]


def diagonal_mask(y, keys, first, count, tokens, rows):
    key_at = lax.rem(lax.broadcasted_iota(jnp.int32, (keys, count), 0) + y * tokens, rows)
    query_at = lax.rem(lax.broadcasted_iota(jnp.int32, (keys, count), 1) + first + y * tokens, rows)
    return key_at <= query_at


def soft_pack_kernel(place, rows_ref, out_ref):
    half = rows_ref.shape[1] // 2
    out_ref[...] = rows_ref[:, pl.ds(pl.multiple_of((1 - place[0]) * half, DH), half)]


def head_of_rows(y, group, h, own_ref, rec_ref):
    if rec_ref is None:
        return own_ref[:, head_rows(h)]
    own = own_ref[:, pl.ds(pl.multiple_of((y * group + h) * DH, DH), DH)]
    return jnp.concatenate((own, rec_ref[:, head_rows(h)]), axis=0)


def soft_forward_kernel(fold, tokens, group, diagonal, last, place, *refs):
    refs = list(refs)
    take = lambda count: [refs.pop(0) for _ in range(count)]
    query_ref = take(1)[0]
    kv_refs = take(fold)
    grad_ref = take(1)[0] if last else None
    query_rec = take(1)[0] if fold > 1 else None
    grad_rec = take(1)[0] if fold > 1 and last else None
    old_peak, old_total, old_acc = take(3) if not diagonal else (None,) * 3
    outs = take(fold + 2 if last else 3)
    peak, total, acc = refs if last else outs
    y = place[0]
    rows = tokens * fold

    def compute():
        kv = jnp.concatenate([r[...] for r in kv_refs], axis=0)
        key, value = kv[:, :DH], kv[:, DH:]
        step = min(FORWARD_CHUNK, rows)
        for h in range(group):
            query = head_of_rows(y, group, h, query_ref, query_rec)
            for at in range(0, rows, step):
                span = slice(at, at + step)
                scores = nt(key, query[span]) * (LOG2E * DH**-0.5)
                if diagonal:
                    mask = diagonal_mask(y, rows, at, step, tokens, rows)
                    scores = jnp.where(mask, scores, negative_fill)
                    fresh = jnp.max(scores, axis=0, keepdims=True)
                    probs = jnp.exp2(scores - fresh)
                    total[h, :, span] = jnp.sum(probs, axis=0, keepdims=True)
                    acc[h, :, span] = tn(value, probs.astype(bf16))
                else:
                    old = old_peak[h, :, span]
                    fresh = jnp.maximum(old, jnp.max(scores, axis=0, keepdims=True))
                    probs = jnp.exp2(scores - fresh)
                    fade = jnp.exp2(old - fresh)
                    total[h, :, span] = old_total[h, :, span] * fade + jnp.sum(
                        probs, axis=0, keepdims=True
                    )
                    acc[h, :, span] = old_acc[h, :, span] * fade + tn(value, probs.astype(bf16))
                peak[h, :, span] = fresh

    if diagonal:
        compute()
    else:
        reached = place[1] >= place[2]
        pl.when(reached)(compute)
        if last:

            @pl.when(jnp.logical_not(reached))
            def _():
                peak[...], total[...], acc[...] = old_peak[...], old_total[...], old_acc[...]

    if last:
        for h in range(group):
            out_t = (acc[h] / total[h]).astype(bf16).astype(f32)
            out = out_t.T.astype(bf16)
            for i in range(fold):
                outs[i][:, head_rows(h)] = out[i * tokens : (i + 1) * tokens]
            grad_t = head_of_rows(y, group, h, grad_ref, grad_rec).astype(f32).T
            outs[fold][h] = peak[h] + jnp.log(total[h]) * LOG2E
            outs[fold + 1][h] = jnp.sum(grad_t * out_t, axis=0, keepdims=True)


def soft_forward(place, query, grad, rec, kv, carry, last, after=()):
    tokens, fold = query.shape[0], len(kv)
    rows, group = tokens * fold, query.shape[1] // DH // fold
    diagonal = carry is None
    lines = jax.ShapeDtypeStruct((group, 1, rows), f32)
    talls = jax.ShapeDtypeStruct((group, DH, rows), f32)
    own = (query, *kv, grad) if last else (query, *kv)
    arrays = (*own, *(rec if last else rec[:1]), *(() if diagonal else carry))
    aliases, scratch = {}, ()
    if last:
        outs = [jax.ShapeDtypeStruct((tokens, group * DH), bf16)] * fold + [lines, lines]
        scratch = [pltpu.VMEM(a.shape, f32) for a in (lines, lines, talls)]
    else:
        outs = [lines, lines, talls]
        if not diagonal:
            aliases = {len(arrays) - 3 + i: i for i in range(3)}
    kernel = functools.partial(soft_forward_kernel, fold, tokens, group, diagonal, last)
    return whole_call(kernel, place, arrays, outs, 3.0 if last else 2.6, after, aliases, scratch)


def soft_backward_kernel(fold, tokens, group, diagonal, first, place, *refs):
    refs = list(refs)
    take = lambda count: [refs.pop(0) for _ in range(count)]
    query_ref, grad_ref, log_ref, delta_ref = take(4)
    kv_refs = take(fold)
    query_rec, grad_rec = take(2) if fold > 1 else (None, None)
    old_acc = take(1)[0] if not first else None
    kv_grad_ref, *outs = refs
    y = place[0]
    rows = tokens * fold

    def compute():
        kv = jnp.concatenate([r[...] for r in kv_refs], axis=0)
        key, value = kv[:, :DH], kv[:, DH:]
        step = min(BACKWARD_CHUNK, rows)
        key_acc, value_acc = jnp.zeros((rows, DH), f32), jnp.zeros((rows, DH), f32)
        for h in range(group):
            query = head_of_rows(y, group, h, query_ref, query_rec)
            grad = head_of_rows(y, group, h, grad_ref, grad_rec)
            for at in range(0, rows, step):
                span = slice(at, at + step)
                scores = nt(key, query[span]) * (LOG2E * DH**-0.5) - log_ref[h, :, span]
                if diagonal:
                    mask = diagonal_mask(y, rows, at, step, tokens, rows)
                    scores = jnp.where(mask, scores, negative_fill)
                probs = jnp.exp2(scores)
                score_grad = (probs * (nt(value, grad[span]) - delta_ref[h, :, span])).astype(bf16)
                value_acc += nn(probs.astype(bf16), grad[span])
                key_acc += nn(score_grad, query[span])
                query_grad = tn(key, score_grad)
                if not first:
                    query_grad += old_acc[h, :, span]
                if diagonal:
                    query_grad = (query_grad * DH**-0.5).T.astype(bf16)
                    i, begin = at // tokens, at % tokens
                    outs[i][begin : begin + step, head_rows(h)] = query_grad
                else:
                    outs[0][h, :, span] = query_grad
        kv_grad_ref[:, :DH] = key_acc * DH**-0.5
        kv_grad_ref[:, DH:] = value_acc

    if diagonal:
        compute()
        return
    reached = place[1] >= place[2]
    pl.when(reached)(compute)

    @pl.when(jnp.logical_not(reached))
    def _():
        kv_grad_ref[...] = jnp.zeros_like(kv_grad_ref)
        if first:
            outs[0][...] = jnp.zeros_like(outs[0])


def soft_backward(place, query, grad, rec, logs, deltas, kv, carry, diagonal, after=()):
    tokens, fold = query.shape[0], len(kv)
    rows, group = tokens * fold, query.shape[1] // DH // fold
    first = carry is None
    arrays = (query, grad, logs, deltas, *kv, *rec, *(() if first else (carry,)))
    outs = [jax.ShapeDtypeStruct((rows, 2 * DH), f32)]
    aliases = {}
    if diagonal:
        outs += [jax.ShapeDtypeStruct((tokens, group * DH), bf16)] * fold
    else:
        outs += [jax.ShapeDtypeStruct((group, DH, rows), f32)]
        if not first:
            aliases = {len(arrays) - 1: 1}
    kernel = functools.partial(soft_backward_kernel, fold, tokens, group, diagonal, first)
    return whole_call(kernel, place, arrays, outs, 3.4, after, aliases)


def body(
    lin_query,
    lin_key,
    lin_value,
    log_decay,
    norm_gain,
    lin_gate,
    lin_grad,
    soft_query,
    soft_key,
    soft_value,
    soft_grad,
):
    count = lax.axis_size("ctx")
    kv_heads = soft_key.shape[1] // DH
    fold = 2 if kv_heads == 2 and count % 2 == 0 else 1
    laps = count // fold
    index = lax.axis_index("ctx")
    y, z = lax.rem(index, fold), lax.div(index, fold)
    place = jnp.stack((y, z)).astype(jnp.int32)
    tokens = soft_query.shape[0]
    rows = tokens * fold
    heads = lin_query.shape[1] // DH
    group = heads // fold
    width = lin_query.shape[1] * lax.axis_size("tp")
    gain = norm_gain[None, :]

    def swap(a):
        return lax.ppermute(a, "ctx", [(i, i ^ 1) for i in range(count)])

    def up(a, s):
        return lax.ppermute(a, "ctx", [(i, i + fold * s) for i in range(count - fold * s)])

    def down(a, s):
        return lax.ppermute(a, "ctx", [(i + fold * s, i) for i in range(count - fold * s)])

    def own_columns(a):
        size = a.shape[1] // 2
        return a if fold == 1 else jnp.where(y == 0, a[:, :size], a[:, size:])

    def partner_columns(a):
        size = a.shape[1] // 2
        return jnp.where(y == 0, a[:, size:], a[:, :size])

    def each(move, parts, s):
        return [move(a, s) for a in parts]

    def at_lap(s):
        return jnp.concatenate((place, jnp.asarray(s, jnp.int32)[None]))

    early = ()
    kv = [jnp.concatenate((own_columns(soft_key), own_columns(soft_value)), axis=1)]
    if fold > 1:
        kv_sent = jnp.concatenate((partner_columns(soft_key), partner_columns(soft_value)), axis=1)
        kv.append(swap(kv_sent))
        early = (kv_sent, kv[0])

    msg_rows = group * DH + extra_rows(group)
    msg = jax.ShapeDtypeStruct((msg_rows, DH), bf16)
    msgs = jax.ShapeDtypeStruct((fold, msg_rows, DH), bf16)
    state = jax.ShapeDtypeStruct((group * DH, DH), bf16)
    flat = jax.ShapeDtypeStruct((tokens, heads * DH), bf16)
    state_msgs, log_rows, log_cols = whole_call(
        functools.partial(lin_state_kernel, heads, fold),
        place,
        (log_decay, lin_key, lin_value),
        [
            msgs,
            jax.ShapeDtypeStruct((heads, tokens), f32),
            jax.ShapeDtypeStruct((tokens, heads), f32),
        ],
        1.4,
        early,
    )
    own_msg, oth_msg = state_msgs[0], state_msgs[fold - 1]
    rec = ()
    if fold > 1:
        half = jax.ShapeDtypeStruct((tokens, group * DH), bf16)
        (sent,) = whole_call(soft_pack_kernel, place, (soft_query,), [half], 0.6, (state_msgs,))
        rec = (swap(sent),)
    unrolled = laps <= 8
    if unrolled:
        kvs = [kv]
        for s in range(1, laps):
            kvs.append(each(up, kvs[-1], 1))

    def pair_states(own, other, backward, after=()):
        if fold == 1:
            return own, (own, own)
        rec = swap(other)
        kernel = functools.partial(lin_pair_kernel, group, backward)
        return whole_call(kernel, place, (own, rec), [msg], 0.6, after)[0], (own, rec)

    def send_states(joint, backward, after=()):
        got, step, move = [], 1, down if backward else up
        while step < laps:
            got.append(move(joint, step))
            step *= 2
            if step < laps:
                kernel = functools.partial(lin_combine_kernel, group)
                (joint,) = whole_call(kernel, place, (joint, got[-1]), [msg], 0.6, after)
        return joint, got

    def take_states(sent, backward, after=()):
        got = whole_call(
            functools.partial(lin_scan_kernel, group, fold, len(sent) - 2, backward),
            place,
            sent,
            [state] * fold,
            0.7,
            after=after,
        )
        return got[0], ((got[0], swap(got[1])) if fold > 1 else tuple(got))

    def forward(kv, s, carry, last, after=()):
        return soft_forward(at_lap(s), soft_query, soft_grad, rec, kv, carry, last, after)

    def backward(kv, s, carry, after=()):
        whole = (soft_query, soft_grad, rec, logs, deltas, kv, carry)
        return soft_backward(at_lap(s), *whole, isinstance(s, int) and s == 0, after)

    joint, pair = pair_states(own_msg, oth_msg, False)
    soft = forward(kv, 0, None, False)
    if fold > 1:
        (grad_sent,) = whole_call(soft_pack_kernel, place, (soft_grad,), [half], 0.6, (joint,))
        rec += (swap(grad_sent),)
    joint, far = send_states(joint, False)
    if unrolled:
        for s in range(1, laps - 1):
            soft = forward(kvs[s], s, soft, False)
        last_kv = kvs[-1]
    else:

        def far_forward(state, s):
            kv, soft = state
            kv = each(up, kv, 1)
            return (kv, forward(kv, s, soft, False)), kv

        (last_kv, soft), far_kvs = lax.scan(far_forward, (kv, soft), jnp.arange(1, laps - 1))
        last_kv = each(up, last_kv, 1)
    soft = forward(last_kv, laps - 1, soft, True)
    outs, (logs, deltas) = soft[:fold], soft[fold:]
    kept, carried = take_states((*pair, *far), False, (logs,))

    def added(kv_grad, hop):
        return (kv_grad + hop.astype(f32)).astype(bf16)

    kv_grad, carry = backward(last_kv, laps - 1, None)
    hop = down(kv_grad.astype(bf16), 1)

    attended, stats = whole_call(
        functools.partial(lin_attend_kernel, heads, fold),
        place,
        (log_rows, log_cols, lin_query, lin_key, lin_value, lin_gate, lin_grad, gain, *carried),
        [
            jax.ShapeDtypeStruct((tokens, heads * DH), f32),
            jax.ShapeDtypeStruct((8, tokens), f32),
        ],
        2.0,
    )
    tp = lax.axis_size("tp")
    if tp <= 4 and tp & (tp - 1) == 0:
        all_stats = [stats] + [
            lax.ppermute(stats, "tp", [(i, i ^ k) for i in range(tp)]) for k in range(1, tp)
        ]
    else:
        all_stats = [lax.psum(stats, "tp")]

    def norm(after):
        return whole_call(
            functools.partial(lin_norm_kernel, heads, fold, width),
            place,
            (log_rows, attended, lin_gate, lin_grad, gain, lin_query, own_msg, oth_msg, *all_stats),
            [flat, flat, flat, msgs],
            2.5,
            after,
        )

    if unrolled:
        after = ()
        for s in range(laps - 2, 0, -1):
            kv_grad, carry = backward(kvs[s], s, carry, after)
            if s == laps - 2:
                lin_out, lin_gate_grad, att_grad, back_msgs = norm(())
            moved = added(kv_grad, hop)
            hop = down(moved, 1)
            after = (moved,)
    else:

        def far_backward(state, given):
            hop, carry = state
            s, kv = given
            kv_grad, carry = backward(kv, s, carry)
            return (down(added(kv_grad, hop), 1), carry), None

        given = (jnp.arange(1, laps - 1), far_kvs)
        (hop, carry), _ = lax.scan(far_backward, (hop, carry), given, reverse=True)
        lin_out, lin_gate_grad, att_grad, back_msgs = norm((carry,))
        after = ()
    joint, pair = pair_states(back_msgs[0], back_msgs[fold - 1], True)
    kv_grad, *query_grads = backward(kv, 0, carry, after)
    joint, far = send_states(joint, True)
    kept, returned = take_states((*pair, *far), True)
    total = added(kv_grad, hop)
    part = jax.ShapeDtypeStruct((tokens, heads * DH), f32)
    lin_query_grad, key_part, value_part = whole_call(
        functools.partial(lin_local_kernel, heads, fold),
        place,
        (log_rows, log_cols, lin_query, lin_key, lin_value, att_grad, *carried),
        [flat, part, part],
        3.4,
    )
    outs, kv_grads = list(outs), [total]
    if fold > 1:
        outs[1], query_grads[1] = swap(outs[1]), swap(query_grads[1])
        kv_grads.append(swap(total[tokens:]))
    thin = jax.ShapeDtypeStruct(soft_key.shape, bf16)
    lin_key_grad, lin_value_grad, soft_out, soft_query_grad, soft_key_grad, soft_value_grad = whole_call(
        functools.partial(final_kernel, heads, fold),
        place,
        (
            *(log_rows, log_cols, lin_key, lin_value, key_part, value_part),
            *(*returned, *outs, *query_grads, *kv_grads),
        ),
        [flat, flat, flat, flat, thin, thin],
        2.0,
    )
    return (
        lin_out,
        lin_query_grad,
        lin_key_grad,
        lin_value_grad,
        lin_gate_grad,
        soft_out,
        soft_query_grad,
        soft_key_grad,
        soft_value_grad,
    )


def solution(mesh):
    spread = P("ctx", "tp")
    return jax.shard_map(
        body,
        mesh=mesh,
        in_specs=(spread, spread, spread, P("tp", "ctx"), P("tp")) + (spread,) * 6,
        out_specs=(spread,) * 9,
        check_vma=False,
    )
```

time: 150 us -> 96.3 us (0.64)
  waiting for transfers between devices: 43.2 us -> 20.9 us
  local copies, waits for them, and re-layouts: 11.9 us -> 0.52 us
  blocking collectives: 7.02 us -> 0 us
  starting transfers between devices: 49.4 us -> 44 us
  Pallas kernels: 31.8 us -> 27.4 us
  other arithmetic: 4.55 us -> 1.53 us
    ppermute x6 -> x5, waiting for transfers between devices: 24.7 us -> 12.4 us  [down(): lax.ppermute(a, 'ctx', [(i + fold * s, i) for i in range(count - fold * s)])]
    unnamed x82 -> x18, local copies, waits for them, and re-layouts: 10.2 us -> 0.47 us
    ppermute x6 -> x8, starting transfers between devices: 30.1 us -> 22.3 us  [up(): lax.ppermute(a, 'ctx', [(i, i + fold * s) for i in range(count - fold * s)])]
    psum x1 -> x0, blocking collectives: 7.02 us -> none  [body(): stats = lax.psum(stats, 'tp')]
    ppermute x6 -> x8, waiting for transfers between devices: 8.91 us -> 1.93 us  [up(): lax.ppermute(a, 'ctx', [(i, i + fold * s) for i in range(count - fold * s)])]
    pallas_call x16 -> x21, Pallas kernels: 31.8 us -> 27.4 us  [whole_call(): pl.pallas_call(ordered, out_shape=outs, in_specs=[SMEM_SPEC] + [VMEM_SPEC...]
    ppermute x10, waiting for transfers between devices: 9.61 us -> 5.25 us  [swap(): return lax.ppermute(a, 'ctx', [(i, i ^ 1) for i in range(count)])]
    concatenate x5 -> x4, other arithmetic: 3.06 us -> 0.19 us  [the longest x2 0.15 us: at_lap(): return jnp.concatenate((place, jnp.asarray(s, jnp.int32)[None]))]
  transfers between devices with their start and end apart: 22 -> 26, of which waited for: 6 -> 8; matrix products, arithmetic and copies ran while one was open for 4% -> 1% of each run, Pallas kernels for 19% -> 25%
where the time goes in v2:
time: 96.3 us; the launch traced here: 95.5 us
  starting transfers between devices  44 us (46%)
  Pallas kernels  27.4 us (28%)
  waiting for transfers between devices  20.9 us (22%)
  other arithmetic  1.53 us (2%)
  between operations  1.09 us (1%)
    pallas_call x21, Pallas kernels, whole_call(): pl.pallas_call(ordered, out_shape=outs, in_specs=[SMEM_SPEC] + [VMEM_SPEC...  27.4 us
    ppermute x8, starting transfers between devices, up(): lax.ppermute(a, 'ctx', [(i, i + fold * s) for i in range(count - fold * s)])  22.3 us
    ppermute x10, starting transfers between devices, swap(): return lax.ppermute(a, 'ctx', [(i, i ^ 1) for i in range(count)])  13 us
    ppermute x5, waiting for transfers between devices, down(): lax.ppermute(a, 'ctx', [(i + fold * s, i) for i in range(count - fold * s)])  12.4 us
    ppermute x5, starting transfers between devices, down(): lax.ppermute(a, 'ctx', [(i + fold * s, i) for i in range(count - fold * s)])  6.81 us
    ppermute x10, waiting for transfers between devices, swap(): return lax.ppermute(a, 'ctx', [(i, i ^ 1) for i in range(count)])  5.25 us
    ppermute x8, waiting for transfers between devices, up(): lax.ppermute(a, 'ctx', [(i, i + fold * s) for i in range(count - fold * s)])  1.93 us
  transfers between devices with their start and end apart: 26, of which 8 were waited for; matrix products, arithmetic and copies ran while one was open for 1% of the time, Pallas kernels for 25%

profile of v2, /device:TPU:0, one launch (start us, length us, event | category | flops | bytes accessed | tf_op | source)
XLA Modules:
  0.0 95.5 jit_solution(2244736378359465514)
XLA Ops:
  1.7 3.0 %collective-permute-start.6 = (bf16[256,256]{1,0:T(8,128)(2,1)S(1)}, bf16[256,256]{1,0:T(8,128)(2,1)S(1)}, u32[]{:S(2)}, u32[]{:S(2)}) collective-permute-start(bf16[256,256]{1,0:T(8,128)(2,1)S(1)} %pad_maximum_fusion.refs_3_), channel_id=1, source_target_pairs={{0,4},{4,0},{8,12},{12,8},{16,20},{20,16},{24,28},{28,24},{1,5},{5... | collective-permute-start | bytes 393224 | tf_op jit(solution)/shard_map/ppermute | solution.py:481
  4.8 3.5 %collective-permute-start.3 = (bf16[256,256]{1,0:T(8,128)(2,1)S(1)}, bf16[256,256]{1,0:T(8,128)(2,1)S(1)}, u32[]{:S(2)}, u32[]{:S(2)}) collective-permute-start(bf16[256,256]{1,0:T(8,128)(2,1)S(1)} %pad_maximum_fusion.1.refs_4_.refs_1_), channel_id=1, source_target_pairs={{0,8},{4,12},{8,16},{12,20},{16,24},{20,28},{1,9},{5,13},{9,17},{1... | collective-permute-start | bytes 393224 | tf_op jit(solution)/shard_map/ppermute | solution.py:484
  8.4 1.4 %shard_map.178 = (bf16[2,528,128]{2,1,0:T(8,128)(2,1)S(1)}, f32[8,256]{1,0:T(8,128)S(1)}, f32[256,8]{1,0:T(8,128)S(1)}) custom-call(s32[2]{0:T(128)S(1)} %pad_add_fusion.place, f32[8,256]{1,0:T(8,128)S(1)} %copy-done.7, bf16[256,1024]{1,0:T(8,128)(2,1)S(1)} %copy-done.5, bf16[256,1024]{1,0:T(8,128)(2,1)S(1)} %copy-done.6, ...), custom_call_target="tpu_custom_call" | custom-call | flops 1610000000 | bytes 1 | tf_op jit(solution)/shard_map/pallas_call | solution.py:42
  12.7 3.5 %collective-permute-start.7 = (bf16[256,256]{1,0:T(8,128)(2,1)S(1)}, bf16[256,256]{1,0:T(8,128)(2,1)S(1)}, u32[]{:S(2)}, u32[]{:S(2)}) collective-permute-start(bf16[256,256]{1,0:T(8,128)(2,1)S(1)} %collective-permute-done.6.refs_2_.refs_5_), channel_id=1, source_target_pairs={{0,8},{4,12},{8,16},{12,20},{16,24},{20,28},{1,9},{5,13},{9,17},{1... | collective-permute-start | bytes 393224 | tf_op jit(solution)/shard_map/ppermute | solution.py:484
  16.2 3.5 %collective-permute-start.4 = (bf16[256,256]{1,0:T(8,128)(2,1)S(1)}, bf16[256,256]{1,0:T(8,128)(2,1)S(1)}, u32[]{:S(2)}, u32[]{:S(2)}) collective-permute-start(bf16[256,256]{1,0:T(8,128)(2,1)S(1)} %collective-permute-done.3.refs_1_.refs_4_), channel_id=1, source_target_pairs={{0,8},{4,12},{8,16},{12,20},{16,24},{20,28},{1,9},{5,13},{9,17},{1... | collective-permute-start | bytes 393224 | tf_op jit(solution)/shard_map/ppermute | solution.py:484
  20.4 1.9 %collective-permute-start.1 = (bf16[528,128]{1,0:T(8,128)(2,1)S(1)}, bf16[528,128]{1,0:T(8,128)(2,1)S(1)}, u32[]{:S(2)}, u32[]{:S(2)}) collective-permute-start(bf16[528,128]{1,0:T(8,128)(2,1)S(1)} %shard_map.179.refs_0_.refs_1_), channel_id=1, source_target_pairs={{0,8},{4,12},{8,16},{12,20},{16,24},{20,28},{1,9},{5,13},{9,17},{1... | collective-permute-start | bytes 405512 | tf_op jit(solution)/shard_map/ppermute | solution.py:484
  23.9 1.9 %collective-permute-start.8 = (bf16[256,256]{1,0:T(8,128)(2,1)S(1)}, bf16[256,256]{1,0:T(8,128)(2,1)S(1)}, u32[]{:S(2)}, u32[]{:S(2)}) collective-permute-start(bf16[256,256]{1,0:T(8,128)(2,1)S(1)} %collective-permute-done.7.refs_2_.refs_5_), channel_id=1, source_target_pairs={{0,8},{4,12},{8,16},{12,20},{16,24},{20,28},{1,9},{5,13},{9,17},{1... | collective-permute-start | bytes 393224 | tf_op jit(solution)/shard_map/ppermute | solution.py:484
  25.8 2.0 %collective-permute-start.5 = (bf16[256,256]{1,0:T(8,128)(2,1)S(1)}, bf16[256,256]{1,0:T(8,128)(2,1)S(1)}, u32[]{:S(2)}, u32[]{:S(2)}) collective-permute-start(bf16[256,256]{1,0:T(8,128)(2,1)S(1)} %collective-permute-done.4.refs_1_.refs_4_), channel_id=1, source_target_pairs={{0,8},{4,12},{8,16},{12,20},{16,24},{20,28},{1,9},{5,13},{9,17},{1... | collective-permute-start | bytes 393224 | tf_op jit(solution)/shard_map/ppermute | solution.py:484
  27.8 2.5 %shard_map.183 = (f32[4,1,512]{2,1,0:T(1,128)S(1)}, f32[4,1,512]{2,1,0:T(1,128)S(1)}, f32[4,128,512]{2,1,0:T(8,128)S(1)}) custom-call(s32[3]{0:T(128)S(1)} %get-tuple-element.97.place, bf16[256,1024]{1,0:T(8,128)(2,1)S(1)} %copy-done.2, bf16[256,256]{1,0:T(8,128)(2,1)S(1)} %pad_maximum_fusion.1.refs_4_.refs_1_, ...), custom_call_target="tpu_custom_call" | custom-call | flops 2990000128 | bytes 1 | tf_op jit(solution)/shard_map/pallas_call | solution.py:42
  31.5 4.4 %collective-permute-start.2 = (bf16[528,128]{1,0:T(8,128)(2,1)S(1)}, bf16[528,128]{1,0:T(8,128)(2,1)S(1)}, u32[]{:S(2)}, u32[]{:S(2)}) collective-permute-start(bf16[528,128]{1,0:T(8,128)(2,1)S(1)} %shard_map.180), channel_id=1, source_target_pairs={{0,16},{4,20},{8,24},{12,28},{1,17},{5,21},{9,25},{13,29},{2,18},{... | collective-permute-start | bytes 405512 | tf_op jit(solution)/shard_map/ppermute | solution.py:484
  36.0 1.6 %collective-permute-start.9 = (bf16[256,256]{1,0:T(8,128)(2,1)S(1)}, bf16[256,256]{1,0:T(8,128)(2,1)S(1)}, u32[]{:S(2)}, u32[]{:S(2)}) collective-permute-start(bf16[256,256]{1,0:T(8,128)(2,1)S(1)} %collective-permute-done.8.refs_2_.refs_5_), channel_id=1, source_target_pairs={{0,8},{4,12},{8,16},{12,20},{16,24},{20,28},{1,9},{5,13},{9,17},{1... | collective-permute-start | bytes 393224 | tf_op jit(solution)/shard_map/ppermute | solution.py:484
  38.1 1.9 %collective-permute-done.9.refs_2_.refs_5_ = bf16[256,256]{1,0:T(8,128)(2,1)S(1)} collective-permute-done((bf16[256,256]{1,0:T(8,128)(2,1)S(1)}, bf16[256,256]{1,0:T(8,128)(2,1)S(1)}, u32[]{:S(2)}, u32[]{:S(2)}) %collective-permute-start.9) | collective-permute-done | bytes 131104 | tf_op jit(solution)/shard_map/ppermute | solution.py:484
  44.8 1.4 %collective-permute-start.21 = (bf16[512,256]{1,0:T(8,128)(2,1)S(1)}, bf16[512,256]{1,0:T(8,128)(2,1)S(1)}, u32[]{:S(2)}, u32[]{:S(2)}) collective-permute-start(bf16[512,256]{1,0:T(8,128)(2,1)S(1)} %convert_element_type.21), channel_id=1, source_target_pairs={{8,0},{12,4},{16,8},{20,12},{24,16},{28,20},{9,1},{13,5},{17,9},{2... | collective-permute-start | bytes 786440 | tf_op jit(solution)/shard_map/ppermute | solution.py:487
  46.9 2.0 %shard_map.188 = (f32[256,1024]{1,0:T(8,128)S(1)}, f32[8,256]{1,0:T(8,128)S(1)}) custom-call(s32[2]{0:T(128)S(1)} %pad_add_fusion.place, f32[8,256]{1,0:T(8,128)S(1)} %get-tuple-element.53.refs_0_, f32[256,8]{1,0:T(8,128)S(1)} %get-tuple-element.54.refs_1_, bf16[256,1024]{1,0:T(8,128)(2,1)S(1)} %copy-done.4, bf16[256,1024]{1,0:T(8,128)(2,1)S(1)} %copy-done.5, ...), custom_call_target="tpu_custom_call" | custom-call | flops 2300000000 | bytes 1 | tf_op jit(solution)/shard_map/pallas_call | solution.py:42
  49.0 1.6 %collective-permute-start.14 = (f32[8,256]{1,0:T(8,128)S(1)}, f32[8,256]{1,0:T(8,128)S(1)}, u32[]{:S(2)}, u32[]{:S(2)}) collective-permute-start(f32[8,256]{1,0:T(8,128)S(1)} %get-tuple-element.69.refs_8_), channel_id=1, source_target_pairs={{0,2},{1,3},{2,0},{3,1},{4,6},{5,7},{6,4},{7,5},{8,10},{9,11},{10,... | collective-permute-start | bytes 24584 | tf_op jit(solution)/shard_map/ppermute | solution.py:616
  52.7 2.5 %shard_map.189 = (bf16[256,1024]{1,0:T(8,128)(2,1)}, bf16[256,1024]{1,0:T(8,128)(2,1)}, bf16[256,1024]{1,0:T(8,128)(2,1)S(1)}, bf16[2,528,128]{2,1,0:T(8,128)(2,1)S(1)}) custom-call(s32[2]{0:T(128)S(1)} %pad_add_fusion.place, f32[8,256]{1,0:T(8,128)S(1)} %get-tuple-element.53.refs_0_, f32[256,1024]{1,0:T(8,128)S(1)} %get-tuple-element.68.refs_1_, ...), custom_call_target="tpu_custom_call" | custom-call | flops 2875000064 | bytes 1 | tf_op jit(solution)/shard_map/pallas_call | solution.py:42
  57.8 3.6 %collective-permute-done.16.refs_1_ = bf16[528,128]{1,0:T(8,128)(2,1)S(1)} collective-permute-done((bf16[528,128]{1,0:T(8,128)(2,1)S(1)}, bf16[528,128]{1,0:T(8,128)(2,1)S(1)}, u32[]{:S(2)}, u32[]{:S(2)}) %collective-permute-start.16) | collective-permute-done | bytes 135200 | tf_op jit(solution)/shard_map/ppermute | solution.py:481
  64.0 7.0 %collective-permute-done.17.refs_1_.refs_2_ = bf16[528,128]{1,0:T(8,128)(2,1)S(1)} collective-permute-done((bf16[528,128]{1,0:T(8,128)(2,1)S(1)}, bf16[528,128]{1,0:T(8,128)(2,1)S(1)}, u32[]{:S(2)}, u32[]{:S(2)}) %collective-permute-start.17) | collective-permute-done | bytes 135200 | tf_op jit(solution)/shard_map/ppermute | solution.py:487
  73.0 1.5 %collective-permute-start.24 = (bf16[512,256]{1,0:T(8,128)(2,1)S(1)}, bf16[512,256]{1,0:T(8,128)(2,1)S(1)}, u32[]{:S(2)}, u32[]{:S(2)}) collective-permute-start(bf16[512,256]{1,0:T(8,128)(2,1)S(1)} %add_convert_fusion.1.refs_9_), channel_id=1, source_target_pairs={{8,0},{12,4},{16,8},{20,12},{24,16},{28,20},{9,1},{13,5},{17,9},{2... | collective-permute-start | bytes 786440 | tf_op jit(solution)/shard_map/ppermute | solution.py:487
  74.5 3.4 %shard_map.197 = (f32[512,256]{1,0:T(8,128)S(1)}, bf16[256,512]{1,0:T(8,128)(2,1)S(1)}, bf16[256,512]{1,0:T(8,128)(2,1)S(1)}) custom-call(s32[3]{0:T(128)S(1)} %get-tuple-element.97.place, bf16[256,1024]{1,0:T(8,128)(2,1)S(1)} %copy-done.2, bf16[256,1024]{1,0:T(8,128)(2,1)S(1)} %copy-done.3, f32[4,1,512]{2,1,0:T(1,128)S(1)} %get-tuple-element.65.refs_4_.refs_2_, ...), custom_call_target="tpu_custom_call" | custom-call | flops 3910000128 | bytes 1 | tf_op jit(solution)/shard_map/pallas_call | solution.py:42
  77.9 1.7 %collective-permute-start.23 = (bf16[256,512]{1,0:T(8,128)(2,1)S(1)}, bf16[256,512]{1,0:T(8,128)(2,1)S(1)}, u32[]{:S(2)}, u32[]{:S(2)}) collective-permute-start(bf16[256,512]{1,0:T(8,128)(2,1)S(1)} %get-tuple-element.88), channel_id=1, source_target_pairs={{0,4},{4,0},{8,12},{12,8},{16,20},{20,16},{24,28},{28,24},{1,5},{5... | collective-permute-start | bytes 786440 | tf_op jit(solution)/shard_map/ppermute | solution.py:481
  79.6 5.4 %collective-permute-done.18.refs_3_ = bf16[528,128]{1,0:T(8,128)(2,1)S(1)} collective-permute-done((bf16[528,128]{1,0:T(8,128)(2,1)S(1)}, bf16[528,128]{1,0:T(8,128)(2,1)S(1)}, u32[]{:S(2)}, u32[]{:S(2)}) %collective-permute-start.18) | collective-permute-done | bytes 135200 | tf_op jit(solution)/shard_map/ppermute | solution.py:487
  88.0 3.5 %shard_map.190 = (bf16[256,1024]{1,0:T(8,128)(2,1)}, f32[256,1024]{1,0:T(8,128)S(1)}, f32[256,1024]{1,0:T(8,128)S(1)}) custom-call(s32[2]{0:T(128)S(1)} %pad_add_fusion.place, f32[8,256]{1,0:T(8,128)S(1)} %get-tuple-element.53.refs_0_, f32[256,8]{1,0:T(8,128)S(1)} %get-tuple-element.54.refs_1_, bf16[256,1024]{1,0:T(8,128)(2,1)S(1)} %copy-done.4, ...), custom_call_target="tpu_custom_call" | custom-call | flops 3910000128 | bytes 1 | tf_op jit(solution)/shard_map/pallas_call | solution.py:42
  92.4 3.0 %shard_map.198 = (bf16[256,1024]{1,0:T(8,128)(2,1)}, bf16[256,1024]{1,0:T(8,128)(2,1)}, bf16[256,1024]{1,0:T(8,128)(2,1)}, bf16[256,1024]{1,0:T(8,128)(2,1)}, bf...) custom-call(s32[2]{0:T(128)S(1)} %pad_add_fusion.place, f32[8,256]{1,0:T(8,128)S(1)} %get-tuple-element.53.refs_0_, ...), custom_call_target="tpu_custom_call" | custom-call | flops 2300000000 | bytes 1 | tf_op jit(solution)/shard_map/pallas_call | solution.py:42
  (80 shorter events, 26.4 us)
Async XLA Ops:
  1.7 10.9 %collective-permute-start.6 = (bf16[256,256]{1,0:T(8,128)(2,1)S(1)}, bf16[256,256]{1,0:T(8,128)(2,1)S(1)}, u32[]{:S(2)}, u32[]{:S(2)}) collective-permute-start(bf16[256,256]{1,0:T(8,128)(2,1)S(1)} %pad_maximum_fusion.refs_3_), channel_id=1, source_target_pairs={{0,4},{4,0},{8,12},{12,8},{16,20},{20,16},{24,28},{28,24},{1,5},{5... | collective-permute-start | bytes 393224 | tf_op jit(solution)/shard_map/ppermute | solution.py:481
  4.8 11.4 %collective-permute-start.3 = (bf16[256,256]{1,0:T(8,128)(2,1)S(1)}, bf16[256,256]{1,0:T(8,128)(2,1)S(1)}, u32[]{:S(2)}, u32[]{:S(2)}) collective-permute-start(bf16[256,256]{1,0:T(8,128)(2,1)S(1)} %pad_maximum_fusion.1.refs_4_.refs_1_), channel_id=1, source_target_pairs={{0,8},{4,12},{8,16},{12,20},{16,24},{20,28},{1,9},{5,13},{9,17},{1... | collective-permute-start | bytes 393224 | tf_op jit(solution)/shard_map/ppermute | solution.py:484
  9.9 9.9 %collective-permute-start = (bf16[528,128]{1,0:T(8,128)(2,1)S(1)}, bf16[528,128]{1,0:T(8,128)(2,1)S(1)}, u32[]{:S(2)}, u32[]{:S(2)}) collective-permute-start(bf16[528,128]{1,0:T(8,128)(2,1)S(1)} %get-tuple-element.101.refs_7_), channel_id=1, source_target_pairs={{0,4},{4,0},{8,12},{12,8},{16,20},{20,16},{24,28},{28,24},{1,5},{5... | collective-permute-start | bytes 405512 | tf_op jit(solution)/shard_map/ppermute | solution.py:481
  11.4 16.4 %collective-permute-start.10 = (bf16[256,512]{1,0:T(8,128)(2,1)S(1)}, bf16[256,512]{1,0:T(8,128)(2,1)S(1)}, u32[]{:S(2)}, u32[]{:S(2)}) collective-permute-start(bf16[256,512]{1,0:T(8,128)(2,1)S(1)} %shard_map.181), channel_id=1, source_target_pairs={{0,4},{4,0},{8,12},{12,8},{16,20},{20,16},{24,28},{28,24},{1,5},{5... | collective-permute-start | bytes 786440 | tf_op jit(solution)/shard_map/ppermute | solution.py:481
  12.7 11.2 %collective-permute-start.7 = (bf16[256,256]{1,0:T(8,128)(2,1)S(1)}, bf16[256,256]{1,0:T(8,128)(2,1)S(1)}, u32[]{:S(2)}, u32[]{:S(2)}) collective-permute-start(bf16[256,256]{1,0:T(8,128)(2,1)S(1)} %collective-permute-done.6.refs_2_.refs_5_), channel_id=1, source_target_pairs={{0,8},{4,12},{8,16},{12,20},{16,24},{20,28},{1,9},{5,13},{9,17},{1... | collective-permute-start | bytes 393224 | tf_op jit(solution)/shard_map/ppermute | solution.py:484
  16.2 9.6 %collective-permute-start.4 = (bf16[256,256]{1,0:T(8,128)(2,1)S(1)}, bf16[256,256]{1,0:T(8,128)(2,1)S(1)}, u32[]{:S(2)}, u32[]{:S(2)}) collective-permute-start(bf16[256,256]{1,0:T(8,128)(2,1)S(1)} %collective-permute-done.3.refs_1_.refs_4_), channel_id=1, source_target_pairs={{0,8},{4,12},{8,16},{12,20},{16,24},{20,28},{1,9},{5,13},{9,17},{1... | collective-permute-start | bytes 393224 | tf_op jit(solution)/shard_map/ppermute | solution.py:484
  20.4 10.5 %collective-permute-start.1 = (bf16[528,128]{1,0:T(8,128)(2,1)S(1)}, bf16[528,128]{1,0:T(8,128)(2,1)S(1)}, u32[]{:S(2)}, u32[]{:S(2)}) collective-permute-start(bf16[528,128]{1,0:T(8,128)(2,1)S(1)} %shard_map.179.refs_0_.refs_1_), channel_id=1, source_target_pairs={{0,8},{4,12},{8,16},{12,20},{16,24},{20,28},{1,9},{5,13},{9,17},{1... | collective-permute-start | bytes 405512 | tf_op jit(solution)/shard_map/ppermute | solution.py:484
  22.9 15.3 %collective-permute-start.11 = (bf16[256,512]{1,0:T(8,128)(2,1)S(1)}, bf16[256,512]{1,0:T(8,128)(2,1)S(1)}, u32[]{:S(2)}, u32[]{:S(2)}) collective-permute-start(bf16[256,512]{1,0:T(8,128)(2,1)S(1)} %shard_map.182), channel_id=1, source_target_pairs={{0,4},{4,0},{8,12},{12,8},{16,20},{20,16},{24,28},{28,24},{1,5},{5... | collective-permute-start | bytes 786440 | tf_op jit(solution)/shard_map/ppermute | solution.py:481
  23.9 12.1 %collective-permute-start.8 = (bf16[256,256]{1,0:T(8,128)(2,1)S(1)}, bf16[256,256]{1,0:T(8,128)(2,1)S(1)}, u32[]{:S(2)}, u32[]{:S(2)}) collective-permute-start(bf16[256,256]{1,0:T(8,128)(2,1)S(1)} %collective-permute-done.7.refs_2_.refs_5_), channel_id=1, source_target_pairs={{0,8},{4,12},{8,16},{12,20},{16,24},{20,28},{1,9},{5,13},{9,17},{1... | collective-permute-start | bytes 393224 | tf_op jit(solution)/shard_map/ppermute | solution.py:484
  25.8 12.3 %collective-permute-start.5 = (bf16[256,256]{1,0:T(8,128)(2,1)S(1)}, bf16[256,256]{1,0:T(8,128)(2,1)S(1)}, u32[]{:S(2)}, u32[]{:S(2)}) collective-permute-start(bf16[256,256]{1,0:T(8,128)(2,1)S(1)} %collective-permute-done.4.refs_1_.refs_4_), channel_id=1, source_target_pairs={{0,8},{4,12},{8,16},{12,20},{16,24},{20,28},{1,9},{5,13},{9,17},{1... | collective-permute-start | bytes 393224 | tf_op jit(solution)/shard_map/ppermute | solution.py:484
  31.5 9.6 %collective-permute-start.2 = (bf16[528,128]{1,0:T(8,128)(2,1)S(1)}, bf16[528,128]{1,0:T(8,128)(2,1)S(1)}, u32[]{:S(2)}, u32[]{:S(2)}) collective-permute-start(bf16[528,128]{1,0:T(8,128)(2,1)S(1)} %shard_map.180), channel_id=1, source_target_pairs={{0,16},{4,20},{8,24},{12,28},{1,17},{5,21},{9,25},{13,29},{2,18},{... | collective-permute-start | bytes 405512 | tf_op jit(solution)/shard_map/ppermute | solution.py:484
  36.0 4.1 %collective-permute-start.9 = (bf16[256,256]{1,0:T(8,128)(2,1)S(1)}, bf16[256,256]{1,0:T(8,128)(2,1)S(1)}, u32[]{:S(2)}, u32[]{:S(2)}) collective-permute-start(bf16[256,256]{1,0:T(8,128)(2,1)S(1)} %collective-permute-done.8.refs_2_.refs_5_), channel_id=1, source_target_pairs={{0,8},{4,12},{8,16},{12,20},{16,24},{20,28},{1,9},{5,13},{9,17},{1... | collective-permute-start | bytes 393224 | tf_op jit(solution)/shard_map/ppermute | solution.py:484
  41.8 5.1 %collective-permute-start.12 = (bf16[512,128]{1,0:T(8,128)(2,1)S(1)}, bf16[512,128]{1,0:T(8,128)(2,1)S(1)}, u32[]{:S(2)}, u32[]{:S(2)}) collective-permute-start(bf16[512,128]{1,0:T(8,128)(2,1)S(1)} %get-tuple-element.67), channel_id=1, source_target_pairs={{0,4},{4,0},{8,12},{12,8},{16,20},{20,16},{24,28},{28,24},{1,5},{5... | collective-permute-start | bytes 393224 | tf_op jit(solution)/shard_map/ppermute | solution.py:481
  43.1 48.4 %collective-permute-start.20 = (bf16[256,512]{1,0:T(8,128)(2,1)S(1)}, bf16[256,512]{1,0:T(8,128)(2,1)S(1)}, u32[]{:S(2)}, u32[]{:S(2)}) collective-permute-start(bf16[256,512]{1,0:T(8,128)(2,1)S(1)} %get-tuple-element.79), channel_id=1, source_target_pairs={{0,4},{4,0},{8,12},{12,8},{16,20},{20,16},{24,28},{28,24},{1,5},{5... | collective-permute-start | bytes 786440 | tf_op jit(solution)/shard_map/ppermute | solution.py:481
  44.8 11.7 %collective-permute-start.21 = (bf16[512,256]{1,0:T(8,128)(2,1)S(1)}, bf16[512,256]{1,0:T(8,128)(2,1)S(1)}, u32[]{:S(2)}, u32[]{:S(2)}) collective-permute-start(bf16[512,256]{1,0:T(8,128)(2,1)S(1)} %convert_element_type.21), channel_id=1, source_target_pairs={{8,0},{12,4},{16,8},{20,12},{24,16},{28,20},{9,1},{13,5},{17,9},{2... | collective-permute-start | bytes 786440 | tf_op jit(solution)/shard_map/ppermute | solution.py:487
  49.0 3.7 %collective-permute-start.14 = (f32[8,256]{1,0:T(8,128)S(1)}, f32[8,256]{1,0:T(8,128)S(1)}, u32[]{:S(2)}, u32[]{:S(2)}) collective-permute-start(f32[8,256]{1,0:T(8,128)S(1)} %get-tuple-element.69.refs_8_), channel_id=1, source_target_pairs={{0,2},{1,3},{2,0},{3,1},{4,6},{5,7},{6,4},{7,5},{8,10},{9,11},{10,... | collective-permute-start | bytes 24584 | tf_op jit(solution)/shard_map/ppermute | solution.py:616
  55.2 6.2 %collective-permute-start.16 = (bf16[528,128]{1,0:T(8,128)(2,1)S(1)}, bf16[528,128]{1,0:T(8,128)(2,1)S(1)}, u32[]{:S(2)}, u32[]{:S(2)}) collective-permute-start(bf16[528,128]{1,0:T(8,128)(2,1)S(1)} %get-tuple-element.99), channel_id=1, source_target_pairs={{0,4},{4,0},{8,12},{12,8},{16,20},{20,16},{24,28},{28,24},{1,5},{5... | collective-permute-start | bytes 405512 | tf_op jit(solution)/shard_map/ppermute | solution.py:481
  56.5 16.3 %collective-permute-start.22 = (bf16[512,256]{1,0:T(8,128)(2,1)S(1)}, bf16[512,256]{1,0:T(8,128)(2,1)S(1)}, u32[]{:S(2)}, u32[]{:S(2)}) collective-permute-start(bf16[512,256]{1,0:T(8,128)(2,1)S(1)} %add_convert_fusion.2.refs_9_), channel_id=1, source_target_pairs={{8,0},{12,4},{16,8},{20,12},{24,16},{28,20},{9,1},{13,5},{17,9},{2... | collective-permute-start | bytes 786440 | tf_op jit(solution)/shard_map/ppermute | solution.py:487
  62.1 8.9 %collective-permute-start.17 = (bf16[528,128]{1,0:T(8,128)(2,1)S(1)}, bf16[528,128]{1,0:T(8,128)(2,1)S(1)}, u32[]{:S(2)}, u32[]{:S(2)}) collective-permute-start(bf16[528,128]{1,0:T(8,128)(2,1)S(1)} %shard_map.191.refs_0_), channel_id=1, source_target_pairs={{8,0},{12,4},{16,8},{20,12},{24,16},{28,20},{9,1},{13,5},{17,9},{2... | collective-permute-start | bytes 405512 | tf_op jit(solution)/shard_map/ppermute | solution.py:487
  71.6 13.5 %collective-permute-start.18 = (bf16[528,128]{1,0:T(8,128)(2,1)S(1)}, bf16[528,128]{1,0:T(8,128)(2,1)S(1)}, u32[]{:S(2)}, u32[]{:S(2)}) collective-permute-start(bf16[528,128]{1,0:T(8,128)(2,1)S(1)} %shard_map.192), channel_id=1, source_target_pairs={{16,0},{20,4},{24,8},{28,12},{17,1},{21,5},{25,9},{29,13},{18,2},{... | collective-permute-start | bytes 405512 | tf_op jit(solution)/shard_map/ppermute | solution.py:487
  73.0 14.1 %collective-permute-start.24 = (bf16[512,256]{1,0:T(8,128)(2,1)S(1)}, bf16[512,256]{1,0:T(8,128)(2,1)S(1)}, u32[]{:S(2)}, u32[]{:S(2)}) collective-permute-start(bf16[512,256]{1,0:T(8,128)(2,1)S(1)} %add_convert_fusion.1.refs_9_), channel_id=1, source_target_pairs={{8,0},{12,4},{16,8},{20,12},{24,16},{28,20},{9,1},{13,5},{17,9},{2... | collective-permute-start | bytes 786440 | tf_op jit(solution)/shard_map/ppermute | solution.py:487
  77.9 13.6 %collective-permute-start.23 = (bf16[256,512]{1,0:T(8,128)(2,1)S(1)}, bf16[256,512]{1,0:T(8,128)(2,1)S(1)}, u32[]{:S(2)}, u32[]{:S(2)}) collective-permute-start(bf16[256,512]{1,0:T(8,128)(2,1)S(1)} %get-tuple-element.88), channel_id=1, source_target_pairs={{0,4},{4,0},{8,12},{12,8},{16,20},{20,16},{24,28},{28,24},{1,5},{5... | collective-permute-start | bytes 786440 | tf_op jit(solution)/shard_map/ppermute | solution.py:481
  85.7 5.8 %collective-permute-start.19 = (bf16[512,128]{1,0:T(8,128)(2,1)S(1)}, bf16[512,128]{1,0:T(8,128)(2,1)S(1)}, u32[]{:S(2)}, u32[]{:S(2)}) collective-permute-start(bf16[512,128]{1,0:T(8,128)(2,1)S(1)} %get-tuple-element.77), channel_id=1, source_target_pairs={{0,4},{4,0},{8,12},{12,8},{16,20},{20,16},{24,28},{28,24},{1,5},{5... | collective-permute-start | bytes 393224 | tf_op jit(solution)/shard_map/ppermute | solution.py:481
  87.2 5.3 %collective-permute-start.25 = (bf16[256,256]{1,0:T(8,128)(2,1)S(1)}, bf16[256,256]{1,0:T(8,128)(2,1)S(1)}, u32[]{:S(2)}, u32[]{:S(2)}) collective-permute-start(bf16[256,256]{1,0:T(8,128)(2,1)S(1)} %slice.40), channel_id=1, source_target_pairs={{0,4},{4,0},{8,12},{12,8},{16,20},{20,16},{24,28},{28,24},{1,5},{5... | collective-permute-start | bytes 393224 | tf_op jit(solution)/shard_map/ppermute | solution.py:481
  (11 other events, 38.2 us)

commit v3 on v2

--- a/solution.py
+++ b/solution.py
@@ -15,7 +15,7 @@
 bf16 = jnp.bfloat16
 VMEM_BYTES = 24 * 1024 * 1024
 FORWARD_CHUNK = 128
-FLOPS_PER_MICRO = 1150 * 10**6
+FLOPS_PER_MICRO = 2000 * 10**6
 BACKWARD_CHUNK = 256
 
 SMEM_SPEC = pl.BlockSpec(memory_space=pltpu.SMEM)
@@ -35,7 +35,7 @@
     return lax.dot_general(a, b, (((0,), (0,)), ((), ())), preferred_element_type=f32)
 
 
-def whole_call(kernel, place, arrays, outs, micros, after=(), aliases={}, scratch=()):
+def whole_call(kernel, place, arrays, outs, micros, after=(), aliases={}, scratch=(), out_spec=VMEM_SPEC):
     def ordered(place, *refs):
         kernel(place, *refs[: len(arrays)], *refs[len(arrays) + len(after) :])
 
@@ -43,7 +43,7 @@
         ordered,
         out_shape=outs,
         in_specs=[SMEM_SPEC] + [VMEM_SPEC] * len(arrays) + [ANY_SPEC] * len(after),
-        out_specs=[VMEM_SPEC] * len(outs),
+        out_specs=[out_spec] * len(outs),
         scratch_shapes=list(scratch),
         input_output_aliases={i + 1: o for i, o in aliases.items()},
         compiler_params=pltpu.CompilerParams(vmem_limit_bytes=VMEM_BYTES),
@@ -255,27 +255,37 @@
 
 def final_kernel(heads, fold, place, row_ref, col_ref, key_ref, value_ref, key_part_ref, value_part_ref, *rest):
     states, rest = rest[:fold], rest[fold:]
-    halves, outs = rest[:-6], rest[-6:]
+    *halves, key_made, value_made, sems = rest
+    halves, outs = halves[:-6], halves[-6:]
     y = place[0]
     rows = key_ref.shape[0]
+    copies = []
+
+    def send(source, target):
+        copies.append(pltpu.make_async_copy(source, target, sems.at[len(copies)]))
+        copies[-1].start()
+
+    for i in range(fold):
+        at = (y + i) % fold
+        for out, part in ((outs[2], halves[i]), (outs[3], halves[fold + i])):
+            size = part.shape[1]
+            send(part, out.at[:, pl.ds(pl.multiple_of(at * size, DH), size)])
+        for j in range(2):
+            part = halves[2 * fold + i].at[:rows, j * DH : (j + 1) * DH]
+            send(part, outs[4 + j].at[:, pl.ds(pl.multiple_of(at * DH, DH), DH)])
     for h in range(heads):
-        key, value = key_ref[:, head_rows(h)], value_ref[:, head_rows(h)]
+        span = head_rows(h)
+        key, value = key_ref[:, span], value_ref[:, span]
         tail = jnp.exp(row_ref[h : h + 1, rows - 1 : rows] - col_ref[:, h : h + 1])
         state = pick_state(states, h, heads // fold, y)
-        key_grad = key_part_ref[:, head_rows(h)] + tail * nt(value, state)
-        value_grad = value_part_ref[:, head_rows(h)] + tail * nn(key, state)
-        outs[0][:, head_rows(h)] = key_grad.astype(bf16)
-        outs[1][:, head_rows(h)] = value_grad.astype(bf16)
-    count = len(halves) // 3
-    for i in range(fold):
-        at = (y + i) % fold
-        for out, part in ((outs[2], halves[i]), (outs[3], halves[count + i])):
-            size = part.shape[1]
-            out[:, pl.ds(pl.multiple_of(at * size, DH), size)] = part[...]
-        part = halves[2 * count + i]
-        for j in range(2):
-            there = pl.ds(pl.multiple_of(at * DH, DH), DH)
-            outs[4 + j][:, there] = part[:rows, j * DH : (j + 1) * DH]
+        key_made[:, span] = (key_part_ref[:, span] + tail * nt(value, state)).astype(bf16)
+        value_made[:, span] = (value_part_ref[:, span] + tail * nn(key, state)).astype(bf16)
+        if h % 2 == 1:
+            pair = slice((h - 1) * DH, (h + 1) * DH)
+            send(key_made.at[:, pair], outs[0].at[:, pair])
+            send(value_made.at[:, pair], outs[1].at[:, pair])
+    for copy in copies:
+        copy.wait()
 
 
 def diagonal_mask(y, keys, first, count, tokens, rows):
@@ -447,7 +457,7 @@
         if not first:
             aliases = {len(arrays) - 1: 1}
     kernel = functools.partial(soft_backward_kernel, fold, tokens, group, diagonal, first)
-    return whole_call(kernel, place, arrays, outs, 3.4, after, aliases)
+    return whole_call(kernel, place, arrays, outs, 0.01 if diagonal else 3.4, after, aliases)
 
 
 def body(
@@ -480,11 +490,13 @@
     def swap(a):
         return lax.ppermute(a, "ctx", [(i, i ^ 1) for i in range(count)])
 
-    def up(a, s):
-        return lax.ppermute(a, "ctx", [(i, i + fold * s) for i in range(count - fold * s)])
-
-    def down(a, s):
-        return lax.ppermute(a, "ctx", [(i + fold * s, i) for i in range(count - fold * s)])
+    def up(a, s, least=0):
+        pairs = [(i, i + fold * s) for i in range(fold * least, count - fold * s)]
+        return lax.ppermute(a, "ctx", pairs)
+
+    def down(a, s, least=0):
+        pairs = [(i + fold * s, i) for i in range(fold * max(least - s, 0), count - fold * s)]
+        return lax.ppermute(a, "ctx", pairs)
 
     def own_columns(a):
         size = a.shape[1] // 2
@@ -494,8 +506,8 @@
         size = a.shape[1] // 2
         return jnp.where(y == 0, a[:, size:], a[:, :size])
 
-    def each(move, parts, s):
-        return [move(a, s) for a in parts]
+    def each(move, parts, *way):
+        return [move(a, *way) for a in parts]
 
     def at_lap(s):
         return jnp.concatenate((place, jnp.asarray(s, jnp.int32)[None]))
@@ -534,7 +546,7 @@
     if unrolled:
         kvs = [kv]
         for s in range(1, laps):
-            kvs.append(each(up, kvs[-1], 1))
+            kvs.append(each(up, kvs[-1], 1, s - 1))
 
     def pair_states(own, other, backward, after=()):
         if fold == 1:
@@ -572,11 +584,11 @@
         return soft_backward(at_lap(s), *whole, isinstance(s, int) and s == 0, after)
 
     joint, pair = pair_states(own_msg, oth_msg, False)
-    soft = forward(kv, 0, None, False)
     if fold > 1:
         (grad_sent,) = whole_call(soft_pack_kernel, place, (soft_grad,), [half], 0.6, (joint,))
         rec += (swap(grad_sent),)
     joint, far = send_states(joint, False)
+    soft = forward(kv, 0, None, False, (joint,))
     if unrolled:
         for s in range(1, laps - 1):
             soft = forward(kvs[s], s, soft, False)
@@ -590,16 +602,11 @@
 
         (last_kv, soft), far_kvs = lax.scan(far_forward, (kv, soft), jnp.arange(1, laps - 1))
         last_kv = each(up, last_kv, 1)
-    soft = forward(last_kv, laps - 1, soft, True)
-    outs, (logs, deltas) = soft[:fold], soft[fold:]
-    kept, carried = take_states((*pair, *far), False, (logs,))
-
-    def added(kv_grad, hop):
-        return (kv_grad + hop.astype(f32)).astype(bf16)
-
-    kv_grad, carry = backward(last_kv, laps - 1, None)
-    hop = down(kv_grad.astype(bf16), 1)
-
+    kept, carried = take_states((*pair, *far), False, (soft[0],))
+    soft = forward(last_kv, laps - 1, soft, True, (kept,))
+    outs, (logs, deltas) = list(soft[:fold]), soft[fold:]
+    if fold > 1:
+        outs[1] = swap(outs[1])
     attended, stats = whole_call(
         functools.partial(lin_attend_kernel, heads, fold),
         place,
@@ -609,6 +616,7 @@
             jax.ShapeDtypeStruct((8, tokens), f32),
         ],
         2.0,
+        (logs,),
     )
     tp = lax.axis_size("tp")
     if tp <= 4 and tp & (tp - 1) == 0:
@@ -617,6 +625,12 @@
         ]
     else:
         all_stats = [lax.psum(stats, "tp")]
+
+    def added(kv_grad, hop):
+        return (kv_grad + hop.astype(f32)).astype(bf16)
+
+    kv_grad, carry = backward(last_kv, laps - 1, None, (stats, outs[-1]))
+    hop = down(kv_grad.astype(bf16), 1, laps - 1 if unrolled else 0)
 
     def norm(after):
         return whole_call(
@@ -628,16 +642,18 @@
             after,
         )
 
+    lin_out, lin_gate_grad, att_grad, back_msgs = norm((carry,))
     if unrolled:
-        after = ()
+        after = (back_msgs,)
         for s in range(laps - 2, 0, -1):
             kv_grad, carry = backward(kvs[s], s, carry, after)
+            moved = added(kv_grad, hop)
+            hop = down(moved, 1, s)
             if s == laps - 2:
-                lin_out, lin_gate_grad, att_grad, back_msgs = norm(())
-            moved = added(kv_grad, hop)
-            hop = down(moved, 1)
-            after = (moved,)
+                joint, pair = pair_states(back_msgs[0], back_msgs[fold - 1], True, (moved,))
+            after = (joint, moved)
     else:
+        after = ()
 
         def far_backward(state, given):
             hop, carry = state
@@ -647,11 +663,9 @@
 
         given = (jnp.arange(1, laps - 1), far_kvs)
         (hop, carry), _ = lax.scan(far_backward, (hop, carry), given, reverse=True)
-        lin_out, lin_gate_grad, att_grad, back_msgs = norm((carry,))
-        after = ()
-    joint, pair = pair_states(back_msgs[0], back_msgs[fold - 1], True)
-    kv_grad, *query_grads = backward(kv, 0, carry, after)
-    joint, far = send_states(joint, True)
+        joint, pair = pair_states(back_msgs[0], back_msgs[fold - 1], True)
+    joint, far = send_states(joint, True, after)
+    kv_grad, *query_grads = backward(kv, 0, carry, (joint,))
     kept, returned = take_states((*pair, *far), True)
     total = added(kv_grad, hop)
     part = jax.ShapeDtypeStruct((tokens, heads * DH), f32)
@@ -660,11 +674,11 @@
         place,
         (log_rows, log_cols, lin_query, lin_key, lin_value, att_grad, *carried),
         [flat, part, part],
-        3.4,
+        0.01,
     )
-    outs, kv_grads = list(outs), [total]
+    kv_grads = [total]
     if fold > 1:
-        outs[1], query_grads[1] = swap(outs[1]), swap(query_grads[1])
+        query_grads[1] = swap(query_grads[1])
         kv_grads.append(swap(total[tokens:]))
     thin = jax.ShapeDtypeStruct(soft_key.shape, bf16)
     lin_key_grad, lin_value_grad, soft_out, soft_query_grad, soft_key_grad, soft_value_grad = whole_call(
@@ -676,6 +690,12 @@
         ),
         [flat, flat, flat, flat, thin, thin],
         2.0,
+        scratch=(
+            pltpu.VMEM(flat.shape, bf16),
+            pltpu.VMEM(flat.shape, bf16),
+            pltpu.SemaphoreType.DMA((4 * fold + heads,)),
+        ),
+        out_spec=ANY_SPEC,
     )
     return (
         lin_out,

time: 96.3 us -> 92.5 us (0.961)
  starting transfers between devices: 44 us -> 38.9 us
  waiting for transfers between devices: 20.9 us -> 22.8 us
    ppermute x13, starting transfers between devices: 29.1 us -> 24.9 us  [the longest x8 19.4 us: up(): return lax.ppermute(a, 'ctx', pairs)]
    ppermute x10, waiting for transfers between devices: 5.25 us -> 7.3 us  [swap(): return lax.ppermute(a, 'ctx', [(i, i ^ 1) for i in range(count)])]
  transfers between devices with their start and end apart: 26 -> 26, of which waited for: 8 -> 6; matrix products, arithmetic and copies ran while one was open for 1% -> 1% of each run, Pallas kernels for 25% -> 26%
where the time goes in v3:
time: 92.5 us; the launch traced here: 91.9 us
  starting transfers between devices  38.9 us (42%)
  Pallas kernels  26.8 us (29%)
  waiting for transfers between devices  22.8 us (25%)
  other arithmetic  1.52 us (2%)
  between operations  1.29 us (1%)
    pallas_call x21, Pallas kernels, whole_call(): pl.pallas_call(ordered, out_shape=outs, in_specs=[SMEM_SPEC] + [VMEM_SPEC...  26.8 us
    ppermute x8, starting transfers between devices, up(): return lax.ppermute(a, 'ctx', pairs)  19.4 us
    ppermute x5, waiting for transfers between devices, down(): return lax.ppermute(a, 'ctx', pairs)  15 us
    ppermute x10, starting transfers between devices, swap(): return lax.ppermute(a, 'ctx', [(i, i ^ 1) for i in range(count)])  12.1 us
    ppermute x10, waiting for transfers between devices, swap(): return lax.ppermute(a, 'ctx', [(i, i ^ 1) for i in range(count)])  7.3 us
    ppermute x5, starting transfers between devices, down(): return lax.ppermute(a, 'ctx', pairs)  5.45 us
    ppermute x3, starting transfers between devices, body(): lax.ppermute(stats, 'tp', [(i, i ^ k) for i in range(tp)])  1.92 us
  transfers between devices with their start and end apart: 26, of which 6 were waited for; matrix products, arithmetic and copies ran while one was open for 1% of the time, Pallas kernels for 26%

profile of v3, /device:TPU:0, one launch (start us, length us, event | category | flops | bytes accessed | tf_op | source)
XLA Modules:
  0.0 91.9 jit_solution(2145649943149094361)
XLA Ops:
  1.7 3.0 %collective-permute-start.5 = (bf16[256,256]{1,0:T(8,128)(2,1)S(1)}, bf16[256,256]{1,0:T(8,128)(2,1)S(1)}, u32[]{:S(2)}, u32[]{:S(2)}) collective-permute-start(bf16[256,256]{1,0:T(8,128)(2,1)S(1)} %pad_maximum_fusion.refs_3_), channel_id=1, source_target_pairs={{0,4},{4,0},{8,12},{12,8},{16,20},{20,16},{24,28},{28,24},{1,5},{5... | collective-permute-start | bytes 393224 | tf_op jit(solution)/shard_map/ppermute | solution.py:491
  4.8 3.5 %collective-permute-start.3 = (bf16[256,256]{1,0:T(8,128)(2,1)S(1)}, bf16[256,256]{1,0:T(8,128)(2,1)S(1)}, u32[]{:S(2)}, u32[]{:S(2)}) collective-permute-start(bf16[256,256]{1,0:T(8,128)(2,1)S(1)} %pad_maximum_fusion.1.refs_4_.refs_1_), channel_id=1, source_target_pairs={{0,8},{4,12},{8,16},{12,20},{16,24},{20,28},{1,9},{5,13},{9,17},{1... | collective-permute-start | bytes 393224 | tf_op jit(solution)/shard_map/ppermute | solution.py:495
  8.4 1.4 %shard_map.178 = (bf16[2,528,128]{2,1,0:T(8,128)(2,1)S(1)}, f32[8,256]{1,0:T(8,128)S(1)}, f32[256,8]{1,0:T(8,128)S(1)}) custom-call(s32[2]{0:T(128)S(1)} %pad_add_fusion.place, f32[8,256]{1,0:T(8,128)S(1)} %copy-done.7, bf16[256,1024]{1,0:T(8,128)(2,1)S(1)} %copy-done.3, bf16[256,1024]{1,0:T(8,128)(2,1)S(1)} %copy-done.4, ...), custom_call_target="tpu_custom_call" | custom-call | flops 2800000000 | bytes 1 | tf_op jit(solution)/shard_map/pallas_call | solution.py:42
  11.4 1.2 %collective-permute-start.8 = (bf16[256,512]{1,0:T(8,128)(2,1)S(1)}, bf16[256,512]{1,0:T(8,128)(2,1)S(1)}, u32[]{:S(2)}, u32[]{:S(2)}) collective-permute-start(bf16[256,512]{1,0:T(8,128)(2,1)S(1)} %shard_map.181), channel_id=1, source_target_pairs={{0,4},{4,0},{8,12},{12,8},{16,20},{20,16},{24,28},{28,24},{1,5},{5... | collective-permute-start | bytes 786440 | tf_op jit(solution)/shard_map/ppermute | solution.py:491
  12.7 3.5 %collective-permute-start.6 = (bf16[256,256]{1,0:T(8,128)(2,1)S(1)}, bf16[256,256]{1,0:T(8,128)(2,1)S(1)}, u32[]{:S(2)}, u32[]{:S(2)}) collective-permute-start(bf16[256,256]{1,0:T(8,128)(2,1)S(1)} %collective-permute-done.5.refs_2_.refs_5_), channel_id=1, source_target_pairs={{0,8},{4,12},{8,16},{12,20},{16,24},{20,28},{1,9},{5,13},{9,17},{1... | collective-permute-start | bytes 393224 | tf_op jit(solution)/shard_map/ppermute | solution.py:495
  17.5 4.7 %collective-permute-start.1 = (bf16[528,128]{1,0:T(8,128)(2,1)S(1)}, bf16[528,128]{1,0:T(8,128)(2,1)S(1)}, u32[]{:S(2)}, u32[]{:S(2)}) collective-permute-start(bf16[528,128]{1,0:T(8,128)(2,1)S(1)} %shard_map.179.refs_0_.refs_1_), channel_id=1, source_target_pairs={{0,8},{4,12},{8,16},{12,20},{16,24},{20,28},{1,9},{5,13},{9,17},{1... | collective-permute-start | bytes 405512 | tf_op jit(solution)/shard_map/ppermute | solution.py:495
  25.8 5.1 %collective-permute-start.2 = (bf16[528,128]{1,0:T(8,128)(2,1)S(1)}, bf16[528,128]{1,0:T(8,128)(2,1)S(1)}, u32[]{:S(2)}, u32[]{:S(2)}) collective-permute-start(bf16[528,128]{1,0:T(8,128)(2,1)S(1)} %shard_map.180.refs_4_), channel_id=1, source_target_pairs={{0,16},{4,20},{8,24},{12,28},{1,17},{5,21},{9,25},{13,29},{2,18},{... | collective-permute-start | bytes 405512 | tf_op jit(solution)/shard_map/ppermute | solution.py:495
  30.9 2.5 %shard_map.182 = (f32[4,1,512]{2,1,0:T(1,128)S(1)}, f32[4,1,512]{2,1,0:T(1,128)S(1)}, f32[4,128,512]{2,1,0:T(8,128)S(1)}) custom-call(s32[3]{0:T(128)S(1)} %get-tuple-element.107.place, bf16[256,1024]{1,0:T(8,128)(2,1)S(1)} %copy-done, bf16[256,256]{1,0:T(8,128)(2,1)S(1)} %pad_maximum_fusion.1.refs_4_.refs_1_, ...), custom_call_target="tpu_custom_call" | custom-call | flops 5200000000 | bytes 1 | tf_op jit(solution)/shard_map/pallas_call | solution.py:42
  35.9 1.7 %collective-permute-start.9 = (bf16[512,128]{1,0:T(8,128)(2,1)S(1)}, bf16[512,128]{1,0:T(8,128)(2,1)S(1)}, u32[]{:S(2)}, u32[]{:S(2)}) collective-permute-start(bf16[512,128]{1,0:T(8,128)(2,1)S(1)} %get-tuple-element.64), channel_id=1, source_target_pairs={{0,4},{4,0},{8,12},{12,8},{16,20},{20,16},{24,28},{28,24},{1,5},{5... | collective-permute-start | bytes 393224 | tf_op jit(solution)/shard_map/ppermute | solution.py:491
  37.6 1.2 %shard_map.187 = (bf16[256,512]{1,0:T(8,128)(2,1)S(1)}, bf16[256,512]{1,0:T(8,128)(2,1)S(1)}, f32[4,1,512]{2,1,0:T(1,128)S(1)}, f32[4,1,512]{2,1,0:T(1,128)S(1)}) custom-call(s32[3]{0:T(128)S(1)} %get-tuple-element.97.place, bf16[256,1024]{1,0:T(8,128)(2,1)S(1)} %copy-done, bf16[256,256]{1,0:T(8,128)(2,1)S(1)} %collective-permute-done.10.refs_1_.refs_4_, ...), custom_call_target="tpu_custom_call" | custom-call | flops 6000000000 | bytes 1 | tf_op jit(solution)/shard_map/pallas_call | solution.py:42
  39.4 3.0 %collective-permute-done.9.refs_9_.refs_7_ = bf16[512,128]{1,0:T(8,128)(2,1)S(1)} collective-permute-done((bf16[512,128]{1,0:T(8,128)(2,1)S(1)}, bf16[512,128]{1,0:T(8,128)(2,1)S(1)}, u32[]{:S(2)}, u32[]{:S(2)}) %collective-permute-start.9) | collective-permute-done | bytes 131104 | tf_op jit(solution)/shard_map/ppermute | solution.py:491
  42.4 2.0 %shard_map.188 = (f32[256,1024]{1,0:T(8,128)S(1)}, f32[8,256]{1,0:T(8,128)S(1)}) custom-call(s32[2]{0:T(128)S(1)} %pad_add_fusion.place, f32[8,256]{1,0:T(8,128)S(1)} %get-tuple-element.53.refs_0_, f32[256,8]{1,0:T(8,128)S(1)} %get-tuple-element.54.refs_1_, bf16[256,1024]{1,0:T(8,128)(2,1)S(1)} %copy-done.2, bf16[256,1024]{1,0:T(8,128)(2,1)S(1)} %copy-done.3, ...), custom_call_target="tpu_custom_call" | custom-call | flops 4000000000 | bytes 1 | tf_op jit(solution)/shard_map/pallas_call | solution.py:42
  44.4 1.6 %collective-permute-start.14 = (f32[8,256]{1,0:T(8,128)S(1)}, f32[8,256]{1,0:T(8,128)S(1)}, u32[]{:S(2)}, u32[]{:S(2)}) collective-permute-start(f32[8,256]{1,0:T(8,128)S(1)} %get-tuple-element.69.refs_8_), channel_id=1, source_target_pairs={{0,2},{1,3},{2,0},{3,1},{4,6},{5,7},{6,4},{7,5},{8,10},{9,11},{10,... | collective-permute-start | bytes 24584 | tf_op jit(solution)/shard_map/ppermute | solution.py:624
  48.2 2.5 %shard_map.190 = (bf16[256,1024]{1,0:T(8,128)(2,1)}, bf16[256,1024]{1,0:T(8,128)(2,1)}, bf16[256,1024]{1,0:T(8,128)(2,1)S(1)}, bf16[2,528,128]{2,1,0:T(8,128)(2,1)S(1)}) custom-call(s32[2]{0:T(128)S(1)} %pad_add_fusion.place, f32[8,256]{1,0:T(8,128)S(1)} %get-tuple-element.53.refs_0_, f32[256,1024]{1,0:T(8,128)S(1)} %get-tuple-element.68.refs_1_, ...), custom_call_target="tpu_custom_call" | custom-call | flops 5000000000 | bytes 1 | tf_op jit(solution)/shard_map/pallas_call | solution.py:42
  53.0 3.6 %collective-permute-done.17.refs_1_ = bf16[528,128]{1,0:T(8,128)(2,1)S(1)} collective-permute-done((bf16[528,128]{1,0:T(8,128)(2,1)S(1)}, bf16[528,128]{1,0:T(8,128)(2,1)S(1)}, u32[]{:S(2)}, u32[]{:S(2)}) %collective-permute-start.17) | collective-permute-done | bytes 135200 | tf_op jit(solution)/shard_map/ppermute | solution.py:491
  57.2 1.3 %collective-permute-start.19 = (bf16[528,128]{1,0:T(8,128)(2,1)S(1)}, bf16[528,128]{1,0:T(8,128)(2,1)S(1)}, u32[]{:S(2)}, u32[]{:S(2)}) collective-permute-start(bf16[528,128]{1,0:T(8,128)(2,1)S(1)} %shard_map.193.refs_9_.refs_0_.refs_2_), channel_id=1, source_target_pairs={{8,0},{12,4},{16,8},{20,12},{24,16},{28,20},{9,1},{13,5},{17,9},{2... | collective-permute-start | bytes 405512 | tf_op jit(solution)/shard_map/ppermute | solution.py:499
  59.2 5.6 %collective-permute-done.19.refs_1_.refs_2_ = bf16[528,128]{1,0:T(8,128)(2,1)S(1)} collective-permute-done((bf16[528,128]{1,0:T(8,128)(2,1)S(1)}, bf16[528,128]{1,0:T(8,128)(2,1)S(1)}, u32[]{:S(2)}, u32[]{:S(2)}) %collective-permute-start.19) | collective-permute-done | bytes 135200 | tf_op jit(solution)/shard_map/ppermute | solution.py:499
  65.5 1.3 %collective-permute-start.21 = (bf16[528,128]{1,0:T(8,128)(2,1)S(1)}, bf16[528,128]{1,0:T(8,128)(2,1)S(1)}, u32[]{:S(2)}, u32[]{:S(2)}) collective-permute-start(bf16[528,128]{1,0:T(8,128)(2,1)S(1)} %shard_map.195.refs_9_), channel_id=1, source_target_pairs={{16,0},{20,4},{24,8},{28,12},{17,1},{21,5},{25,9},{29,13},{18,2},{... | collective-permute-start | bytes 405512 | tf_op jit(solution)/shard_map/ppermute | solution.py:499
  66.8 1.5 %collective-permute-start.24 = (bf16[512,256]{1,0:T(8,128)(2,1)S(1)}, bf16[512,256]{1,0:T(8,128)(2,1)S(1)}, u32[]{:S(2)}, u32[]{:S(2)}) collective-permute-start(bf16[512,256]{1,0:T(8,128)(2,1)S(1)} %add_convert_fusion.1.refs_3_), channel_id=1, source_target_pairs={{8,0},{12,4},{16,8},{20,12},{24,16},{28,20},{9,1},{13,5},{17,9},{2... | collective-permute-start | bytes 786440 | tf_op jit(solution)/shard_map/ppermute | solution.py:499
  68.3 3.4 %shard_map.197 = (f32[512,256]{1,0:T(8,128)S(1)}, bf16[256,512]{1,0:T(8,128)(2,1)S(1)}, bf16[256,512]{1,0:T(8,128)(2,1)S(1)}) custom-call(s32[3]{0:T(128)S(1)} %get-tuple-element.107.place, bf16[256,1024]{1,0:T(8,128)(2,1)S(1)} %copy-done, bf16[256,1024]{1,0:T(8,128)(2,1)S(1)} %copy-done.1, f32[4,1,512]{2,1,0:T(1,128)S(1)} %get-tuple-element.67.refs_10_.refs_2_, ...), custom_call_target="tpu_custom_call" | custom-call | flops 20000000 | bytes 1 | tf_op jit(solution)/shard_map/pallas_call | solution.py:42
  72.8 9.3 %collective-permute-done.21.refs_3_ = bf16[528,128]{1,0:T(8,128)(2,1)S(1)} collective-permute-done((bf16[528,128]{1,0:T(8,128)(2,1)S(1)}, bf16[528,128]{1,0:T(8,128)(2,1)S(1)}, u32[]{:S(2)}, u32[]{:S(2)}) %collective-permute-start.21) | collective-permute-done | bytes 135200 | tf_op jit(solution)/shard_map/ppermute | solution.py:499
  83.7 1.3 %collective-permute-start.25 = (bf16[256,256]{1,0:T(8,128)(2,1)S(1)}, bf16[256,256]{1,0:T(8,128)(2,1)S(1)}, u32[]{:S(2)}, u32[]{:S(2)}) collective-permute-start(bf16[256,256]{1,0:T(8,128)(2,1)S(1)} %slice.40), channel_id=1, source_target_pairs={{0,4},{4,0},{8,12},{12,8},{16,20},{20,16},{24,28},{28,24},{1,5},{5... | collective-permute-start | bytes 393224 | tf_op jit(solution)/shard_map/ppermute | solution.py:491
  85.0 3.5 %shard_map.191 = (bf16[256,1024]{1,0:T(8,128)(2,1)}, f32[256,1024]{1,0:T(8,128)S(1)}, f32[256,1024]{1,0:T(8,128)S(1)}) custom-call(s32[2]{0:T(128)S(1)} %pad_add_fusion.place, f32[8,256]{1,0:T(8,128)S(1)} %get-tuple-element.53.refs_0_, f32[256,8]{1,0:T(8,128)S(1)} %get-tuple-element.54.refs_1_, bf16[256,1024]{1,0:T(8,128)(2,1)S(1)} %copy-done.2, ...), custom_call_target="tpu_custom_call" | custom-call | flops 20000000 | bytes 1 | tf_op jit(solution)/shard_map/pallas_call | solution.py:42
  89.2 2.5 %shard_map.198 = (bf16[256,1024]{1,0:T(8,128)(2,1)}, bf16[256,1024]{1,0:T(8,128)(2,1)}, bf16[256,1024]{1,0:T(8,128)(2,1)}, bf16[256,1024]{1,0:T(8,128)(2,1)}, bf...) custom-call(s32[2]{0:T(128)S(1)} %pad_add_fusion.place, f32[8,256]{1,0:T(8,128)S(1)} %get-tuple-element.53.refs_0_, ...), custom_call_target="tpu_custom_call" | custom-call | flops 4000000000 | bytes 1 | tf_op jit(solution)/shard_map/pallas_call | solution.py:42
  (80 shorter events, 20.3 us)
Async XLA Ops:
  1.7 10.9 %collective-permute-start.5 = (bf16[256,256]{1,0:T(8,128)(2,1)S(1)}, bf16[256,256]{1,0:T(8,128)(2,1)S(1)}, u32[]{:S(2)}, u32[]{:S(2)}) collective-permute-start(bf16[256,256]{1,0:T(8,128)(2,1)S(1)} %pad_maximum_fusion.refs_3_), channel_id=1, source_target_pairs={{0,4},{4,0},{8,12},{12,8},{16,20},{20,16},{24,28},{28,24},{1,5},{5... | collective-permute-start | bytes 393224 | tf_op jit(solution)/shard_map/ppermute | solution.py:491
  4.8 11.4 %collective-permute-start.3 = (bf16[256,256]{1,0:T(8,128)(2,1)S(1)}, bf16[256,256]{1,0:T(8,128)(2,1)S(1)}, u32[]{:S(2)}, u32[]{:S(2)}) collective-permute-start(bf16[256,256]{1,0:T(8,128)(2,1)S(1)} %pad_maximum_fusion.1.refs_4_.refs_1_), channel_id=1, source_target_pairs={{0,8},{4,12},{8,16},{12,20},{16,24},{20,28},{1,9},{5,13},{9,17},{1... | collective-permute-start | bytes 393224 | tf_op jit(solution)/shard_map/ppermute | solution.py:495
  9.9 7.0 %collective-permute-start = (bf16[528,128]{1,0:T(8,128)(2,1)S(1)}, bf16[528,128]{1,0:T(8,128)(2,1)S(1)}, u32[]{:S(2)}, u32[]{:S(2)}) collective-permute-start(bf16[528,128]{1,0:T(8,128)(2,1)S(1)} %get-tuple-element.101.refs_7_), channel_id=1, source_target_pairs={{0,4},{4,0},{8,12},{12,8},{16,20},{20,16},{24,28},{28,24},{1,5},{5... | collective-permute-start | bytes 405512 | tf_op jit(solution)/shard_map/ppermute | solution.py:491
  11.4 19.5 %collective-permute-start.8 = (bf16[256,512]{1,0:T(8,128)(2,1)S(1)}, bf16[256,512]{1,0:T(8,128)(2,1)S(1)}, u32[]{:S(2)}, u32[]{:S(2)}) collective-permute-start(bf16[256,512]{1,0:T(8,128)(2,1)S(1)} %shard_map.181), channel_id=1, source_target_pairs={{0,4},{4,0},{8,12},{12,8},{16,20},{20,16},{24,28},{28,24},{1,5},{5... | collective-permute-start | bytes 786440 | tf_op jit(solution)/shard_map/ppermute | solution.py:491
  12.7 11.2 %collective-permute-start.6 = (bf16[256,256]{1,0:T(8,128)(2,1)S(1)}, bf16[256,256]{1,0:T(8,128)(2,1)S(1)}, u32[]{:S(2)}, u32[]{:S(2)}) collective-permute-start(bf16[256,256]{1,0:T(8,128)(2,1)S(1)} %collective-permute-done.5.refs_2_.refs_5_), channel_id=1, source_target_pairs={{0,8},{4,12},{8,16},{12,20},{16,24},{20,28},{1,9},{5,13},{9,17},{1... | collective-permute-start | bytes 393224 | tf_op jit(solution)/shard_map/ppermute | solution.py:495
  16.2 8.4 %collective-permute-start.4 = (bf16[256,256]{1,0:T(8,128)(2,1)S(1)}, bf16[256,256]{1,0:T(8,128)(2,1)S(1)}, u32[]{:S(2)}, u32[]{:S(2)}) collective-permute-start(bf16[256,256]{1,0:T(8,128)(2,1)S(1)} %collective-permute-done.3.refs_1_.refs_4_), channel_id=1, source_target_pairs={{8,16},{12,20},{16,24},{20,28},{9,17},{13,21},{17,25},{21,29},{10,... | collective-permute-start | bytes 393224 | tf_op jit(solution)/shard_map/ppermute | solution.py:495
  17.5 7.8 %collective-permute-start.1 = (bf16[528,128]{1,0:T(8,128)(2,1)S(1)}, bf16[528,128]{1,0:T(8,128)(2,1)S(1)}, u32[]{:S(2)}, u32[]{:S(2)}) collective-permute-start(bf16[528,128]{1,0:T(8,128)(2,1)S(1)} %shard_map.179.refs_0_.refs_1_), channel_id=1, source_target_pairs={{0,8},{4,12},{8,16},{12,20},{16,24},{20,28},{1,9},{5,13},{9,17},{1... | collective-permute-start | bytes 405512 | tf_op jit(solution)/shard_map/ppermute | solution.py:495
  22.9 14.7 %collective-permute-start.12 = (bf16[256,512]{1,0:T(8,128)(2,1)S(1)}, bf16[256,512]{1,0:T(8,128)(2,1)S(1)}, u32[]{:S(2)}, u32[]{:S(2)}) collective-permute-start(bf16[256,512]{1,0:T(8,128)(2,1)S(1)} %shard_map.186), channel_id=1, source_target_pairs={{0,4},{4,0},{8,12},{12,8},{16,20},{20,16},{24,28},{28,24},{1,5},{5... | collective-permute-start | bytes 786440 | tf_op jit(solution)/shard_map/ppermute | solution.py:491
  23.9 10.1 %collective-permute-start.7 = (bf16[256,256]{1,0:T(8,128)(2,1)S(1)}, bf16[256,256]{1,0:T(8,128)(2,1)S(1)}, u32[]{:S(2)}, u32[]{:S(2)}) collective-permute-start(bf16[256,256]{1,0:T(8,128)(2,1)S(1)} %collective-permute-done.6.refs_2_.refs_5_), channel_id=1, source_target_pairs={{8,16},{12,20},{16,24},{20,28},{9,17},{13,21},{17,25},{21,29},{10,... | collective-permute-start | bytes 393224 | tf_op jit(solution)/shard_map/ppermute | solution.py:495
  24.6 13.0 %collective-permute-start.10 = (bf16[256,256]{1,0:T(8,128)(2,1)S(1)}, bf16[256,256]{1,0:T(8,128)(2,1)S(1)}, u32[]{:S(2)}, u32[]{:S(2)}) collective-permute-start(bf16[256,256]{1,0:T(8,128)(2,1)S(1)} %collective-permute-done.4.refs_1_.refs_4_), channel_id=1, source_target_pairs={{16,24},{20,28},{17,25},{21,29},{18,26},{22,30},{19,27},{23,31}} | collective-permute-start | bytes 393224 | tf_op jit(solution)/shard_map/ppermute | solution.py:495
  25.8 9.4 %collective-permute-start.2 = (bf16[528,128]{1,0:T(8,128)(2,1)S(1)}, bf16[528,128]{1,0:T(8,128)(2,1)S(1)}, u32[]{:S(2)}, u32[]{:S(2)}) collective-permute-start(bf16[528,128]{1,0:T(8,128)(2,1)S(1)} %shard_map.180.refs_4_), channel_id=1, source_target_pairs={{0,16},{4,20},{8,24},{12,28},{1,17},{5,21},{9,25},{13,29},{2,18},{... | collective-permute-start | bytes 405512 | tf_op jit(solution)/shard_map/ppermute | solution.py:495
  34.0 3.6 %collective-permute-start.11 = (bf16[256,256]{1,0:T(8,128)(2,1)S(1)}, bf16[256,256]{1,0:T(8,128)(2,1)S(1)}, u32[]{:S(2)}, u32[]{:S(2)}) collective-permute-start(bf16[256,256]{1,0:T(8,128)(2,1)S(1)} %collective-permute-done.7.refs_2_.refs_5_), channel_id=1, source_target_pairs={{16,24},{20,28},{17,25},{21,29},{18,26},{22,30},{19,27},{23,31}} | collective-permute-start | bytes 393224 | tf_op jit(solution)/shard_map/ppermute | solution.py:495
  35.9 6.5 %collective-permute-start.9 = (bf16[512,128]{1,0:T(8,128)(2,1)S(1)}, bf16[512,128]{1,0:T(8,128)(2,1)S(1)}, u32[]{:S(2)}, u32[]{:S(2)}) collective-permute-start(bf16[512,128]{1,0:T(8,128)(2,1)S(1)} %get-tuple-element.64), channel_id=1, source_target_pairs={{0,4},{4,0},{8,12},{12,8},{16,20},{20,16},{24,28},{28,24},{1,5},{5... | collective-permute-start | bytes 393224 | tf_op jit(solution)/shard_map/ppermute | solution.py:491
  38.9 7.4 %collective-permute-start.16 = (bf16[256,512]{1,0:T(8,128)(2,1)S(1)}, bf16[256,512]{1,0:T(8,128)(2,1)S(1)}, u32[]{:S(2)}, u32[]{:S(2)}) collective-permute-start(bf16[256,512]{1,0:T(8,128)(2,1)S(1)} %get-tuple-element.71), channel_id=1, source_target_pairs={{0,4},{4,0},{8,12},{12,8},{16,20},{20,16},{24,28},{28,24},{1,5},{5... | collective-permute-start | bytes 786440 | tf_op jit(solution)/shard_map/ppermute | solution.py:491
  44.4 3.7 %collective-permute-start.14 = (f32[8,256]{1,0:T(8,128)S(1)}, f32[8,256]{1,0:T(8,128)S(1)}, u32[]{:S(2)}, u32[]{:S(2)}) collective-permute-start(f32[8,256]{1,0:T(8,128)S(1)} %get-tuple-element.69.refs_8_), channel_id=1, source_target_pairs={{0,2},{1,3},{2,0},{3,1},{4,6},{5,7},{6,4},{7,5},{8,10},{9,11},{10,... | collective-permute-start | bytes 24584 | tf_op jit(solution)/shard_map/ppermute | solution.py:624
  47.0 5.3 %collective-permute-start.18 = (bf16[512,256]{1,0:T(8,128)(2,1)S(1)}, bf16[512,256]{1,0:T(8,128)(2,1)S(1)}, u32[]{:S(2)}, u32[]{:S(2)}) collective-permute-start(bf16[512,256]{1,0:T(8,128)(2,1)S(1)} %convert_element_type.21), channel_id=1, source_target_pairs={{24,16},{28,20},{25,17},{29,21},{26,18},{30,22},{27,19},{31,23}} | collective-permute-start | bytes 786440 | tf_op jit(solution)/shard_map/ppermute | solution.py:499
  50.7 5.9 %collective-permute-start.17 = (bf16[528,128]{1,0:T(8,128)(2,1)S(1)}, bf16[528,128]{1,0:T(8,128)(2,1)S(1)}, u32[]{:S(2)}, u32[]{:S(2)}) collective-permute-start(bf16[528,128]{1,0:T(8,128)(2,1)S(1)} %get-tuple-element.99), channel_id=1, source_target_pairs={{0,4},{4,0},{8,12},{12,8},{16,20},{20,16},{24,28},{28,24},{1,5},{5... | collective-permute-start | bytes 405512 | tf_op jit(solution)/shard_map/ppermute | solution.py:491
  52.3 6.8 %collective-permute-start.20 = (bf16[512,256]{1,0:T(8,128)(2,1)S(1)}, bf16[512,256]{1,0:T(8,128)(2,1)S(1)}, u32[]{:S(2)}, u32[]{:S(2)}) collective-permute-start(bf16[512,256]{1,0:T(8,128)(2,1)S(1)} %add_convert_fusion.2.refs_2_.refs_10_), channel_id=1, source_target_pairs={{16,8},{20,12},{24,16},{28,20},{17,9},{21,13},{25,17},{29,21},{18,... | collective-permute-start | bytes 786440 | tf_op jit(solution)/shard_map/ppermute | solution.py:499
  57.2 7.6 %collective-permute-start.19 = (bf16[528,128]{1,0:T(8,128)(2,1)S(1)}, bf16[528,128]{1,0:T(8,128)(2,1)S(1)}, u32[]{:S(2)}, u32[]{:S(2)}) collective-permute-start(bf16[528,128]{1,0:T(8,128)(2,1)S(1)} %shard_map.193.refs_9_.refs_0_.refs_2_), channel_id=1, source_target_pairs={{8,0},{12,4},{16,8},{20,12},{24,16},{28,20},{9,1},{13,5},{17,9},{2... | collective-permute-start | bytes 405512 | tf_op jit(solution)/shard_map/ppermute | solution.py:499
  65.5 16.7 %collective-permute-start.21 = (bf16[528,128]{1,0:T(8,128)(2,1)S(1)}, bf16[528,128]{1,0:T(8,128)(2,1)S(1)}, u32[]{:S(2)}, u32[]{:S(2)}) collective-permute-start(bf16[528,128]{1,0:T(8,128)(2,1)S(1)} %shard_map.195.refs_9_), channel_id=1, source_target_pairs={{16,0},{20,4},{24,8},{28,12},{17,1},{21,5},{25,9},{29,13},{18,2},{... | collective-permute-start | bytes 405512 | tf_op jit(solution)/shard_map/ppermute | solution.py:499
  66.8 16.9 %collective-permute-start.24 = (bf16[512,256]{1,0:T(8,128)(2,1)S(1)}, bf16[512,256]{1,0:T(8,128)(2,1)S(1)}, u32[]{:S(2)}, u32[]{:S(2)}) collective-permute-start(bf16[512,256]{1,0:T(8,128)(2,1)S(1)} %add_convert_fusion.1.refs_3_), channel_id=1, source_target_pairs={{8,0},{12,4},{16,8},{20,12},{24,16},{28,20},{9,1},{13,5},{17,9},{2... | collective-permute-start | bytes 786440 | tf_op jit(solution)/shard_map/ppermute | solution.py:499
  71.7 16.8 %collective-permute-start.23 = (bf16[256,512]{1,0:T(8,128)(2,1)S(1)}, bf16[256,512]{1,0:T(8,128)(2,1)S(1)}, u32[]{:S(2)}, u32[]{:S(2)}) collective-permute-start(bf16[256,512]{1,0:T(8,128)(2,1)S(1)} %get-tuple-element.88), channel_id=1, source_target_pairs={{0,4},{4,0},{8,12},{12,8},{16,20},{20,16},{24,28},{28,24},{1,5},{5... | collective-permute-start | bytes 786440 | tf_op jit(solution)/shard_map/ppermute | solution.py:491
  82.8 5.8 %collective-permute-start.22 = (bf16[512,128]{1,0:T(8,128)(2,1)S(1)}, bf16[512,128]{1,0:T(8,128)(2,1)S(1)}, u32[]{:S(2)}, u32[]{:S(2)}) collective-permute-start(bf16[512,128]{1,0:T(8,128)(2,1)S(1)} %get-tuple-element.84), channel_id=1, source_target_pairs={{0,4},{4,0},{8,12},{12,8},{16,20},{20,16},{24,28},{28,24},{1,5},{5... | collective-permute-start | bytes 393224 | tf_op jit(solution)/shard_map/ppermute | solution.py:491
  83.7 5.5 %collective-permute-start.25 = (bf16[256,256]{1,0:T(8,128)(2,1)S(1)}, bf16[256,256]{1,0:T(8,128)(2,1)S(1)}, u32[]{:S(2)}, u32[]{:S(2)}) collective-permute-start(bf16[256,256]{1,0:T(8,128)(2,1)S(1)} %slice.40), channel_id=1, source_target_pairs={{0,4},{4,0},{8,12},{12,8},{16,20},{20,16},{24,28},{28,24},{1,5},{5... | collective-permute-start | bytes 393224 | tf_op jit(solution)/shard_map/ppermute | solution.py:491
  (11 other events, 48.7 us)
